TPU v7x, 32 devices: a whole 2x2x4 slice. The times are simulated.
32 devices in a mesh: dp: 4 (over y, x), tensor: 8 (over z, core).
Axes of the slice: x: 2, y: 2, z: 4, core: 2. Of those that a mesh axis runs over, the one named last changes fastest.
Arguments:
- tokens: float32 [1376, 8, 1024], P('tensor', 'dp'), may hold values from -6 to 6
- cotangent: float32 [1376, 8, 1024], P('tensor', 'dp'), may hold values from -6 to 6
- attention_in: float32 [2, 1024, 3072], P(None, 'dp', 'tensor'), may hold values from -0.1875 to 0.1875
- attention_out: float32 [2, 1024, 1024], P(None, 'dp', 'tensor'), may hold values from -0.75 to 0.75
- hidden_up: float32 [2, 1024, 4096], P(None, 'dp', 'tensor'), may hold values from -0.1875 to 0.1875
- hidden_down: float32 [2, 1024, 4096], P(None, 'dp', 'tensor'), may hold values from -0.09375 to 0.09375
- attention_in_momentum: float32 [2, 1024, 3072], P(None, 'dp', 'tensor')
- attention_out_momentum: float32 [2, 1024, 1024], P(None, 'dp', 'tensor')
- hidden_up_momentum: float32 [2, 1024, 4096], P(None, 'dp', 'tensor')
- hidden_down_momentum: float32 [2, 1024, 4096], P(None, 'dp', 'tensor')
- row_params: float32 [2, 8, 1024], replicated, may hold values from -1.2 to 1.5
- column_bias: float32 [2, 16, 384], P(None, 'tensor'), may hold values from -1.5 to 1.5
- lengths: int32 [8], P('dp'), may hold values from 344 to 1376, as said below
Outputs:
- layer_output: float32 [1376, 8, 1024], P('tensor', 'dp')
- tokens_grad: float32 [1376, 8, 1024], P('tensor', 'dp')
- attention_in_grad: float32 [2, 1024, 3072], P(None, 'dp', 'tensor')
- attention_out_grad: float32 [2, 1024, 1024], P(None, 'dp', 'tensor')
- hidden_up_grad: float32 [2, 1024, 4096], P(None, 'dp', 'tensor')
- hidden_down_grad: float32 [2, 1024, 4096], P(None, 'dp', 'tensor')
- attention_in_momentum_new: float32 [2, 1024, 3072], P(None, 'dp', 'tensor')
- attention_out_momentum_new: float32 [2, 1024, 1024], P(None, 'dp', 'tensor')
- hidden_up_momentum_new: float32 [2, 1024, 4096], P(None, 'dp', 'tensor')
- hidden_down_momentum_new: float32 [2, 1024, 4096], P(None, 'dp', 'tensor')
- attention_in_new: float32 [2, 1024, 3072], P(None, 'dp', 'tensor')
- attention_out_new: float32 [2, 1024, 1024], P(None, 'dp', 'tensor')
- hidden_up_new: float32 [2, 1024, 4096], P(None, 'dp', 'tensor')
- hidden_down_new: float32 [2, 1024, 4096], P(None, 'dp', 'tensor')
- row_grad: float32 [2, 8, 1024], replicated
- row_new: float32 [2, 8, 1024], replicated
- column_grad: float32 [2, 16, 384], P(None, 'tensor', 'dp')
- column_new: float32 [2, 16, 384], P(None, 'tensor', 'dp')
Inputs may be any that keep to these rules, and one draw needn't show every extreme that they name: `lengths`: in each block of 2 images of one index of dp, one image, drawn from the seed, has exactly 1376 valid positions.
All inputs are finite; a program needn't handle non-finite values.
Results may differ from a plain program's by a relative error of at most 0.012.
Values may be sent and summed in bfloat16 or wider, within the bound.
No kernel may reach another device: no remote copies, remote signals or barrier semaphores. Data moves between devices by JAX's collectives and lax.ppermute only.
A program may use at most 320 MiB of HBM per device.

v0:
```python
import math

import jax
import jax.numpy as jnp
from jax import lax
from jax.sharding import PartitionSpec as P

D = 1024
HD = 64
FF = 4096
NS_STEPS = 5


EPS_NORM = 1e-06
EPS_GRAM = 1e-07
NS_A = 3.4445
NS_B = -4.775
NS_C = 2.0315
MOMENTUM = 0.95
MUON_RATE = 0.5
SCORE_FLOOR = -1e30
HIGHEST = lax.Precision.HIGHEST


def layer_norm(values, norm_gain, norm_shift):
    centered = values - jnp.mean(values, axis=-1, keepdims=True)
    inverse = lax.rsqrt(jnp.mean(centered * centered, axis=-1, keepdims=True) + EPS_NORM)
    normed = centered * inverse
    return (normed * norm_gain + norm_shift, normed, inverse)


def norm_backward(grad_out, normed, inverse, norm_gain):
    scaled = grad_out * norm_gain
    grad_in = inverse * (
        scaled
        - jnp.mean(scaled, axis=-1, keepdims=True)
        - normed * jnp.mean(scaled * normed, axis=-1, keepdims=True)
    )
    return (grad_in, jnp.sum(grad_out * normed, axis=(0, 1)), jnp.sum(grad_out, axis=(0, 1)))


def gelu_exact(values):
    return jax.nn.gelu(values, approximate=False)


def attend_image(operands):
    query_rows, key_rows, value_rows, key_valid = operands
    score_scale = query_rows.shape[-1] ** (-0.5)
    scores = (
        jnp.einsum("qhe,khe->hqk", query_rows, key_rows, preferred_element_type=jnp.float32)
        * score_scale
    )
    scores = jnp.where(key_valid[None, None, :], scores, SCORE_FLOOR)
    row_max = jnp.max(scores, axis=-1, keepdims=True)
    exponent = jnp.exp(scores - row_max)
    row_total = jnp.sum(exponent, axis=-1, keepdims=True)
    softmax_low = (exponent / row_total).astype(jnp.bfloat16)
    mixed = jnp.einsum("hqk,khe->qhe", softmax_low, value_rows, preferred_element_type=jnp.float32)
    return (mixed.astype(jnp.bfloat16), row_max, row_total)


def attend_back(operands):
    query_rows, key_rows, value_rows, key_valid, row_max, row_total, grad_mixed = operands
    score_scale = query_rows.shape[-1] ** (-0.5)
    scores = (
        jnp.einsum("qhe,khe->hqk", query_rows, key_rows, preferred_element_type=jnp.float32)
        * score_scale
    )
    scores = jnp.where(key_valid[None, None, :], scores, SCORE_FLOOR)
    softmax_rows = jnp.exp(scores - row_max) / row_total
    grad_value = jnp.einsum(
        "hqk,qhe->khe",
        softmax_rows.astype(jnp.bfloat16),
        grad_mixed,
        preferred_element_type=jnp.float32,
    )
    grad_soft = jnp.einsum(
        "qhe,khe->hqk", grad_mixed, value_rows, preferred_element_type=jnp.float32
    )
    grad_scores = softmax_rows * (
        grad_soft - jnp.sum(softmax_rows * grad_soft, axis=-1, keepdims=True)
    )
    grad_low = grad_scores.astype(jnp.bfloat16)
    grad_query = (
        jnp.einsum("hqk,khe->qhe", grad_low, key_rows, preferred_element_type=jnp.float32)
        * score_scale
    )
    grad_key = (
        jnp.einsum("hqk,qhe->khe", grad_low, query_rows, preferred_element_type=jnp.float32)
        * score_scale
    )
    return (grad_query, grad_key, grad_value)


def gather_rows(normed_low):
    return lax.all_gather(normed_low, "tensor", axis=0, tiled=True)


def project_out(head_rows, weight_cols):
    return lax.psum_scatter(
        jnp.einsum("sic,dc->sid", head_rows, weight_cols, preferred_element_type=jnp.float32),
        "tensor",
        scatter_dimension=0,
        tiled=True,
    )


def project_back(grad_low, head_rows, weight_cols):
    shard_rows = lax.all_gather(grad_low, "tensor", axis=0, tiled=True)
    weight_grad = jnp.einsum(
        "sid,sic->dc", shard_rows, head_rows, preferred_element_type=jnp.float32
    )
    head_term = jnp.einsum(
        "sid,dc->sic", shard_rows, weight_cols, preferred_element_type=jnp.float32
    )
    return (head_term, weight_grad)


def sum_inputs(grad_low, weight_cols):
    return lax.psum_scatter(
        jnp.einsum("sic,dc->sid", grad_low, weight_cols, preferred_element_type=jnp.float32),
        "tensor",
        scatter_dimension=0,
        tiled=True,
    )


def orthogonalize(received):
    current = received[0]
    for iteration in range(NS_STEPS):
        gram_part = jnp.einsum(
            "pac,pbc->pab", current, current, precision=HIGHEST, preferred_element_type=jnp.float32
        )
        gram_rows = lax.psum_scatter(gram_part, "tensor", scatter_dimension=1, tiled=True)
        gram = lax.all_gather(gram_rows, "tensor", axis=1, tiled=True)
        if iteration == 0:
            inverse = lax.rsqrt(jnp.trace(gram, axis1=1, axis2=2) + EPS_GRAM)[:, None, None]
            current = current * inverse
            gram = gram * (inverse * inverse)
        polynomial = NS_B * gram + NS_C * jnp.einsum(
            "pab,pbc->pac", gram, gram, precision=HIGHEST, preferred_element_type=jnp.float32
        )
        current = NS_A * current + jnp.einsum(
            "pab,pbc->pac",
            polynomial,
            current,
            precision=HIGHEST,
            preferred_element_type=jnp.float32,
        )
    return lax.all_to_all(current[None], "dp", split_axis=2, concat_axis=0, tiled=True)


def per_device(
    tokens,
    cotangent,
    attention_in,
    attention_out,
    hidden_up,
    hidden_down,
    attention_in_momentum,
    attention_out_momentum,
    hidden_up_momentum,
    hidden_down_momentum,
    row_params,
    column_bias,
    lengths,
):
    local_rows, image_count, model_width = tokens.shape
    tensor_count = lax.axis_size("tensor")
    data_count = lax.axis_size("dp")
    seq_total = local_rows * tensor_count
    layer_count = attention_in.shape[0]
    head_count = column_bias.shape[1]
    key_valid = lax.broadcasted_iota(jnp.int32, (image_count, seq_total), 1) < lengths[:, None]
    residual = tokens
    kept_layers = []
    for block_index in range(layer_count):
        row_set = row_params[block_index]
        col_set = column_bias[block_index]
        unit_bias = col_set[:, 2 * HD :].reshape(-1)
        input_cols, output_cols, expand_cols, reduce_cols = (
            lax.all_gather(
                attention_in[block_index].astype(jnp.bfloat16), "dp", axis=0, tiled=True
            ),
            lax.all_gather(
                attention_out[block_index].astype(jnp.bfloat16), "dp", axis=0, tiled=True
            ),
            lax.all_gather(hidden_up[block_index].astype(jnp.bfloat16), "dp", axis=0, tiled=True),
            lax.all_gather(hidden_down[block_index].astype(jnp.bfloat16), "dp", axis=0, tiled=True),
        )
        norm_one, normed_first, inverse_first = layer_norm(residual, row_set[0], row_set[1])
        first_rows = gather_rows(norm_one.astype(jnp.bfloat16))
        projected = jnp.einsum(
            "sid,dc->sic", first_rows, input_cols, preferred_element_type=jnp.float32
        )
        projected = projected.reshape(seq_total, image_count, head_count, 3, HD)
        query_rows = jnp.moveaxis(
            (projected[:, :, :, 0] + col_set[:, :HD]).astype(jnp.bfloat16), 1, 0
        )
        key_rows = jnp.moveaxis(projected[:, :, :, 1].astype(jnp.bfloat16), 1, 0)
        value_rows = jnp.moveaxis(
            (projected[:, :, :, 2] + col_set[:, HD : 2 * HD]).astype(jnp.bfloat16), 1, 0
        )
        head_out, row_max, row_total = lax.map(
            attend_image, (query_rows, key_rows, value_rows, key_valid)
        )
        head_rows = jnp.moveaxis(head_out, 0, 1).reshape(seq_total, image_count, head_count * HD)
        branch_one = project_out(head_rows, output_cols) + row_set[2]
        middle = residual + row_set[3] * branch_one
        norm_two, normed_second, inverse_second = layer_norm(middle, row_set[4], row_set[5])
        second_rows = gather_rows(norm_two.astype(jnp.bfloat16))
        preactivation = (
            jnp.einsum("sid,dc->sic", second_rows, expand_cols, preferred_element_type=jnp.float32)
            + unit_bias
        )
        hidden_low = gelu_exact(preactivation).astype(jnp.bfloat16)
        branch_two = project_out(hidden_low, reduce_cols) + row_set[6]
        residual = middle + row_set[7] * branch_two
        kept_layers.append(
            (
                input_cols,
                output_cols,
                expand_cols,
                reduce_cols,
                normed_first,
                inverse_first,
                first_rows,
                query_rows,
                key_rows,
                value_rows,
                row_max,
                row_total,
                head_rows,
                branch_one,
                normed_second,
                inverse_second,
                second_rows,
                preactivation,
                hidden_low,
                branch_two,
            )
        )
    grad_residual = cotangent
    row_terms = []
    column_terms = []
    grad_lists = ([], [], [], [])
    for block_index in reversed(range(layer_count)):
        (
            input_cols,
            output_cols,
            expand_cols,
            reduce_cols,
            normed_first,
            inverse_first,
            first_rows,
            query_rows,
            key_rows,
            value_rows,
            row_max,
            row_total,
            head_rows,
            branch_one,
            normed_second,
            inverse_second,
            second_rows,
            preactivation,
            hidden_low,
            branch_two,
        ) = kept_layers[block_index]
        row_set = row_params[block_index]
        grad_branch_two = grad_residual * row_set[7]
        scale_two = jnp.sum(grad_residual * branch_two, axis=(0, 1))
        shift_down = jnp.sum(grad_branch_two, axis=(0, 1))
        grad_hidden, reduce_grad = project_back(
            grad_branch_two.astype(jnp.bfloat16), hidden_low, reduce_cols
        )
        grad_pre = jax.vjp(gelu_exact, preactivation)[1](grad_hidden)[0]
        unit_grad = jnp.sum(grad_pre, axis=(0, 1))
        grad_pre_low = grad_pre.astype(jnp.bfloat16)
        expand_grad = jnp.einsum(
            "sid,sic->dc", second_rows, grad_pre_low, preferred_element_type=jnp.float32
        )
        grad_norm_two = sum_inputs(grad_pre_low, expand_cols)
        grad_in_two, gain_two, shift_two = norm_backward(
            grad_norm_two, normed_second, inverse_second, row_set[4]
        )
        grad_residual = grad_residual + grad_in_two
        grad_branch_one = grad_residual * row_set[3]
        scale_one = jnp.sum(grad_residual * branch_one, axis=(0, 1))
        shift_out = jnp.sum(grad_branch_one, axis=(0, 1))
        grad_heads, output_grad = project_back(
            grad_branch_one.astype(jnp.bfloat16), head_rows, output_cols
        )
        grad_heads_low = jnp.moveaxis(
            grad_heads.astype(jnp.bfloat16).reshape(seq_total, image_count, head_count, HD), 1, 0
        )
        grad_query, grad_key, grad_value = lax.map(
            attend_back,
            (query_rows, key_rows, value_rows, key_valid, row_max, row_total, grad_heads_low),
        )
        query_bias_grad = jnp.sum(grad_query, axis=(0, 1))
        value_bias_grad = jnp.sum(grad_value, axis=(0, 1))
        grad_projected = jnp.stack([grad_query, grad_key, grad_value], axis=3).astype(jnp.bfloat16)
        grad_proj_low = jnp.moveaxis(grad_projected, 0, 1).reshape(
            seq_total, image_count, head_count * 3 * HD
        )
        input_grad = jnp.einsum(
            "sid,sic->dc", first_rows, grad_proj_low, preferred_element_type=jnp.float32
        )
        grad_norm_one = sum_inputs(grad_proj_low, input_cols)
        grad_in_one, gain_one, shift_one = norm_backward(
            grad_norm_one, normed_first, inverse_first, row_set[0]
        )
        grad_residual = grad_residual + grad_in_one
        row_terms.append(
            jnp.stack(
                [
                    gain_one,
                    shift_one,
                    shift_out,
                    scale_one,
                    gain_two,
                    shift_two,
                    shift_down,
                    scale_two,
                ]
            )
        )
        column_term = jnp.concatenate(
            [query_bias_grad, value_bias_grad, unit_grad.reshape(head_count, -1)], axis=1
        )
        reduced = (
            lax.psum_scatter(input_grad, "dp", scatter_dimension=0, tiled=True),
            lax.psum_scatter(output_grad, "dp", scatter_dimension=0, tiled=True),
            lax.psum_scatter(expand_grad, "dp", scatter_dimension=0, tiled=True),
            lax.psum_scatter(reduce_grad, "dp", scatter_dimension=0, tiled=True),
            lax.psum_scatter(column_term, "dp", scatter_dimension=1, tiled=True),
        )
        for kind_index in range(4):
            grad_lists[kind_index].append(reduced[kind_index])
        column_terms.append(reduced[4])
    row_grad = lax.psum(jnp.stack(row_terms[::-1]), ("dp", "tensor"))
    column_grad = jnp.stack(column_terms[::-1])
    grads_by_kind = [jnp.stack(grad_lists[kind_index][::-1]) for kind_index in range(4)]
    weights_by_kind = (attention_in, attention_out, hidden_up, hidden_down)
    moments_by_kind = (
        attention_in_momentum,
        attention_out_momentum,
        hidden_up_momentum,
        hidden_down_momentum,
    )
    fans_by_kind = (D, D // 16, D, FF)
    moments_new = [
        MOMENTUM * moments_by_kind[kind_index] + grads_by_kind[kind_index]
        for kind_index in range(4)
    ]
    pad_width = hidden_up.shape[2]
    rows_owned = hidden_up.shape[1]
    padded = []
    for block_index in range(layer_count):
        for kind_index in range(4):
            source = moments_new[kind_index][block_index]
            padded.append(jnp.pad(source, ((0, 0), (0, pad_width - source.shape[1]))))
    send_buffer = jnp.stack(padded).reshape(
        data_count, 4 * layer_count // data_count, rows_owned, pad_width
    )
    returned = orthogonalize(
        lax.all_to_all(send_buffer, "dp", split_axis=0, concat_axis=2, tiled=True)
    )
    returned = returned.reshape(layer_count, 4, rows_owned, pad_width)
    weights_new = []
    for kind_index in range(4):
        local_cols = weights_by_kind[kind_index].shape[2]
        full_cols = local_cols * tensor_count
        rate = MUON_RATE * math.sqrt(max(D, full_cols) / fans_by_kind[kind_index])
        weights_new.append(
            weights_by_kind[kind_index] - rate * returned[:, kind_index, :, :local_cols]
        )
    small_rate = 0.3 / math.sqrt(image_count * data_count * seq_total)
    row_new = row_params - small_rate * row_grad
    owned_width = column_grad.shape[2]
    column_old = lax.dynamic_slice_in_dim(
        column_bias, lax.axis_index("dp") * owned_width, owned_width, 2
    )
    column_new = column_old - small_rate * column_grad
    return (
        residual,
        grad_residual,
        grads_by_kind[0],
        grads_by_kind[1],
        grads_by_kind[2],
        grads_by_kind[3],
        moments_new[0],
        moments_new[1],
        moments_new[2],
        moments_new[3],
        weights_new[0],
        weights_new[1],
        weights_new[2],
        weights_new[3],
        row_grad,
        row_new,
        column_grad,
        column_new,
    )


def solution(mesh):
    in_specs = (
        P("tensor", "dp", None),
        P("tensor", "dp", None),
        P(None, "dp", "tensor"),
        P(None, "dp", "tensor"),
        P(None, "dp", "tensor"),
        P(None, "dp", "tensor"),
        P(None, "dp", "tensor"),
        P(None, "dp", "tensor"),
        P(None, "dp", "tensor"),
        P(None, "dp", "tensor"),
        P(),
        P(None, "tensor", None),
        P("dp"),
    )
    out_specs = (
        P("tensor", "dp", None),
        P("tensor", "dp", None),
        P(None, "dp", "tensor"),
        P(None, "dp", "tensor"),
        P(None, "dp", "tensor"),
        P(None, "dp", "tensor"),
        P(None, "dp", "tensor"),
        P(None, "dp", "tensor"),
        P(None, "dp", "tensor"),
        P(None, "dp", "tensor"),
        P(None, "dp", "tensor"),
        P(None, "dp", "tensor"),
        P(None, "dp", "tensor"),
        P(None, "dp", "tensor"),
        P(),
        P(),
        P(None, "tensor", "dp"),
        P(None, "tensor", "dp"),
    )
    return jax.shard_map(
        per_device, mesh=mesh, in_specs=in_specs, out_specs=out_specs, check_vma=False
    )
```

profile of v0, /device:TPU:0, one launch (start us, length us, event | category | flops | bytes accessed | tf_op | source)
XLA Modules:
  0.0 4401.5 jit_solution(5927164234658006077)
XLA Ops:
  42.8 37.3 all-gather.26.cloned.1.call-done
  86.3 45.4 %while.56 = (s32[]{:T(128)}, bf16[2,1376,2,64]{1,3,2,0:T(8,128)(2,1)S(1)}, f32[2,2,1376,1]{2,1,3,0:T(2,128)S(1)}, f32[2,2,1376,1]{2,1,3,0:T(2,128)S(1)}, bf16[2,...) while((s32[]{:T(128)}, ...), condition=%wide.region_5.6_spmd, body=%wide.region_2.5_spmd.sunk | while | flops 999873152 | bytes 46990380 | solution.py:204
  133.5 17.6 copy.151
  154.5 225.4 %all-reduce.24.cloned.1.call-done = f32[1376,2,1024]{2,1,0:T(2,128)} async-done(((f32[1376,2,1024]{2,1,0:T(2,128)}), f32[1376,2,1024]{2,1,0:T(2,128)}) %all-reduce.24.cloned.1.call-update) | async-done | bytes 11272208
  383.3 14.3 add_convert_fusion.2
  400.4 56.6 %all-gather.28.cloned.1.call-done = bf16[1376,2,1024]{2,1,0:T(2,128)(2,1)} async-done(((bf16[172,2,1024]{2,1,0:T(2,128)(2,1)}), bf16[1376,2,1024]{2,1,0:T(2,128)(2,1)}) %all-gather.28.cloned.1.call-update) | async-done | bytes 5636112 | tf_op jit(solution)/shard_map/all_gather | solution.py:96
  468.0 14.1 multiply_convert_fusion.3
  489.7 17.5 copy.153
  507.3 229.7 %all-reduce.26.cloned.1.call-done = f32[1376,2,1024]{2,1,0:T(2,128)} async-done(((f32[1376,2,1024]{2,1,0:T(2,128)}), f32[1376,2,1024]{2,1,0:T(2,128)}) %all-reduce.26.cloned.1.call-update) | async-done | bytes 11272208
  763.8 38.2 all-gather.30.cloned.1.call-done
  811.2 47.5 %while.57 = (s32[]{:T(128)}, bf16[2,1376,2,64]{1,3,2,0:T(8,128)(2,1)}, f32[2,2,1376,1]{2,1,3,0:T(2,128)}, f32[2,2,1376,1]{2,1,3,0:T(2,128)}, bf16[2,1376,2,64]{1...) while((s32[]{:T(128)}, ...), condition=%wide.region_15.16_spmd, body=%wide.region_12.15_spmd.sunk | while | flops 999873152 | bytes 55444096 | solution.py:204
  861.7 17.5 copy.157
  880.0 227.7 %all-reduce.28.cloned.1.call-done = f32[1376,2,1024]{2,1,0:T(2,128)} async-done(((f32[1376,2,1024]{2,1,0:T(2,128)}), f32[1376,2,1024]{2,1,0:T(2,128)}) %all-reduce.28.cloned.1.call-update) | async-done | bytes 11272208
  1117.4 19.4 all-gather.56.cloned.1.call-done
  1136.8 61.3 %all-gather.32.cloned.1.call-done = bf16[1376,2,1024]{2,1,0:T(2,128)(2,1)} async-done(((bf16[172,2,1024]{2,1,0:T(2,128)(2,1)}), bf16[1376,2,1024]{2,1,0:T(2,128)(2,1)}) %all-gather.32.cloned.1.call-update) | async-done | bytes 5636112 | tf_op jit(solution)/shard_map/all_gather | solution.py:96
  1209.1 14.1 multiply_convert_fusion.2
  1225.6 61.3 %all-gather.34.cloned.1.call-done = bf16[1376,2,1024]{2,1,0:T(2,128)(2,1)} async-done(((bf16[172,2,1024]{2,1,0:T(2,128)(2,1)}), bf16[1376,2,1024]{2,1,0:T(2,128)(2,1)}) %all-gather.34.cloned.1.call-update) | async-done | bytes 5636112 | tf_op jit(solution)/shard_map/all_gather | solution.py:109
  1302.5 17.5 copy.161
  1320.1 228.7 %all-reduce.30.cloned.1.call-done = f32[1376,2,1024]{2,1,0:T(2,128)} async-done(((f32[1376,2,1024]{2,1,0:T(2,128)}), f32[1376,2,1024]{2,1,0:T(2,128)}) %all-reduce.30.cloned.1.call-update) | async-done | bytes 11272208
  1562.8 57.8 %all-gather.36.cloned.1.call-done = bf16[1376,2,1024]{2,1,0:T(2,128)(2,1)} async-done(((bf16[172,2,1024]{2,1,0:T(2,128)(2,1)}), bf16[1376,2,1024]{2,1,0:T(2,128)(2,1)}) %all-gather.36.cloned.1.call-update) | async-done | bytes 5636112 | tf_op jit(solution)/shard_map/all_gather | solution.py:109
  1630.0 71.5 %while.58 = (s32[]{:T(128)}, f32[2,1376,2,64]{1,3,2,0:T(8,128)}, bf16[2,1376,2,64]{1,3,2,0:T(8,128)(2,1)}, f32[2,1376,2,64]{1,3,2,0:T(8,128)}, bf16[2,1376,2,64]...) while((s32[]{:T(128)}, f32[2,1376,2,64]{1,3,2,0:T(8,128)}, ...), condition=%wide.region_25.26_spmd, body=%wide.region_23.25_spmd.sunk | while | flops 2461738240 | bytes 141267440 | solution.py:297
  1711.5 17.7 copy.166
  1729.3 228.7 %all-reduce.32.cloned.1.call-done = f32[1376,2,1024]{2,1,0:T(2,128)} async-done(((f32[1376,2,1024]{2,1,0:T(2,128)}), f32[1376,2,1024]{2,1,0:T(2,128)}) %all-reduce.32.cloned.1.call-update) | async-done | bytes 11272208
  1970.8 59.6 %all-gather.38.cloned.1.call-done = bf16[1376,2,1024]{2,1,0:T(2,128)(2,1)} async-done(((bf16[172,2,1024]{2,1,0:T(2,128)(2,1)}), bf16[1376,2,1024]{2,1,0:T(2,128)(2,1)}) %all-gather.38.cloned.1.call-update) | async-done | bytes 5636112 | tf_op jit(solution)/shard_map/all_gather | solution.py:109
  2030.4 12.4 fusion.295
  2046.1 17.5 copy.168
  2064.1 228.0 %all-reduce.34.cloned.1.call-done = f32[1376,2,1024]{2,1,0:T(2,128)} async-done(((f32[1376,2,1024]{2,1,0:T(2,128)}), f32[1376,2,1024]{2,1,0:T(2,128)}) %all-reduce.34.cloned.1.call-update) | async-done | bytes 11272208
  2342.5 21.8 all-gather.40.cloned.1.call-done
  2385.3 71.6 %while.59 = (s32[]{:T(128)}, f32[2,1376,2,64]{1,3,2,0:T(8,128)}, bf16[2,1376,2,64]{1,3,2,0:T(8,128)(2,1)}, f32[2,1376,2,64]{1,3,2,0:T(8,128)}, bf16[2,1376,2,64]...) while((s32[]{:T(128)}, f32[2,1376,2,64]{1,3,2,0:T(8,128)}, ...), condition=%wide.region_34.35_spmd, body=%wide.region_32.34_spmd.sunk | while | flops 2461738240 | bytes 141267440 | solution.py:297
  2477.2 38.3 reduce-scatter.28.cloned.1.call-done
  2518.7 25.1 reduce-scatter.26.cloned.1.call-done
  2543.7 28.5 reduce-scatter.24.cloned.1.call-done
  2574.6 31.4 reduce-scatter.22.cloned.1.call-done
  2606.1 33.7 reduce-scatter.20.cloned.1.call-done
  2643.6 50.6 %all_to_all.30 = f32[4,2,256,512]{3,2,1,0:T(8,128)S(1)} all-to-all(f32[4,2,256,512]{3,2,1,0:T(8,128)S(1)} %bitcast.518), channel_id=1, replica_groups=mesh['dp'=4,'tensor'=8] {'dp'}, dimensions={0} | all-to-all | bytes 8388608 | tf_op jit(solution)/shard_map/all_to_all | solution.py:368
  2696.7 15.8 fusion.296
  2712.6 89.2 %reduce-scatter.36.cloned.1.call-done = f32[2,128,1024]{2,1,0:T(8,128)} async-done(((f32[2,1024,1024]{2,1,0:T(8,128)}), f32[2,128,1024]{2,1,0:T(8,128)}) %reduce-scatter.36.cloned.1.call-update) | async-done | bytes 1048592 | tf_op jit(solution)/shard_map/reduce_scatter | solution.py:134
  2802.2 81.7 %all-gather.42.cloned.1.call-done = f32[2,1024,1024]{2,1,0:T(8,128)} async-done(((f32[2,128,1024]{2,1,0:T(8,128)}), f32[2,1024,1024]{2,1,0:T(8,128)}) %all-gather.42.cloned.1.call-update) | async-done | bytes 8388624 | tf_op jit(solution)/shard_map/all_gather | solution.py:135
  2889.6 28.2 fusion.110
  2917.8 15.2 multiply_add_fusion.5
  2935.1 15.8 fusion.297
  2951.0 88.3 %reduce-scatter.38.cloned.1.call-done = f32[2,128,1024]{2,1,0:T(8,128)} async-done(((f32[2,1024,1024]{2,1,0:T(8,128)}), f32[2,128,1024]{2,1,0:T(8,128)}) %reduce-scatter.38.cloned.1.call-update) | async-done | bytes 1048592 | tf_op jit(solution)/shard_map/reduce_scatter | solution.py:134
  3039.3 80.3 %all-gather.44.cloned.1.call-done = f32[2,1024,1024]{2,1,0:T(8,128)} async-done(((f32[2,128,1024]{2,1,0:T(8,128)}), f32[2,1024,1024]{2,1,0:T(8,128)}) %all-gather.44.cloned.1.call-update) | async-done | bytes 8388624 | tf_op jit(solution)/shard_map/all_gather | solution.py:135
  3119.6 30.3 fusion.298
  3150.0 14.5 multiply_add_fusion.4
  3166.6 16.0 fusion.299
  3182.6 88.0 %reduce-scatter.40.cloned.1.call-done = f32[2,128,1024]{2,1,0:T(8,128)} async-done(((f32[2,1024,1024]{2,1,0:T(8,128)}), f32[2,128,1024]{2,1,0:T(8,128)}) %reduce-scatter.40.cloned.1.call-update) | async-done | bytes 1048592 | tf_op jit(solution)/shard_map/reduce_scatter | solution.py:134
  3270.7 80.6 %all-gather.46.cloned.1.call-done = f32[2,1024,1024]{2,1,0:T(8,128)} async-done(((f32[2,128,1024]{2,1,0:T(8,128)}), f32[2,1024,1024]{2,1,0:T(8,128)}) %all-gather.46.cloned.1.call-update) | async-done | bytes 8388624 | tf_op jit(solution)/shard_map/all_gather | solution.py:135
  3351.3 30.3 fusion.300
  3381.7 14.5 multiply_add_fusion.3
  3398.3 16.0 fusion.301
  3414.3 88.3 %reduce-scatter.42.cloned.1.call-done = f32[2,128,1024]{2,1,0:T(8,128)} async-done(((f32[2,1024,1024]{2,1,0:T(8,128)}), f32[2,128,1024]{2,1,0:T(8,128)}) %reduce-scatter.42.cloned.1.call-update) | async-done | bytes 1048592 | tf_op jit(solution)/shard_map/reduce_scatter | solution.py:134
  3502.7 80.3 %all-gather.48.cloned.1.call-done = f32[2,1024,1024]{2,1,0:T(8,128)} async-done(((f32[2,128,1024]{2,1,0:T(8,128)}), f32[2,1024,1024]{2,1,0:T(8,128)}) %all-gather.48.cloned.1.call-update) | async-done | bytes 8388624 | tf_op jit(solution)/shard_map/all_gather | solution.py:135
  3583.0 30.3 fusion.302
  3613.3 14.5 multiply_add_fusion.2
  3629.9 16.0 fusion.303
  3645.9 88.0 %reduce-scatter.44.cloned.1.call-done = f32[2,128,1024]{2,1,0:T(8,128)} async-done(((f32[2,1024,1024]{2,1,0:T(8,128)}), f32[2,128,1024]{2,1,0:T(8,128)}) %reduce-scatter.44.cloned.1.call-update) | async-done | bytes 1048592 | tf_op jit(solution)/shard_map/reduce_scatter | solution.py:134
  3739.3 17.5 copy.159
  3762.2 17.5 copy.173
  3779.8 34.9 all-gather.50.cloned.1.call-done
  3814.7 30.3 fusion.304
  3845.0 14.6 add_bitcast_fusion
  3873.6 384.1 %all-reduce.36.cloned.1.call-done = (f32[1376,2,1024]{2,1,0:T(2,128)}, f32[1376,2,1024]{2,1,0:T(2,128)}) async-done(((f32[1376,2,1024]{2,1,0:T(2,128)}, f32[1376,2,1024]{2,1,0:T(2,128)}), (f32[1376,2,1024]{2,1,0:T(2,128)}, f32[1376,2,1024]{2,1,0:T(2,128)})) %all-reduce.36.cloned.1.call-update) | async-done | bytes 22544400
  4270.9 113.5 %all-reduce.22.cloned.1.call-done = f32[2,8,1024]{2,1,0:T(8,128)} async-done(((f32[2,8,1024]{2,1,0:T(8,128)}), f32[2,8,1024]{2,1,0:T(8,128)}) %all-reduce.22.cloned.1.call-update) | async-done | bytes 65552 | tf_op jit(solution)/shard_map/psum | solution.py:342
  (621 shorter events, 597.7 us)
Async XLA Ops:
  8.1 72.0 %all-gather.26.cloned.1.call-start = ((), (), s32[]{:S(2)}) async-start(), calls=%async_computation.17 | async-start | bytes 6340608 | tf_op jit(solution)/shard_map/all_gather | solution.py:96
  17.9 362.0 %all-reduce.24.cloned.1.call-start = ((), (), s32[]{:S(2)}) async-start(), calls=%async_computation.50 | async-start | bytes 22544384
  151.1 249.3 %all-gather.52.cloned.1.call-start = ((), (), s32[]{:S(2)}) async-start(), calls=%async_computation.44 | async-start | bytes 1310720 | tf_op jit(solution)/shard_map/all_gather | solution.py:188
  153.2 303.8 %all-gather.28.cloned.1.call-start = ((), (), s32[]{:S(2)}) async-start(), calls=%async_computation.18 | async-start | bytes 6340608 | tf_op jit(solution)/shard_map/all_gather | solution.py:96
  397.6 86.9 %all-gather.54.cloned.1.call-start = ((), (), s32[]{:S(2)}) async-start(), calls=%async_computation.45 | async-start | bytes 1310720 | tf_op jit(solution)/shard_map/all_gather | solution.py:189
  399.8 337.2 %all-reduce.26.cloned.1.call-start = ((), (), s32[]{:S(2)}) async-start(), calls=%async_computation.51 | async-start | bytes 22544384
  507.3 294.8 %all-gather.30.cloned.1.call-start = ((), (), s32[]{:S(2)}) async-start(), calls=%async_computation.19 | async-start | bytes 6340608 | tf_op jit(solution)/shard_map/all_gather | solution.py:96
  739.4 368.3 %copy-start.14 = (f32[172,2,1024]{2,1,0:T(2,128)}, f32[172,2,1024]{2,1,0:T(2,128)S(1)}, u32[]{:S(2)}) copy-start(f32[172,2,1024]{2,1,0:T(2,128)S(1)} %get-tuple-element.396) | copy-start | bytes 4227076
  742.4 365.3 %all-reduce.28.cloned.1.call-start = ((), (), s32[]{:S(2)}) async-start(), calls=%async_computation.52 | async-start | bytes 22544384
  879.2 257.5 %all-gather.56.cloned.1.call-start = ((), (), s32[]{:S(2)}) async-start(), calls=%async_computation.46 | async-start | bytes 1310720 | tf_op jit(solution)/shard_map/all_gather | solution.py:188
  880.0 318.1 %all-gather.32.cloned.1.call-start = ((), (), s32[]{:S(2)}) async-start(), calls=%async_computation.20 | async-start | bytes 6340608 | tf_op jit(solution)/shard_map/all_gather | solution.py:96
  1110.1 444.0 %copy-start.10 = (f32[172,2,1024]{2,1,0:T(2,128)}, f32[172,2,1024]{2,1,0:T(2,128)S(1)}, u32[]{:S(2)}) copy-start(f32[172,2,1024]{2,1,0:T(2,128)S(1)} %get-tuple-element.394) | copy-start | bytes 4227076
  1110.1 438.7 %copy-start.73 = (f32[172,2]{1,0:T(8,128)}, f32[172,2]{1,0:T(8,128)S(1)}, u32[]{:S(2)}) copy-start(f32[172,2]{1,0:T(8,128)S(1)} %broadcast_multiply_fusion.8) | copy-start | bytes 4132
  1111.1 437.8 %copy-start.80 = (f32[172,2]{1,0:T(8,128)}, f32[172,2]{1,0:T(8,128)S(1)}, u32[]{:S(2)}) copy-start(f32[172,2]{1,0:T(8,128)S(1)} %add_rsqrt_fusion) | copy-start | bytes 4132
  1113.8 111.8 %all-gather.58.cloned.1.call-start = ((), (), s32[]{:S(2)}) async-start(), calls=%async_computation.47 | async-start | bytes 1310720 | tf_op jit(solution)/shard_map/all_gather | solution.py:189
  1114.4 172.5 %all-gather.34.cloned.1.call-start = ((), (), s32[]{:S(2)}) async-start(), calls=%async_computation.21 | async-start | bytes 6340608 | tf_op jit(solution)/shard_map/all_gather | solution.py:109
  1117.3 431.5 %all-reduce.30.cloned.1.call-start = ((), (), s32[]{:S(2)}) async-start(), calls=%async_computation.53 | async-start | bytes 22544384
  1320.1 300.6 %all-gather.36.cloned.1.call-start = ((), (), s32[]{:S(2)}) async-start(), calls=%async_computation.22 | async-start | bytes 6340608 | tf_op jit(solution)/shard_map/all_gather | solution.py:109
  1561.0 397.0 %all-reduce.32.cloned.1.call-start = ((), (), s32[]{:S(2)}) async-start(), calls=%async_computation.54 | async-start | bytes 22544384
  1729.3 301.1 %all-gather.38.cloned.1.call-start = ((), (), s32[]{:S(2)}) async-start(), calls=%async_computation.23 | async-start | bytes 6340608 | tf_op jit(solution)/shard_map/all_gather | solution.py:109
  1970.7 321.4 %all-reduce.34.cloned.1.call-start = ((), (), s32[]{:S(2)}) async-start(), calls=%async_computation.55 | async-start | bytes 22544384
  2063.7 300.6 %all-gather.40.cloned.1.call-start = ((), (), s32[]{:S(2)}) async-start(), calls=%async_computation.24 | async-start | bytes 6340608 | tf_op jit(solution)/shard_map/all_gather | solution.py:109
  2304.8 162.8 %reduce-scatter.34.cloned.1.call-start = ((), (), s32[]{:S(2)}) async-start(), calls=%async_computation.32 | async-start | bytes 2621440 | tf_op jit(solution)/shard_map/reduce_scatter | solution.py:336
  2313.0 154.6 %reduce-scatter.32.cloned.1.call-start = ((), (), s32[]{:S(2)}) async-start(), calls=%async_computation.31 | async-start | bytes 2621440 | tf_op jit(solution)/shard_map/reduce_scatter | solution.py:336
  2320.7 156.6 %reduce-scatter.30.cloned.1.call-start = ((), (), s32[]{:S(2)}) async-start(), calls=%async_computation.30 | async-start | bytes 2621440 | tf_op jit(solution)/shard_map/reduce_scatter | solution.py:335
  2329.3 186.3 %reduce-scatter.28.cloned.1.call-start = ((), (), s32[]{:S(2)}) async-start(), calls=%async_computation.29 | async-start | bytes 2621440 | tf_op jit(solution)/shard_map/reduce_scatter | solution.py:335
  2336.7 207.0 %reduce-scatter.26.cloned.1.call-start = ((), (), s32[]{:S(2)}) async-start(), calls=%async_computation.28 | async-start | bytes 655360 | tf_op jit(solution)/shard_map/reduce_scatter | solution.py:334
  2342.5 229.7 %reduce-scatter.24.cloned.1.call-start = ((), (), s32[]{:S(2)}) async-start(), calls=%async_computation.27 | async-start | bytes 655360 | tf_op jit(solution)/shard_map/reduce_scatter | solution.py:334
  2369.8 236.3 %reduce-scatter.22.cloned.1.call-start = ((), (), s32[]{:S(2)}) async-start(), calls=%async_computation.26 | async-start | bytes 1966080 | tf_op jit(solution)/shard_map/reduce_scatter | solution.py:333
  2377.7 262.1 %reduce-scatter.20.cloned.1.call-start = ((), (), s32[]{:S(2)}) async-start(), calls=%async_computation.25 | async-start | bytes 1966080 | tf_op jit(solution)/shard_map/reduce_scatter | solution.py:333
  2467.5 334.2 %reduce-scatter.36.cloned.1.call-start = ((), (), s32[]{:S(2)}) async-start(), calls=%async_computation.33 | async-start | bytes 9437184 | tf_op jit(solution)/shard_map/reduce_scatter | solution.py:134
  2712.6 171.3 %all-gather.42.cloned.1.call-start = ((), (), s32[]{:S(2)}) async-start(), calls=%async_computation.34 | async-start | bytes 9437184 | tf_op jit(solution)/shard_map/all_gather | solution.py:135
  2801.8 237.4 %reduce-scatter.38.cloned.1.call-start = ((), (), s32[]{:S(2)}) async-start(), calls=%async_computation.35 | async-start | bytes 9437184 | tf_op jit(solution)/shard_map/reduce_scatter | solution.py:134
  2950.9 168.7 %all-gather.44.cloned.1.call-start = ((), (), s32[]{:S(2)}) async-start(), calls=%async_computation.36 | async-start | bytes 9437184 | tf_op jit(solution)/shard_map/all_gather | solution.py:135
  3039.3 231.4 %reduce-scatter.40.cloned.1.call-start = ((), (), s32[]{:S(2)}) async-start(), calls=%async_computation.37 | async-start | bytes 9437184 | tf_op jit(solution)/shard_map/reduce_scatter | solution.py:134
  3182.6 168.8 %all-gather.46.cloned.1.call-start = ((), (), s32[]{:S(2)}) async-start(), calls=%async_computation.38 | async-start | bytes 9437184 | tf_op jit(solution)/shard_map/all_gather | solution.py:135
  3270.7 231.9 %reduce-scatter.42.cloned.1.call-start = ((), (), s32[]{:S(2)}) async-start(), calls=%async_computation.39 | async-start | bytes 9437184 | tf_op jit(solution)/shard_map/reduce_scatter | solution.py:134
  3414.3 168.7 %all-gather.48.cloned.1.call-start = ((), (), s32[]{:S(2)}) async-start(), calls=%async_computation.40 | async-start | bytes 9437184 | tf_op jit(solution)/shard_map/all_gather | solution.py:135
  3502.6 231.4 %reduce-scatter.44.cloned.1.call-start = ((), (), s32[]{:S(2)}) async-start(), calls=%async_computation.41 | async-start | bytes 9437184 | tf_op jit(solution)/shard_map/reduce_scatter | solution.py:134
  3645.9 168.8 %all-gather.50.cloned.1.call-start = ((), (), s32[]{:S(2)}) async-start(), calls=%async_computation.42 | async-start | bytes 9437184 | tf_op jit(solution)/shard_map/all_gather | solution.py:135
  3734.0 136.5 %reduce-scatter.48.cloned.1.call-start = ((), (), s32[]{:S(2)}) async-start(), calls=%async_computation.49 | async-start | bytes 245760
  3757.8 113.6 %reduce-scatter.46.cloned.1.call-start = ((), (), s32[]{:S(2)}) async-start(), calls=%async_computation.48 | async-start | bytes 245760
  3758.8 498.9 %all-reduce.36.cloned.1.call-start = ((), (), s32[]{:S(2)}) async-start(), calls=%async_computation.56 | async-start | bytes 45088768
  3865.1 392.6 %copy-start.11 = (f32[172,2,1024]{2,1,0:T(2,128)S(1)}, f32[172,2,1024]{2,1,0:T(2,128)}, u32[]{:S(2)}) copy-start(f32[172,2,1024]{2,1,0:T(2,128)} %copy-done.10) | copy-start | bytes 4227076
  3865.1 392.6 %copy-start.114 = (f32[1,1,1024]{2,1,0:T(1,128)S(1)}, f32[1,1,1024]{2,1,0:T(1,128)}, u32[]{:S(2)}) copy-start(f32[1,1,1024]{2,1,0:T(1,128)} %get-tuple-element.449) | copy-start | bytes 12292
  3865.1 392.6 %copy-start.132 = (f32[1,1,1024]{2,1,0:T(1,128)S(1)}, f32[1,1,1024]{2,1,0:T(1,128)}, u32[]{:S(2)}) copy-start(f32[1,1,1024]{2,1,0:T(1,128)} %get-tuple-element.446) | copy-start | bytes 12292
  3865.1 396.5 %copy-start.118 = (f32[1024]{0:T(1024)S(1)}, f32[1024]{0:T(1024)}, u32[]{:S(2)}) copy-start(f32[1024]{0:T(1024)} %get-tuple-element.298) | copy-start | bytes 12292
  3865.1 396.5 %copy-start.119 = (f32[1024]{0:T(1024)S(1)}, f32[1024]{0:T(1024)}, u32[]{:S(2)}) copy-start(f32[1024]{0:T(1024)} %get-tuple-element.299) | copy-start | bytes 12292
  3865.1 396.5 %copy-start.124 = (f32[1024]{0:T(1024)S(1)}, f32[1024]{0:T(1024)}, u32[]{:S(2)}) copy-start(f32[1024]{0:T(1024)} %get-tuple-element.276) | copy-start | bytes 12292
  3865.1 396.5 %copy-start.125 = (f32[1024]{0:T(1024)S(1)}, f32[1024]{0:T(1024)}, u32[]{:S(2)}) copy-start(f32[1024]{0:T(1024)} %get-tuple-element.286) | copy-start | bytes 12292
  3865.1 396.5 %copy-start.126 = (f32[1024]{0:T(1024)S(1)}, f32[1024]{0:T(1024)}, u32[]{:S(2)}) copy-start(f32[1024]{0:T(1024)} %get-tuple-element.278) | copy-start | bytes 12292
  3865.1 396.5 %copy-start.127 = (f32[1024]{0:T(1024)S(1)}, f32[1024]{0:T(1024)}, u32[]{:S(2)}) copy-start(f32[1024]{0:T(1024)} %get-tuple-element.287) | copy-start | bytes 12292
  3865.2 396.5 %copy-start.17 = (f32[172,2,1024]{2,1,0:T(2,128)S(1)}, f32[172,2,1024]{2,1,0:T(2,128)}, u32[]{:S(2)}) copy-start(f32[172,2,1024]{2,1,0:T(2,128)} %param.21) | copy-start | bytes 4227076
  3865.2 396.5 %copy-start.75 = (f32[172,2]{1,0:T(8,128)S(1)}, f32[172,2]{1,0:T(8,128)}, u32[]{:S(2)}) copy-start(f32[172,2]{1,0:T(8,128)} %copy-done.74) | copy-start | bytes 4132
  3865.2 396.5 %copy-start.82 = (f32[172,2]{1,0:T(8,128)S(1)}, f32[172,2]{1,0:T(8,128)}, u32[]{:S(2)}) copy-start(f32[172,2]{1,0:T(8,128)} %copy-done.81) | copy-start | bytes 4132
  3865.2 396.5 %copy-start.109 = (f32[1,1,1024]{2,1,0:T(1,128)S(1)}, f32[1,1,1024]{2,1,0:T(1,128)}, u32[]{:S(2)}) copy-start(f32[1,1,1024]{2,1,0:T(1,128)} %copy-done.108) | copy-start | bytes 12292
  3865.2 520.6 %all-to-all-start.1 = ((f32[1,2,1024,512]{3,1,0,2:T(2,128)}), f32[1,2,1024,512]{3,1,0,2:T(2,128)}, u32[]{:S(2)}, u32[]{:S(2)}) async-start(f32[1,2,1024,512]{3,1,0,2:T(2,128)} %copy.187), calls=%async_computation.14 | async-start | bytes 8388608 | tf_op jit(solution)/shard_map/all_to_all | solution.py:150
  3870.3 395.8 %copy-start.120 = (f32[1024]{0:T(1024)S(1)}, f32[1024]{0:T(1024)}, u32[]{:S(2)}) copy-start(f32[1024]{0:T(1024)} %get-tuple-element.292) | copy-start | bytes 12292
  3870.3 395.8 %copy-start.121 = (f32[1024]{0:T(1024)S(1)}, f32[1024]{0:T(1024)}, u32[]{:S(2)}) copy-start(f32[1024]{0:T(1024)} %get-tuple-element.293) | copy-start | bytes 12292
  3870.4 395.8 %copy-start.122 = (f32[1024]{0:T(1024)S(1)}, f32[1024]{0:T(1024)}, u32[]{:S(2)}) copy-start(f32[1024]{0:T(1024)} %get-tuple-element.294) | copy-start | bytes 12292
  3870.4 395.8 %copy-start.123 = (f32[1024]{0:T(1024)S(1)}, f32[1024]{0:T(1024)}, u32[]{:S(2)}) copy-start(f32[1024]{0:T(1024)} %get-tuple-element.295) | copy-start | bytes 12292
  3870.4 395.8 %copy-start.128 = (f32[1024]{0:T(1024)S(1)}, f32[1024]{0:T(1024)}, u32[]{:S(2)}) copy-start(f32[1024]{0:T(1024)} %get-tuple-element.272) | copy-start | bytes 12292
  3870.4 395.8 %copy-start.129 = (f32[1024]{0:T(1024)S(1)}, f32[1024]{0:T(1024)}, u32[]{:S(2)}) copy-start(f32[1024]{0:T(1024)} %get-tuple-element.284) | copy-start | bytes 12292
  3870.4 513.9 %all-reduce.22.cloned.1.call-start = ((), (), s32[]{:S(2)}) async-start(), calls=%async_computation.43 | async-start | bytes 131072 | tf_op jit(solution)/shard_map/psum | solution.py:342
  (142 other events, 8745.4 us)
Sparse Core Ops, SparseCore 0:
  18.0 62.0 all-gather.25
  151.2 228.5 all-reduce.23
  742.5 59.4 all-gather.29
  1320.2 228.5 all-reduce.29
  1561.1 59.4 all-gather.35
  1729.4 228.5 all-reduce.31
  1970.8 59.4 all-gather.37
  2712.7 89.0 reduce-scatter.35
  2803.4 80.3 all-gather.41
  2951.1 88.1 reduce-scatter.37
  3270.8 80.4 all-gather.45
  3414.4 88.1 reduce-scatter.41
  3734.1 80.5 all-gather.49
  3817.1 440.4 all-reduce.35
Sparse Core Ops, SparseCore 1:
  154.0 25.1 all-gather.51
  397.7 59.3 all-gather.27
  459.3 25.1 all-gather.53
  507.3 229.6 all-reduce.25
  879.3 228.3 all-reduce.27
  1110.1 26.6 all-gather.55
  1138.9 59.1 all-gather.31
  1200.4 25.1 all-gather.57
  1227.6 59.1 all-gather.33
  2063.7 228.3 all-reduce.33
  2304.9 59.3 all-gather.39
  2367.3 33.7 reduce-scatter.33
  2404.1 35.0 reduce-scatter.31
  2442.2 35.0 reduce-scatter.29
  2480.5 35.0 reduce-scatter.27
  2519.0 24.7 reduce-scatter.25
  2547.4 24.8 reduce-scatter.23
  2575.2 30.8 reduce-scatter.21
  2608.9 30.8 reduce-scatter.19
  3039.4 80.2 all-gather.43
  3182.7 87.9 reduce-scatter.39
  3502.7 80.2 all-gather.47
  3646.0 87.9 reduce-scatter.43
  3757.9 22.5 reduce-scatter.47
  3783.7 24.0 reduce-scatter.45
  4267.0 117.3 all-reduce.21
where the time goes:
time: 4410 us; the launch traced here: 4400 us
  waiting for transfers between devices  3250 us (74%)
  matrix products  615 us (14%)
  other arithmetic  210 us (5%)
  local copies, waits for them, and re-layouts  205 us (5%)
  blocking collectives  94.4 us (2%)
    unnamed x49, waiting for transfers between devices  1750 us
    reduce_scatter x5, waiting for transfers between devices, orthogonalize(): lax.psum_scatter(gram_part, 'tensor', scatter_dimension=1, tiled=True)  442 us
    all_gather x5, waiting for transfers between devices, orthogonalize(): gram = lax.all_gather(gram_rows, 'tensor', axis=1, tiled=True)  358 us
    all_gather x4, waiting for transfers between devices, project_back(): shard_rows = lax.all_gather(grad_low, 'tensor', axis=0, tiled=True)  200 us
    all_gather x4, waiting for transfers between devices, gather_rows(): return lax.all_gather(normed_low, 'tensor', axis=0, tiled=True)  193 us
    dot_general x5, matrix products, orthogonalize(): jnp.einsum('pab,pbc->pac', gram, gram, precision=HIGHEST, preferred_eleme...  149 us
    psum x1, waiting for transfers between devices, per_device(): row_grad = lax.psum(jnp.stack(row_terms[::-1]), ('dp', 'tensor'))  113 us
  transfers between devices with their start and end apart: 41, of which 35 were waited for; matrix products, arithmetic and copies ran while one was open for 8% of the time, Pallas kernels for 0%

commit v1 on v0

v1 whole, which is shorter than its diff:
```python
import math

import jax
import jax.numpy as jnp
from jax import lax
from jax.experimental import pallas as pl
from jax.experimental.pallas import tpu as pltpu
from jax.sharding import Mesh
from jax.sharding import PartitionSpec as P

D = 1024
HD = 64
FF = 4096
NS_STEPS = 5

EPS_NORM = 1e-06
EPS_GRAM = 1e-07
NS_A = 3.4445
NS_B = -4.775
NS_C = 2.0315
MOMENTUM = 0.95
MUON_RATE = 0.5
SCORE_FLOOR = -1e30
F32 = jnp.float32
LOW = jnp.bfloat16

GROUP = ("pair", "core")
ALL = ("dp", "half", "pair", "core")
KINDS = 4


def pin(*values):
    return lax.optimization_barrier(values)


def half_swap(values):
    return lax.ppermute(values, "half", [(0, 1), (1, 0)])


def core_swap(values):
    return lax.ppermute(values, "core", [(0, 1), (1, 0)])


def pair_from(values, shift):
    count = lax.axis_size("pair")
    return lax.ppermute(values, "pair", [((i + shift) % count, i) for i in range(count)])


def from_pairs(block):
    return [pair_from(block, shift) for shift in range(1, lax.axis_size("pair"))]


def on_chips(blocks):
    return jnp.concatenate([part for block in blocks for part in (block, core_swap(block))])


def chip_sum(chunk):
    rows = chunk.shape[0] // 2
    return chunk[:rows].astype(F32) + core_swap(chunk[rows:]).astype(F32)


def far_sums(chunk):
    parts = jnp.split(chunk, lax.axis_size("pair") - 1)
    return [chip_sum(part).astype(LOW) for part in parts]


def to_pairs(sums):
    count = lax.axis_size("pair")
    return [pair_from(part, count - shift) for shift, part in enumerate(sums, 1)]


def pipelined(block, work):
    arriving = from_pairs(block)
    near = on_chips([block])
    *near_out, last = work(near)
    arriving, last = pin(arriving, last)
    total = chip_sum(last)
    far = on_chips(arriving)
    *far_out, last = work(far)
    back = to_pairs(far_sums(last))
    return (near, far), (near_out, far_out), total, back


def arrived(total, back):
    return sum((part.astype(F32) for part in back), total)


def layer_norm(values, norm_gain, norm_shift):
    centered = values - jnp.mean(values, axis=-1, keepdims=True)
    inverse = lax.rsqrt(jnp.mean(centered * centered, axis=-1, keepdims=True) + EPS_NORM)
    normed = centered * inverse
    return (normed * norm_gain + norm_shift, normed, inverse)


def norm_backward(grad_out, normed, inverse, norm_gain):
    scaled = grad_out * norm_gain
    grad_in = inverse * (
        scaled
        - jnp.mean(scaled, axis=-1, keepdims=True)
        - normed * jnp.mean(scaled * normed, axis=-1, keepdims=True)
    )
    return (grad_in, jnp.sum(grad_out * normed, axis=0), jnp.sum(grad_out, axis=0))


def dot(left, right, dims):
    return lax.dot_general(left, right, (dims, ((), ())), preferred_element_type=F32)


def times(left, right):
    return dot(left, right, ((1,), (0,)))


def times_t(left, right):
    return dot(left, right, ((1,), (1,)))


def t_times(left, right):
    return dot(left, right, ((0,), (0,)))


LANES = 128
STEP = 352

def of_head(values, head):
    lane = lax.broadcasted_iota(jnp.int32, values.shape, 1)
    return jnp.where((lane < HD) == (head == 0), values, jnp.zeros_like(values))


def attend_kernel(q_ref, kn_ref, kf_ref, vn_ref, vf_ref, bn_ref, bf_ref, out_ref, lse_ref):
    query = q_ref[...]
    low_half = lax.broadcasted_iota(jnp.int32, (query.shape[0], LANES), 1) < HD
    tops, sums = [], []
    for head in range(2):
        one = of_head(query, head)
        scores = [
            times_t(one, k_ref[...]) + b_ref[...]
            for k_ref, b_ref in ((kn_ref, bn_ref), (kf_ref, bf_ref))
        ]
        top = jnp.maximum(*[jnp.max(s, axis=1, keepdims=True) for s in scores])
        total = jnp.zeros((query.shape[0], LANES), F32)
        for s, v_ref in zip(scores, (vn_ref, vf_ref)):
            value = v_ref[...]
            lane = lax.broadcasted_iota(jnp.int32, value.shape, 1)
            value = jnp.where((lane < HD) == (head == 0), value, jnp.ones_like(value))
            total = total + times(jnp.exp(s - top).astype(LOW), value)
        tops.append(top)
        sums.append(total)
    row_sum = pltpu.roll(jnp.where(low_half, sums[1], sums[0]), HD, 1)
    out_ref[...] = (jnp.where(low_half, sums[0], sums[1]) / row_sum).astype(LOW)
    lse_ref[...] = jnp.where(low_half, tops[0], tops[1]) + jnp.log(row_sum)


def attend(query, near, far, bias_near, bias_far):
    rows, width = query.shape[0], query.shape[1] // 3
    pairs = width // LANES

    def whole(array, offset):
        return pl.BlockSpec((array.shape[0], LANES), lambda p, i: (0, 3 * p + offset))

    def full(array):
        return pl.BlockSpec(array.shape, lambda p, i: (0, 0))

    block = pl.BlockSpec((min(STEP, rows), LANES), lambda p, i: (i, p))
    query_block = pl.BlockSpec(block.block_shape, lambda p, i: (i, 3 * p))
    return pl.pallas_call(
        attend_kernel,
        out_shape=(
            jax.ShapeDtypeStruct((rows, width), LOW),
            jax.ShapeDtypeStruct((rows, width), F32),
        ),
        grid=(pairs, pl.cdiv(rows, STEP)),
        in_specs=[
            query_block,
            whole(near, 1),
            whole(far, 1),
            whole(near, 2),
            whole(far, 2),
            full(bias_near),
            full(bias_far),
        ],
        out_specs=(block, block),
        compiler_params=pltpu.CompilerParams(vmem_limit_bytes=48 * 2**20),
        name="attend",
    )(query, near, far, near, far, bias_near, bias_far)


def attend_back_kernel(
    q_ref, k_ref, v_ref, bias_ref, do_ref, out_ref, lse_ref,
    grad_ref, sum_ref,
    lse_row, delta_row, dq_acc, sum_acc,
):
    step, steps = pl.program_id(1), pl.num_programs(1)
    block = k_ref.shape[0]
    query, grad = q_ref[...], do_ref[...]

    @pl.when(step == 0)
    def _():
        lse_row[...] = jnp.transpose(lse_ref[...])
        delta_row[...] = jnp.transpose(grad.astype(F32) * out_ref[...].astype(F32))
        dq_acc[...] = jnp.zeros_like(dq_acc)
        sum_acc[...] = jnp.zeros_like(sum_acc)

    key, value = k_ref[...], v_ref[...]
    key_turned = jnp.transpose(key.astype(F32)).astype(LOW)
    grad_key = jnp.zeros((block, LANES), F32)
    grad_value = jnp.zeros((block, LANES), F32)
    for head in range(2):
        lanes = pl.ds(head * HD, HD)
        query_one, grad_one = of_head(query, head), of_head(grad, head)
        soft = jnp.exp(times_t(key, query_one) + bias_ref[...] - lse_row[pl.ds(head * HD, 1), :])
        delta = jnp.sum(delta_row[lanes, :], axis=0, keepdims=True)
        slope = (soft * (times_t(value, grad_one) - delta)).astype(LOW)
        grad_value += times(soft.astype(LOW), grad_one)
        grad_key += times(slope, query_one)
        dq_acc[lanes, :] += times(key_turned[head * HD : (head + 1) * HD], slope)
    rows = pl.ds(pl.multiple_of(step * block, 16), block)
    grad_ref[rows, LANES : 2 * LANES] = grad_key.astype(LOW)
    grad_ref[rows, 2 * LANES :] = grad_value.astype(LOW)
    sum_acc[1:2, :] += jnp.sum(grad_value, axis=0, keepdims=True)

    @pl.when(step == steps - 1)
    def _():
        grad_query = jnp.transpose(dq_acc[...]) * HD**-0.5
        grad_ref[:, :LANES] = grad_query.astype(LOW)
        sum_acc[0:1, :] = jnp.sum(grad_query, axis=0, keepdims=True)
        sum_ref[...] = sum_acc[...]


def attend_back(projected, bias, grad_out, out, lse):
    rows, width = out.shape
    pairs, step = width // LANES, rows // 2

    def whole(scale):
        return pl.BlockSpec((rows, LANES), lambda p, i: (0, scale * p))

    def part(offset):
        return pl.BlockSpec((step, LANES), lambda p, i: (i, 3 * p + offset))

    return pl.pallas_call(
        attend_back_kernel,
        out_shape=(
            jax.ShapeDtypeStruct((rows, 3 * width), LOW),
            jax.ShapeDtypeStruct((8, width), F32),
        ),
        grid=(pairs, 2),
        in_specs=[
            whole(3),
            part(1),
            part(2),
            pl.BlockSpec((step, 1), lambda p, i: (i, 0)),
            whole(1),
            whole(1),
            whole(1),
        ],
        out_specs=(
            pl.BlockSpec((rows, 3 * LANES), lambda p, i: (0, p)),
            pl.BlockSpec((8, LANES), lambda p, i: (0, p)),
        ),
        scratch_shapes=[
            pltpu.VMEM((LANES, rows), F32),
            pltpu.VMEM((LANES, rows), F32),
            pltpu.VMEM((LANES, rows), F32),
            pltpu.VMEM((8, LANES), F32),
        ],
        compiler_params=pltpu.CompilerParams(vmem_limit_bytes=56 * 2**20),
        name="attend_back",
    )(projected, projected, projected, bias, grad_out, out, lse)


UNITS = 256


def gelu_and_slope(values):
    size = jnp.abs(values)
    inner = 1.0 / (1.0 + (0.3275911 * 0.5**0.5) * size)
    tail = 0.5 * 1.061405429
    for term in (-1.453152027, 1.421413741, -0.284496736, 0.254829592):
        tail = tail * inner + 0.5 * term
    bell = jnp.exp(-0.5 * values * values)
    tail = tail * inner * bell
    share = jnp.where(values < 0, tail, 1.0 - tail)
    return values * share, share + values * ((2 * math.pi) ** -0.5 * bell)


def hidden_kernel(rows_ref, own_up, own_down, far_up, far_down, bias_ref, low_ref, slope_ref, out_ref, total):
    step, steps = pl.program_id(0), pl.num_programs(0)

    @pl.when(step == 0)
    def _():
        total[...] = jnp.zeros_like(total)

    def work(up_ref, down_ref):
        value, slope = gelu_and_slope(times(rows_ref[...], up_ref[...]) + bias_ref[...])
        value = value.astype(LOW)
        low_ref[...] = value
        slope_ref[...] = slope.astype(LOW)
        total[...] += times_t(value, down_ref[...])

    @pl.when(step < steps // 2)
    def _():
        work(own_up, own_down)

    @pl.when(step >= steps // 2)
    def _():
        work(far_up, far_down)

    @pl.when(step == steps - 1)
    def _():
        out_ref[...] = total[...].astype(LOW)


def hidden_back_kernel(grad_ref, own_up, own_down, far_up, far_down, slope_ref, pre_ref, sum_ref, out_ref, total):
    step, steps = pl.program_id(0), pl.num_programs(0)

    @pl.when(step == 0)
    def _():
        total[...] = jnp.zeros_like(total)

    def work(up_ref, down_ref):
        grad_pre = times(grad_ref[...], down_ref[...]) * slope_ref[...].astype(F32)
        sum_ref[...] = jnp.broadcast_to(jnp.sum(grad_pre, axis=0, keepdims=True), sum_ref.shape)
        grad_pre = grad_pre.astype(LOW)
        pre_ref[...] = grad_pre
        total[...] += times_t(grad_pre, up_ref[...])

    @pl.when(step < steps // 2)
    def _():
        work(own_up, own_down)

    @pl.when(step >= steps // 2)
    def _():
        work(far_up, far_down)

    @pl.when(step == steps - 1)
    def _():
        out_ref[...] = total[...].astype(LOW)


def hidden_call(kernel, rows_in, sides, units, extra, extra_spec, outs, name):
    rows, width = rows_in.shape
    steps = units // UNITS
    half_steps = steps // 2
    block = pl.BlockSpec((rows, UNITS), lambda j: (0, j))
    whole = pl.BlockSpec((rows, width), lambda j: (0, 0))

    def part(at, begin):
        return pl.BlockSpec(
            (width, UNITS),
            lambda j: (0, at // UNITS + jnp.clip(j - begin, 0, half_steps - 1)),
        )

    specs, arrays = [], []
    for side, (array, at) in enumerate(sides):
        specs += [part(at, side * half_steps), part(at + units // 2, side * half_steps)]
        arrays += [array, array]
    return pl.pallas_call(
        kernel,
        out_shape=tuple(shape for shape, _ in outs),
        grid=(steps,),
        in_specs=[whole, *specs, extra_spec or block],
        out_specs=tuple(spec or block for _, spec in outs),
        scratch_shapes=[pltpu.VMEM((rows, width), F32)],
        compiler_params=pltpu.CompilerParams(vmem_limit_bytes=48 * 2**20),
        name=name,
    )(rows_in, *arrays, extra)


def hidden_layer(rows_in, sides, bias):
    rows, width = rows_in.shape
    units = jax.ShapeDtypeStruct((rows, bias.shape[1]), LOW)
    return hidden_call(
        hidden_kernel,
        rows_in,
        sides,
        bias.shape[1],
        bias,
        pl.BlockSpec((1, UNITS), lambda j: (0, j)),
        [
            (units, None),
            (units, None),
            (
                jax.ShapeDtypeStruct((rows, width), LOW),
                pl.BlockSpec((rows, width), lambda j: (0, 0)),
            ),
        ],
        "hidden_layer",
    )


def hidden_back(grad, sides, slope):
    rows, width = grad.shape
    grad_pre, total, out = hidden_call(
        hidden_back_kernel,
        grad,
        sides,
        slope.shape[1],
        slope,
        None,
        [
            (jax.ShapeDtypeStruct(slope.shape, LOW), None),
            (
                jax.ShapeDtypeStruct((8, slope.shape[1]), F32),
                pl.BlockSpec((8, UNITS), lambda j: (0, j)),
            ),
            (
                jax.ShapeDtypeStruct((rows, width), LOW),
                pl.BlockSpec((rows, width), lambda j: (0, 0)),
            ),
        ],
        "hidden_back",
    )
    return grad_pre, total[0], out


def gram_sum(partial, axes, aside):
    middle, quarter = partial.shape[0] // 2, partial.shape[0] // 4
    first_block, side_block = partial[:middle, :middle], partial[:middle, middle:]
    last_block = partial[middle:, middle:]
    if lax.axis_size("pair") != 2 or len(axes) > len(GROUP):
        return pin(lax.psum((first_block, side_block, last_block), axes), aside)
    first = lax.axis_index("core") == 0
    upper = jnp.concatenate([first_block, side_block[:quarter]])
    lower = jnp.concatenate([last_block, side_block[quarter:]])
    mine = jnp.where(first, upper, lower) + core_swap(jnp.where(first, lower, upper))
    far, aside = pin(pair_from(mine, 1), aside)
    mine = mine + far
    other = core_swap(mine)
    upper, lower = jnp.where(first, mine, other), jnp.where(first, other, mine)
    side_block = jnp.concatenate([upper[middle:], lower[middle:]])
    return (upper[:middle], side_block, lower[:middle]), aside


def sum_over(values, axes):
    for axis in axes:
        count, bit = lax.axis_size(axis), 1
        while bit < count:
            values = values + lax.ppermute(values, axis, [(i, i ^ bit) for i in range(count)])
            bit *= 2
    return values


def gram_of(matrix):
    low = matrix.astype(LOW)
    return times_t(low, low)


CHUNK = 256


def newton_schulz_kernel(
    first_ref, side_ref, last_ref, start_ref, out_ref,
    gram, poly, turn, gram_rest, poly_rest, turn_rest, current, current_low,
    gram_col, poly_col, turn_col, gram_row, poly_row,
):
    middle = first_ref.shape[0]
    chunks = 2 * middle // CHUNK
    gram[:middle, :middle] = first_ref[...]
    gram[:middle, middle:] = side_ref[...]
    gram[middle:, :middle] = jnp.transpose(side_ref[...])
    gram[middle:, middle:] = last_ref[...]
    on = lax.broadcasted_iota(jnp.int32, (CHUNK, CHUNK), 0) == lax.broadcasted_iota(
        jnp.int32, (CHUNK, CHUNK), 1
    )

    def part(i):
        return pl.ds(pl.multiple_of(i * CHUNK, CHUNK), CHUNK)

    def each(work):
        def step(i, carry):
            work(part(i))
            return carry

        lax.fori_loop(0, chunks, step, 0)

    def keep(rows, value, excess, whole, rest, col, row):
        whole[rows, :] = value
        rest[rows, :] = value.astype(LOW)
        block = whole[rows, rows] - jnp.where(on, excess, 0.0)
        whole[rows, rows] = block
        rest[rows, rows] = jnp.where(on, 0.0, block).astype(LOW)
        diagonal = jnp.where(on, block, 0.0)
        col[rows, :] = jnp.sum(diagonal, axis=1, keepdims=True)
        if row is not None:
            row[:, rows] = jnp.sum(diagonal, axis=0, keepdims=True)

    def product(rows, left, left_rest, left_col, right, right_rest, right_row):
        return (
            times(left_rest[rows, :], right_rest[...])
            + left_col[rows, :] * right[rows, :]
            + left[rows, :] * right_row[...]
        )

    trace = jnp.zeros((1, 1), F32)
    for i in range(chunks):
        at = slice(i * CHUNK, (i + 1) * CHUNK)
        diagonal = jnp.where(on, gram[at, at], 0.0)
        trace += jnp.sum(jnp.sum(diagonal, axis=1, keepdims=True), axis=0, keepdims=True)
    inverse = lax.rsqrt(trace + EPS_GRAM)

    def begin(rows):
        scaled = gram[rows, :] * (inverse * inverse)
        keep(rows, scaled, 0.0, gram, gram_rest, gram_col, gram_row)
        value = start_ref[rows, :] * inverse
        current[rows, :] = value
        current_low[0, rows, :] = value.astype(LOW)

    each(begin)

    def polynomial(rows):
        square = product(rows, gram, gram_rest, gram_col, gram, gram_rest, gram_row)
        excess = NS_C * gram_col[rows, :] * gram_col[rows, :]
        value = NS_B * gram[rows, :] + NS_C * square
        keep(rows, value, excess, poly, poly_rest, poly_col, poly_row)

    def advanced(rows, slot):
        moved = times(poly_rest[rows, :], current_low[slot])
        return (NS_A + poly_col[rows, :]) * current[rows, :] + moved

    def iterate(iteration, carry):
        slot = lax.rem(iteration, 2)
        each(polynomial)

        def advance(rows):
            value = advanced(rows, slot)
            current[rows, :] = value
            current_low[1 - slot, rows, :] = value.astype(LOW)

        each(advance)

        def first(rows):
            value = product(rows, poly, poly_rest, poly_col, gram, gram_rest, gram_row)
            excess = poly_col[rows, :] * gram_col[rows, :]
            keep(rows, NS_A * gram[rows, :] + value, excess, turn, turn_rest, turn_col, None)

        each(first)

        def second(rows):
            value = product(rows, turn, turn_rest, turn_col, poly, poly_rest, poly_row)
            excess = turn_col[rows, :] * poly_col[rows, :]
            keep(rows, NS_A * turn[rows, :] + value, excess, gram, gram_rest, gram_col, gram_row)

        each(second)
        return carry

    lax.fori_loop(0, NS_STEPS - 1, iterate, 0)
    each(polynomial)

    def finish(rows):
        out_ref[rows, :] = advanced(rows, (NS_STEPS - 1) % 2).astype(LOW)

    each(finish)


def orthogonalize(start, gram):
    size, width = start.shape
    square = [pltpu.VMEM((size, size), F32)] * 3 + [pltpu.VMEM((size, size), LOW)] * 3
    return pl.pallas_call(
        newton_schulz_kernel,
        out_shape=jax.ShapeDtypeStruct((size, width), LOW),
        in_specs=[pl.BlockSpec(memory_space=pltpu.VMEM)] * 4,
        out_specs=pl.BlockSpec(memory_space=pltpu.VMEM),
        scratch_shapes=square
        + [pltpu.VMEM((size, width), F32), pltpu.VMEM((2, size, width), LOW)]
        + [pltpu.VMEM((size, 1), F32)] * 3
        + [pltpu.VMEM((1, size), F32)] * 2,
        compiler_params=pltpu.CompilerParams(vmem_limit_bytes=56 * 2**20),
        name="newton_schulz",
    )(*gram, start)


def per_device(
    tokens,
    cotangent,
    attention_in,
    attention_out,
    hidden_up,
    hidden_down,
    attention_in_momentum,
    attention_out_momentum,
    hidden_up_momentum,
    hidden_down_momentum,
    row_params,
    column_bias,
    lengths,
):
    local_rows, image_count, _ = tokens.shape
    pair_count = lax.axis_size("pair")
    data_count = lax.axis_size("dp")
    half = lax.axis_index("half")
    layer_count = attention_in.shape[0]
    rows_owned = hidden_up.shape[1]
    head_own = column_bias.shape[1]
    heads = 2 * head_own
    head_width = heads * HD
    seq_total = local_rows * 4 * pair_count

    def away(values):
        own = jnp.where(half == 0, values[:, 0], values[:, 1])
        return own, jnp.where(half == 0, values[:, 1], values[:, 0]).astype(LOW)

    def together(own, other):
        return jnp.concatenate([own, other.astype(F32)], axis=0)

    def at_home(own, other):
        other = other.astype(F32)
        return jnp.where(
            half == 0, jnp.stack([own, other], axis=1), jnp.stack([other, own], axis=1)
        )

    place = []
    for shift in range(pair_count):
        chip = lax.rem(lax.axis_index("pair") + shift, pair_count)
        for flip in range(2):
            core = lax.axis_index("core") ^ flip
            for other in range(2):
                block = ((half ^ other) * pair_count + chip) * 2 + core
                place.append(block * local_rows + jnp.arange(local_rows, dtype=jnp.int32))
    length = jnp.where(half == 0, lengths[0], lengths[1])
    key_bias = jnp.where(jnp.concatenate(place) < length, 0.0, SCORE_FLOOR).astype(F32)
    near_rows = 4 * local_rows
    bias_near, bias_far = key_bias[None, :near_rows], key_bias[None, near_rows:]

    column_other = half_swap(column_bias)
    column_all = jnp.concatenate([column_bias, column_other], axis=1)
    data_index = lax.axis_index("dp")
    kinds = range(KINDS)
    side_width = 3 * head_own * HD
    by_side = head_own * HD == LANES
    matrix_count = layer_count * KINDS
    wide = data_count * 2 == matrix_count
    pad_width = hidden_up.shape[2]
    column_axes = GROUP if wide else GROUP + ("half",)

    def dp_xor(values, offset):
        return lax.ppermute(values, "dp", [(i, i ^ offset) for i in range(data_count)])

    def data_gather(piece):
        return lax.all_gather(piece, "dp", axis=0, tiled=True)

    def data_sum(partial):
        return lax.psum_scatter(partial, "dp", scatter_dimension=0, tiled=True)

    def sides(own, other):
        if not by_side:
            own, other = (w.reshape(-1, 3, head_own * HD) for w in (own, other))
        return jnp.concatenate([own, other], axis=-1).reshape(own.shape[0], 2 * side_width)

    def own_weights(block_index):
        first = attention_in[block_index].astype(LOW).reshape(rows_owned, head_own, 3, HD)
        first = jnp.swapaxes(first, 1, 2).reshape(rows_owned, -1)
        return (
            jnp.concatenate([first, attention_out[block_index].astype(LOW)], axis=1),
            jnp.concatenate(
                [hidden_up[block_index].astype(LOW), hidden_down[block_index].astype(LOW)], axis=1
            ),
        )

    def attention_matrices(own, other):
        return (
            sides(own[:, :side_width], other[:, :side_width]),
            jnp.concatenate([own[:, side_width:], other[:, side_width:]], axis=1),
        )

    moments_old = (
        attention_in_momentum,
        attention_out_momentum,
        hidden_up_momentum,
        hidden_down_momentum,
    )

    def padded(array):
        return jnp.pad(array, ((0, 0), (0, pad_width - array.shape[1])))

    def moment_away():
        first, second = (
            jnp.concatenate([m[layer] for m in moments_old], axis=1).astype(LOW)
            for layer in range(2)
        )
        return jnp.where(half == 0, first, second), jnp.where(half == 0, second, first)

    def moment_items(own, other):
        items, at = [], 0
        for kind, moment in enumerate(moments_old):
            width = moment.shape[2]
            if wide:
                pair = [padded(array[:, at : at + width]) for array in (own, other)]
                items.append((kind, jnp.concatenate(pair, axis=1)))
            else:
                items += [
                    (l * KINDS + kind, padded(moment[l].astype(LOW))) for l in range(layer_count)
                ]
            at += width
        return items

    def to_owner(items):
        stack = jnp.stack([rows for _, rows in sorted(items, key=lambda item: item[0])])
        blocks = []
        for offset in range(data_count):
            block = lax.dynamic_index_in_dim(stack, data_index ^ offset, 0, keepdims=False)
            blocks.append(dp_xor(block, offset) if offset else block)
        return blocks

    def from_owner(matrix):
        blocks = jnp.split(matrix, data_count)

        def gathered(parts):
            return [
                lax.dynamic_index_in_dim(jnp.stack(parts), data_index ^ owner, 0, keepdims=False)
                for owner in range(data_count)
            ]

        if not wide:
            parts = gathered([dp_xor(b, i) if i else b for i, b in enumerate(blocks)])
            return [parts[layer * KINDS : (layer + 1) * KINDS] for layer in range(layer_count)]
        far, near = [], []
        for offset, block in enumerate(blocks):
            pairs = [
                (2 * i + h, 2 * (i ^ offset) + 1 - h) for i in range(data_count) for h in range(2)
            ]
            far.append(lax.ppermute(block[:, pad_width:], ("dp", "half"), pairs))
        for offset, block in enumerate(blocks):
            near.append(
                dp_xor(block[:, :pad_width], offset) if offset else block[:, :pad_width]
            )
        near, far = gathered(near), gathered(far)
        return [
            [jnp.where(half == layer, n, f) for n, f in zip(near, far)]
            for layer in range(layer_count)
        ]

    own_low = [own_weights(block_index) for block_index in range(layer_count)]
    params = row_params
    part_of = jnp.arange(3 * head_width) % (3 * LANES) // LANES
    query_scale = jnp.where(part_of == 0, HD**-0.5, 1.0).astype(LOW)
    own_tokens, other_tokens = away(tokens)
    other_tokens = half_swap(other_tokens)
    first_own = data_gather(own_low[0][0])
    first_other = half_swap(own_low[0][0])
    first_own, first_other, own = pin(first_own, first_other, own_low[0][1])
    first_other = data_gather(first_other)
    hidden_other = half_swap(own)
    hidden_own = data_gather(own)
    residual = together(own_tokens, other_tokens)
    kept = []

    for block_index in range(layer_count):
        last = block_index == layer_count - 1
        row_set = params[block_index]
        col_set = column_all[block_index]
        unit_bias = col_set[:, 2 * HD :].reshape(1, -1)
        query_bias = col_set[:, :HD].reshape(-1, LANES)
        value_bias = col_set[:, HD : 2 * HD].reshape(-1, LANES)
        in_bias = jnp.concatenate(
            [query_bias, jnp.zeros_like(query_bias), value_bias], axis=1
        ).reshape(-1)
        norm_one, normed_first, inverse_first = layer_norm(residual, row_set[0], row_set[1])
        block = norm_one.astype(LOW)
        arriving = from_pairs(block)
        near = on_chips([block])
        w_in, w_out = attention_matrices(first_own, first_other)

        def project(rows):
            return (times(rows, w_in) + in_bias).astype(LOW) * query_scale

        query_near = project(near)
        if block_index > 0:
            query_near, own = pin(query_near, own_low[block_index][1])
            hidden_other = half_swap(own)
            hidden_own = data_gather(own)
        arriving, query_near = pin(arriving, query_near)
        far = on_chips(arriving)
        query_far = project(far)
        heads_far, lse_far = attend(query_far, query_near, query_far, bias_near, bias_far)
        if last:
            heads_far, hidden_other, (own_cotangent, other) = pin(
                heads_far, hidden_other, away(cotangent)
            )
            aside = half_swap(other)
        else:
            heads_far, hidden_other, first_own = pin(
                heads_far, hidden_other, own_low[block_index + 1][0]
            )
            aside = half_swap(first_own)
            first_own = data_gather(first_own)
        hidden_other = data_gather(hidden_other)
        sums, query_held = pin(far_sums(times_t(heads_far, w_out).astype(LOW)), query_near)
        back = to_pairs(sums)
        heads_near, lse_near = attend(query_held, query_near, query_far, bias_near, bias_far)
        heads_near, back, aside = pin(heads_near, back, aside)
        if last:
            other_cotangent = aside
        else:
            first_other = data_gather(aside)
        total = chip_sum(times_t(heads_near, w_out).astype(LOW))
        branch_one = arrived(total, back) + row_set[2]
        middle = residual + row_set[3] * branch_one
        norm_two, normed_second, inverse_second = layer_norm(middle, row_set[4], row_set[5])
        hidden_full = ((hidden_own, 0), (hidden_other, 0))
        second, second_out, total, back = pipelined(
            norm_two.astype(LOW),
            lambda rows: hidden_layer(rows, hidden_full, unit_bias),
        )
        branch_two = arrived(total, back) + row_set[6]
        residual = middle + row_set[7] * branch_two
        kept.append(
            (
                (w_in, w_out, hidden_full),
                normed_first,
                inverse_first,
                jnp.concatenate([near, far]),
                jnp.concatenate([query_near, query_far]),
                jnp.concatenate([lse_near, lse_far]),
                jnp.concatenate([heads_near, heads_far]),
                branch_one,
                normed_second,
                inverse_second,
                second,
                second_out,
                branch_two,
            )
        )
    grad_residual = together(own_cotangent, other_cotangent)

    row_terms = [None] * layer_count
    column_terms = [None] * layer_count
    owner_layers = [[None] * layer_count for _ in kinds]

    def to_half(reduced, layer):
        width = reduced.shape[1] // 2
        swapped = jnp.concatenate([reduced[:, width:], reduced[:, :width]], axis=1)
        return reduced, lax.ppermute(swapped, "half", [(1 - layer, layer)])

    def attention_grads(rows_in, rows_out, grad_proj, head_rows):
        in_grad, out_grad = t_times(rows_in, grad_proj), t_times(rows_out, head_rows)
        if not by_side:
            in_grad = in_grad.reshape(D, 3, 2, head_own * HD).transpose(0, 2, 1, 3).reshape(D, -1)
        first, second = jnp.split(in_grad, 2, axis=1), jnp.split(out_grad, 2, axis=1)
        return jnp.concatenate([first[0], second[0], first[1], second[1]], axis=1).astype(LOW)

    def settle(layer, both, part):
        full = both[0].astype(F32) + both[1].astype(F32)
        own, other = jnp.split(full, 2, axis=1)
        if part == "attention":
            owner_layers[0][layer] = (own[:, :side_width], other[:, :side_width])
            owner_layers[1][layer] = (own[:, side_width:], other[:, side_width:])
        else:
            owner_layers[part][layer] = (own, other)

    def heads_first(array):
        return jnp.swapaxes(array.reshape(-1, 3, head_own, HD), 1, 2).reshape(array.shape)

    def give_back(layer, owned):
        sent = jnp.concatenate([owned[k][layer][1].astype(LOW) for k in kinds], axis=1)
        return lax.ppermute(sent, "half", [(layer, 1 - layer)])

    def home_grads(layer, arrived_low):
        grads, at = [], 0
        for kind in kinds:
            own = owner_layers[kind][layer][0]
            width = own.shape[1]
            own = jnp.where(half == layer, own, arrived_low[:, at : at + width].astype(F32))
            at += width
            grads.append(heads_first(own) if kind == 0 else own)
        return grads

    def owner_items(kind):
        pair = [
            jnp.where(half == 0, first, second).astype(LOW)
            for first, second in zip(*owner_layers[kind])
        ]
        if kind == 0:
            pair = [heads_first(part) for part in pair]
        return [(kind, jnp.concatenate([padded(part) for part in pair], axis=1))]

    top = layer_count - 1
    for block_index in reversed(range(layer_count)):
        last = block_index == top
        (
            (w_in, w_out, hidden_full),
            normed_first,
            inverse_first,
            first,
            projected,
            lse,
            head_rows,
            branch_one,
            normed_second,
            inverse_second,
            second,
            second_out,
            branch_two,
        ) = kept[block_index]
        row_set = params[block_index]
        near_rows = 4 * local_rows
        grad_two = grad_residual * row_set[7]
        slopes = iter([chunk[1] for chunk in second_out])
        reach, back_out, total, back = pipelined(
            grad_two.astype(LOW),
            lambda rows: hidden_back(rows, hidden_full, next(slopes)),
        )
        scale_two = jnp.sum(grad_residual * branch_two, axis=0)
        shift_down = jnp.sum(grad_two, axis=0)
        unit_grad = sum(chunk[1] for chunk in back_out)
        down_grad = t_times(jnp.concatenate(reach), jnp.concatenate([c[0] for c in second_out]))
        back, down_grad = pin(back, down_grad.astype(LOW))
        if not last:
            down_sum = data_sum(down_grad)
            back, sums_late = pin(back, jnp.split(sums_late, 3))
            down_late = to_half(sums_late[0], top)
        grad_norm = arrived(total, back)
        grad_in, gain_two, shift_two = norm_backward(
            grad_norm, normed_second, inverse_second, row_set[4]
        )
        grad_residual = grad_residual + grad_in

        grad_one = grad_residual * row_set[3]
        block = grad_one.astype(LOW)
        arriving = from_pairs(block)
        scale_one = jnp.sum(grad_residual * branch_one, axis=0)
        shift_out = jnp.sum(grad_one, axis=0)
        near = on_chips([block])
        heads_near = times(near, w_out).astype(LOW)
        up_grad = t_times(jnp.concatenate(second), jnp.concatenate([c[0] for c in back_out]))
        arriving, heads_near, up_grad = pin(arriving, heads_near, up_grad.astype(LOW))
        if not last:
            heads_near, down_late = pin(heads_near, down_late)
            settle(top, down_late, 3)
            up_late = to_half(sums_late[1], top)
        far = on_chips(arriving)
        grad_heads = jnp.concatenate([heads_near, times(far, w_out).astype(LOW)])
        if not last:
            up_sum = data_sum(up_grad)
            grad_heads, down_sum = pin(grad_heads, down_sum)
            down_half = to_half(down_sum, block_index)
        if last:
            grad_heads, (own_moment, away_moment) = pin(grad_heads, moment_away())
            other_moment = half_swap(away_moment)
        else:
            grad_heads, own_moment, other_moment = pin(grad_heads, own_moment, other_moment)
            owner_moment = to_owner(moment_items(own_moment, other_moment))
        grad_proj, head_sums = attend_back(projected, key_bias[:, None], grad_heads, head_rows, lse)
        if last:
            grad_proj, other_moment, residual = pin(grad_proj, other_moment, residual)
            output_other = half_swap(residual[local_rows:].astype(LOW))
        else:
            grad_proj, owner_moment, up_late, down_half, up_sum = pin(
                grad_proj, owner_moment, up_late, down_half, up_sum
            )
            up_half = to_half(up_sum, block_index)
            settle(top, up_late, 2)
            attention_late = to_half(sums_late[2], top)
        reach = jnp.concatenate([near, far])
        if not last:
            attention_low = attention_grads(first, reach, grad_proj, head_rows)
            attention_low, grad_proj = pin(attention_low, grad_proj)
            attention_sum = data_sum(attention_low)
        sums, (grad_proj, reach, head_rows, first) = pin(
            far_sums(times_t(grad_proj[near_rows:], w_in).astype(LOW)),
            (grad_proj, reach, head_rows, first),
        )
        back = to_pairs(sums)
        total = chip_sum(times_t(grad_proj[:near_rows], w_in).astype(LOW))
        if last:
            attention_low = attention_grads(first, reach, grad_proj, head_rows)
            blocks = zip(*[jnp.split(g, data_count) for g in (down_grad, up_grad, attention_low)])
            sums_late = data_sum(jnp.concatenate([g for block in blocks for g in block]))
            back, total, attention_low, output_other = pin(back, total, attention_low, output_other)
            layer_output = at_home(residual[:local_rows], output_other)
        else:
            settle(block_index, down_half, 3)
            total, attention_late, up_half = pin(total, attention_late, up_half)
            settle(top, attention_late, "attention")
            settle(block_index, up_half, 2)
            total, attention_sum = pin(total, attention_sum)
            attention_half = to_half(attention_sum, 0)
            back, total = pin(back, total)
        grad_norm = sum((part.astype(F32) for part in back), total)
        grad_in, gain_one, shift_one = norm_backward(
            grad_norm, normed_first, inverse_first, row_set[0]
        )
        grad_residual = grad_residual + grad_in
        row_terms[block_index] = jnp.stack(
            [
                gain_one,
                shift_one,
                shift_out,
                scale_one,
                gain_two,
                shift_two,
                shift_down,
                scale_two,
            ]
        )
        column_terms[block_index] = jnp.concatenate(
            [
                head_sums[0].reshape(heads, HD),
                head_sums[1].reshape(heads, HD),
                unit_grad.reshape(heads, -1),
            ],
            axis=1,
        )
    settle(0, attention_half, "attention")
    if wide:
        owner_grad = to_owner([item for kind in kinds for item in owner_items(kind)])
        owner_grad, owner_layers, grad_residual, row_terms, column_terms = pin(
            owner_grad, owner_layers, grad_residual, row_terms, column_terms
        )
    else:
        grads = [home_grads(layer, give_back(layer, owner_layers)) for layer in range(layer_count)]
        owner_grad = to_owner(
            [
                (layer * KINDS + kind, padded(grads[layer][kind].astype(LOW)))
                for layer in range(layer_count)
                for kind in kinds
            ]
        )
    start = jnp.concatenate(
        [MOMENTUM * m.astype(F32) + g.astype(F32) for m, g in zip(owner_moment, owner_grad)]
    )
    gram_part = gram_of(start)
    grad_residual, row_terms, column_terms, gram_part = pin(
        grad_residual, row_terms, column_terms, gram_part
    )
    columns = jnp.stack(column_terms)
    flat = jnp.pad(columns.reshape(-1), (0, -columns.size % D)).reshape(-1, D)
    small = sum_over(jnp.concatenate([jnp.stack(row_terms).reshape(-1, D), flat]), ("dp",))
    rows_small = 8 * layer_count
    columns = small[rows_small:].reshape(-1)[: columns.size].reshape(columns.shape)
    owned_width = column_bias.shape[2] // data_count
    columns = lax.dynamic_slice_in_dim(columns, data_index * owned_width, owned_width, 2)
    column_grad = columns[:, :head_own] + half_swap(columns[:, head_own:])
    row_grad = sum_over(small[:rows_small], ("core", "pair", "half")).reshape(row_params.shape)
    gram, (row_grad, column_grad) = gram_sum(gram_part, column_axes, (row_grad, column_grad))
    tokens_other = grad_residual[local_rows:].astype(LOW)
    gram, row_grad, column_grad, tokens_other, owner_layers = pin(
        gram, row_grad, column_grad, tokens_other, owner_layers
    )
    tokens_other = half_swap(tokens_other)
    returning = [give_back(layer, owner_layers) for layer in range(layer_count)] if wide else []
    finish, returning, tokens_other = pin(orthogonalize(start, gram), returning, tokens_other)
    returned = from_owner(finish)
    if wide:
        grads = [home_grads(layer, arrived_low) for layer, arrived_low in enumerate(returning)]
    tokens_grad = at_home(grad_residual[:local_rows], tokens_other)
    grads = [jnp.stack(layers) for layers in zip(*grads)]
    moments = [MOMENTUM * m + g for m, g in zip(moments_old, grads)]
    olds = (attention_in, attention_out, hidden_up, hidden_down)
    fans = (D, D // 16, D, FF)
    news = []
    for kind in range(KINDS):
        width = olds[kind].shape[2]
        rate = MUON_RATE * math.sqrt(max(D, width * 4 * pair_count) / fans[kind])
        step = jnp.stack([returned[layer][kind][:, :width] for layer in range(layer_count)])
        news.append(olds[kind] - rate * step.astype(F32))
    small_rate = 0.3 / math.sqrt(image_count * data_count * seq_total)
    row_new = row_params - small_rate * row_grad
    owned_width = column_grad.shape[2]
    column_old = lax.dynamic_slice_in_dim(
        column_bias, lax.axis_index("dp") * owned_width, owned_width, 2
    )
    column_new = column_old - small_rate * column_grad
    return (
        layer_output,
        tokens_grad,
        *grads,
        *moments,
        *news,
        row_grad,
        row_new,
        column_grad,
        column_new,
    )


def solution(mesh):
    data_count, tensor_count = mesh.shape["dp"], mesh.shape["tensor"]
    cut = Mesh(mesh.devices.reshape(data_count, 2, tensor_count // 4, 2), ALL)
    tensor = ("half", "pair", "core")
    token_spec = P(tensor, "dp", None)
    matrix_spec = P(None, "dp", tensor)
    in_specs = (
        (token_spec,) * 2 + (matrix_spec,) * 8 + (P(), P(None, tensor, None), P("dp"))
    )
    out_specs = (
        (token_spec,) * 2 + (matrix_spec,) * 12 + (P(), P()) + (P(None, tensor, "dp"),) * 2
    )
    return jax.shard_map(
        per_device, mesh=cut, in_specs=in_specs, out_specs=out_specs, check_vma=False
    )
```

time: 4410 us -> 1060 us (0.24)
  waiting for transfers between devices: 3250 us -> 335 us
  matrix products: 615 us -> 70.7 us
  Pallas kernels: 0 us -> 248 us
  starting transfers between devices: 8.2 us -> 131 us
  blocking collectives: 94.4 us -> 0 us
  local copies, waits for them, and re-layouts: 205 us -> 116 us
  other arithmetic: 210 us -> 125 us
    unnamed x49 -> x12, waiting for transfers between devices: 1750 us -> 0.2 us
    all_gather x17 -> x8, waiting for transfers between devices: 776 us -> 48.8 us  [data_gather(): return lax.all_gather(piece, 'dp', axis=0, tiled=True)]
    reduce_scatter x13 -> x4, waiting for transfers between devices: 605 us -> 4 us  [data_sum(): return lax.psum_scatter(partial, 'dp', scatter_dimension=0, tiled=True)]
    dot_general x67 -> x25, matrix products: 615 us -> 70.7 us  [dot(): lax.dot_general(left, right, (dims, ((), ())), preferred_element_type=F32)]
    ppermute x0 -> x88, waiting for transfers between devices: none -> 282 us  [the longest x17 88.9 us: pair_from(): lax.ppermute(values, 'pair', [((i + shift) % count, i) for i in range(cou...]
    pallas_call x0 -> x15, Pallas kernels: none -> 248 us  [the longest x8 77.9 us: hidden_call(): pl.pallas_call(kernel, out_shape=tuple((shape for shape, _ in outs)), gri...]
    dot_general x8 -> x0, local copies, waits for them, and re-layouts: 140 us -> none  [the longest x4 70.2 us: sum_inputs(): jnp.einsum('sic,dc->sid', grad_low, weight_cols, preferred_element_type=j...]
    ppermute x0 -> x88, starting transfers between devices: none -> 129 us  [the longest x17 57.1 us: pair_from(): lax.ppermute(values, 'pair', [((i + shift) % count, i) for i in range(cou...]
  transfers between devices with their start and end apart: 41 -> 100, of which waited for: 35 -> 51; matrix products, arithmetic and copies ran while one was open for 8% -> 19% of each run, Pallas kernels for 0% -> 21%
where the time goes in v1:
time: 1060 us; the launch traced here: 1050 us
  waiting for transfers between devices  335 us (32%)
  Pallas kernels  248 us (23%)
  starting transfers between devices  131 us (12%)
  other arithmetic  125 us (12%)
  local copies, waits for them, and re-layouts  116 us (11%)
  matrix products  70.7 us (7%)
  between operations  20 us (2%)
    ppermute x17, waiting for transfers between devices, pair_from(): lax.ppermute(values, 'pair', [((i + shift) % count, i) for i in range(cou...  88.9 us
    pallas_call x8, Pallas kernels, hidden_call(): pl.pallas_call(kernel, out_shape=tuple((shape for shape, _ in outs)), gri...  77.9 us
    pallas_call x1, Pallas kernels, orthogonalize(): pl.pallas_call(newton_schulz_kernel, out_shape=jax.ShapeDtypeStruct((size...  73.5 us
    dot_general x25, matrix products, dot(): lax.dot_general(left, right, (dims, ((), ())), preferred_element_type=F32)  70.7 us
    ppermute x11, waiting for transfers between devices, half_swap(): return lax.ppermute(values, 'half', [(0, 1), (1, 0)])  66.6 us
    ppermute x17, starting transfers between devices, pair_from(): lax.ppermute(values, 'pair', [((i + shift) % count, i) for i in range(cou...  57.1 us
    unnamed x574, local copies, waits for them, and re-layouts  56.4 us
    pallas_call x2, Pallas kernels, attend_back(): pl.pallas_call(attend_back_kernel, out_shape=(jax.ShapeDtypeStruct((rows,...  53.4 us
  transfers between devices with their start and end apart: 100, of which 51 were waited for; matrix products, arithmetic and copies ran while one was open for 19% of the time, Pallas kernels for 21%

profile of v1, /device:TPU:0, one launch (start us, length us, event | category | flops | bytes accessed | tf_op | source)
XLA Modules:
  0.0 1045.5 jit_solution(850704762883213681)
XLA Ops:
  10.8 4.0 collective-permute-start.3
  26.0 16.7 %collective-permute-done = bf16[172,1024]{1,0:T(8,128)(2,1)} collective-permute-done((bf16[172,1024]{1,0:T(8,128)(2,1)}, bf16[172,1024]{1,0:T(8,128)(2,1)}, u32[]{:S(2)}, u32[]{:S(2)}) %collective-permute-start) | collective-permute-done | bytes 352288 | tf_op jit(solution)/shard_map/ppermute | solution.py:37
  48.1 23.7 %all-gather.11.cloned.1.call-done = bf16[1024,512]{0,1:T(8,128)(2,1)} async-done(((bf16[256,512]{0,1:T(8,128)(2,1)}), bf16[1024,512]{0,1:T(8,128)(2,1)}) %all-gather.11.cloned.1.call-update) | async-done | bytes 1048592 | tf_op jit(solution)/shard_map/all_gather | solution.py:638
  83.4 3.1 fusion.97.q_ref.kf_ref.vf_ref
  86.5 10.7 %attend.4 = (bf16[688,256]{1,0:T(8,128)(2,1)S(1)}, f32[688,256]{1,0:T(8,128)S(1)}) custom-call(bf16[688,768]{1,0:T(8,128)(2,1)S(1)} %fusion.97.q_ref.kf_ref.vf_ref, bf16[688,768]{1,0:T(8,128)(2,1)S(1)} %fusion.94.kn_ref.vn_ref.q_ref, bf16[688,768]{1,0:T(8,128)(2,1)S(1)} %fusion.97.q_ref.kf_ref.vf_ref, bf16[688,768]{1,0:T(8,128)(2,1)S(1)} %fusion.94.kn_ref.vn_ref.q_ref, ...), custom_call_target="tpu_custom_call" | custom-call | tf_op jit(solution)/shard_map/attend/pallas_call | solution.py:165
  98.1 7.0 collective-permute-done.6
  110.5 3.4 collective-permute-start.9
  114.4 10.7 %attend.5 = (bf16[688,256]{1,0:T(8,128)(2,1)S(1)}, f32[688,256]{1,0:T(8,128)S(1)}) custom-call(bf16[688,768]{1,0:T(8,128)(2,1)S(1)} %fusion.94.kn_ref.vn_ref.q_ref, bf16[688,768]{1,0:T(8,128)(2,1)S(1)} %fusion.94.kn_ref.vn_ref.q_ref, bf16[688,768]{1,0:T(8,128)(2,1)S(1)} %fusion.97.q_ref.kf_ref.vf_ref, bf16[688,768]{1,0:T(8,128)(2,1)S(1)} %fusion.94.kn_ref.vn_ref.q_ref, ...), custom_call_target="tpu_custom_call" | custom-call | tf_op jit(solution)/shard_map/attend/pallas_call | solution.py:165
  126.0 5.8 collective-permute-done.9
  146.7 10.6 %hidden_layer.4 = (bf16[688,1024]{1,0:T(8,128)(2,1)S(1)}, bf16[688,1024]{1,0:T(8,128)(2,1)S(1)}, bf16[688,1024]{1,0:T(8,128)(2,1)S(1)}) custom-call(bf16[688,1024]{1,0:T(8,128)(2,1)S(1)} %pad_maximum_fusion.16.rows_ref, bf16[1024,1024]{1,0:T(8,128)(2,1)} %all-gather.13.cloned.1.call-done.own_up.own_down, ...), custom_call_target="tpu_custom_call" | custom-call | tf_op jit(solution)/shard_map/hidden_layer/pallas_call | solution.py:356
  165.2 10.8 %hidden_layer.5 = (bf16[688,1024]{1,0:T(8,128)(2,1)S(1)}, bf16[688,1024]{1,0:T(8,128)(2,1)S(1)}, bf16[688,1024]{1,0:T(8,128)(2,1)S(1)}) custom-call(bf16[688,1024]{1,0:T(8,128)(2,1)S(1)} %pad_maximum_fusion.17.rows_ref, bf16[1024,1024]{1,0:T(8,128)(2,1)} %all-gather.13.cloned.1.call-done.own_up.own_down, ...), custom_call_target="tpu_custom_call" | custom-call | tf_op jit(solution)/shard_map/hidden_layer/pallas_call | solution.py:356
  185.4 16.6 %collective-permute-done.16 = bf16[344,1024]{1,0:T(8,128)(2,1)} collective-permute-done((bf16[344,1024]{1,0:T(8,128)(2,1)}, bf16[344,1024]{1,0:T(8,128)(2,1)}, u32[]{:S(2)}, u32[]{:S(2)}) %collective-permute-start.16) | collective-permute-done | bytes 704544 | tf_op jit(solution)/shard_map/ppermute | solution.py:46
  210.4 23.9 %all-gather.19.cloned.1.call-done = bf16[1024,512]{0,1:T(8,128)(2,1)} async-done(((bf16[256,512]{0,1:T(8,128)(2,1)}), bf16[1024,512]{0,1:T(8,128)(2,1)}) %all-gather.19.cloned.1.call-update) | async-done | bytes 1048592 | tf_op jit(solution)/shard_map/all_gather | solution.py:638
  253.4 10.7 %attend.6 = (bf16[688,256]{1,0:T(8,128)(2,1)S(1)}, f32[688,256]{1,0:T(8,128)S(1)}) custom-call(bf16[688,768]{1,0:T(8,128)(2,1)S(1)} %fusion.103.q_ref.kf_ref.vf_ref, bf16[688,768]{1,0:T(8,128)(2,1)S(1)} %fusion.100.kn_ref.vn_ref.q_ref, bf16[688,768]{1,0:T(8,128)(2,1)S(1)} %fusion.103.q_ref.kf_ref.vf_ref, bf16[688,768]{1,0:T(8,128)(2,1)S(1)} %fusion.100.kn_ref.vn_ref.q_ref, ...), custom_call_target="tpu_custom_call" | custom-call | tf_op jit(solution)/shard_map/attend/pallas_call | solution.py:165
  265.0 4.9 collective-permute-done.20
  275.3 3.5 collective-permute-start.23
  280.1 10.9 %attend.7 = (bf16[688,256]{1,0:T(8,128)(2,1)S(1)}, f32[688,256]{1,0:T(8,128)S(1)}) custom-call(bf16[688,768]{1,0:T(8,128)(2,1)S(1)} %fusion.100.kn_ref.vn_ref.q_ref, bf16[688,768]{1,0:T(8,128)(2,1)S(1)} %fusion.100.kn_ref.vn_ref.q_ref, bf16[688,768]{1,0:T(8,128)(2,1)S(1)} %copy-done.1, bf16[688,768]{1,0:T(8,128)(2,1)S(1)} %fusion.100.kn_ref.vn_ref.q_ref, ...), custom_call_target="tpu_custom_call" | custom-call | tf_op jit(solution)/shard_map/attend/pallas_call | solution.py:165
  291.0 7.7 collective-permute-done.23
  314.0 10.6 %hidden_layer.6 = (bf16[688,1024]{1,0:T(8,128)(2,1)S(1)}, bf16[688,1024]{1,0:T(8,128)(2,1)S(1)}, bf16[688,1024]{1,0:T(8,128)(2,1)S(1)}) custom-call(bf16[688,1024]{1,0:T(8,128)(2,1)S(1)} %copy-done.3, bf16[1024,1024]{1,0:T(8,128)(2,1)} %all-gather.21.cloned.1.call-done.own_up.own_down, bf16[1024,1024]{1,0:T(8,128)(2,1)} %all-gather.21.cloned.1.call-done.own_up.own_down, ...), custom_call_target="tpu_custom_call" | custom-call | tf_op jit(solution)/shard_map/hidden_layer/pallas_call | solution.py:356
  330.5 11.0 %hidden_layer.7 = (bf16[688,1024]{1,0:T(8,128)(2,1)S(1)}, bf16[688,1024]{1,0:T(8,128)(2,1)S(1)}, bf16[688,1024]{1,0:T(8,128)(2,1)S(1)}) custom-call(bf16[688,1024]{1,0:T(8,128)(2,1)S(1)} %pad_maximum_fusion.22.rows_ref, bf16[1024,1024]{1,0:T(8,128)(2,1)} %all-gather.21.cloned.1.call-done.own_up.own_down, ...), custom_call_target="tpu_custom_call" | custom-call | tf_op jit(solution)/shard_map/hidden_layer/pallas_call | solution.py:356
  347.1 15.0 %collective-permute-done.40 = bf16[344,1024]{1,0:T(8,128)(2,1)S(1)} collective-permute-done((bf16[344,1024]{1,0:T(8,128)(2,1)S(1)}, bf16[344,1024]{1,0:T(8,128)(2,1)S(1)}, u32[]{:S(2)}, u32[]{:S(2)}) %collective-permute-start.40) | collective-permute-done | bytes 704544 | tf_op jit(solution)/shard_map/ppermute | solution.py:46
  367.5 8.7 hidden_back.4
  376.3 6.5 collective-permute-done.25
  390.7 8.8 hidden_back.5
  404.5 6.3 fusion.61
  410.9 9.5 collective-permute-done.33
  427.8 6.2 fusion.56
  434.8 8.5 collective-permute-done.34
  453.9 26.8 %attend_back.2 = (bf16[1376,768]{1,0:T(8,128)(2,1)}, f32[8,256]{1,0:T(8,128)}) custom-call(bf16[1376,768]{1,0:T(8,128)(2,1)} %pad_maximum_fusion.5.q_ref.k_ref.v_ref, bf16[1376,768]{1,0:T(8,128)(2,1)} %pad_maximum_fusion.5.q_ref.k_ref.v_ref, bf16[1376,768]{1,0:T(8,128)(2,1)} %pad_maximum_fusion.5.q_ref.k_ref.v_ref, ...), custom_call_target="tpu_custom_call" | custom-call | tf_op jit(solution)/shard_map/attend_back/pallas_call | solution.py:239
  480.7 5.6 collective-permute-done.37
  486.3 3.3 convolution_convert_fusion.5
  513.4 3.2 collective-permute-start.44
  517.0 18.9 %collective-permute-done.44 = bf16[172,1024]{1,0:T(8,128)(2,1)} collective-permute-done((bf16[172,1024]{1,0:T(8,128)(2,1)S(1)}, bf16[172,1024]{1,0:T(8,128)(2,1)}, u32[]{:S(2)}, u32[]{:S(2)}) %collective-permute-start.44) | collective-permute-done | bytes 352288 | tf_op jit(solution)/shard_map/ppermute | solution.py:37
  544.8 8.7 hidden_back.6
  553.5 7.2 collective-permute-done.45
  563.0 8.7 hidden_back.7
  576.7 4.9 fusion.51
  581.6 11.7 %collective-permute-done.50 = bf16[344,1024]{1,0:T(8,128)(2,1)} collective-permute-done((bf16[344,1024]{1,0:T(8,128)(2,1)}, bf16[344,1024]{1,0:T(8,128)(2,1)}, u32[]{:S(2)}, u32[]{:S(2)}) %collective-permute-start.50) | collective-permute-done | bytes 704544 | tf_op jit(solution)/shard_map/ppermute | solution.py:46
  600.3 3.2 multiply_reduce_fusion.6
  607.7 7.2 fusion.46
  617.7 6.5 collective-permute-done.51
  627.4 3.7 collective-permute-start.53
  634.4 8.9 collective-permute-done.53
  655.4 26.6 %attend_back.3 = (bf16[1376,768]{1,0:T(8,128)(2,1)}, f32[8,256]{1,0:T(8,128)}) custom-call(bf16[1376,768]{1,0:T(8,128)(2,1)} %pad_maximum_fusion.6.q_ref.k_ref.v_ref, bf16[1376,768]{1,0:T(8,128)(2,1)} %pad_maximum_fusion.6.q_ref.k_ref.v_ref, bf16[1376,768]{1,0:T(8,128)(2,1)} %pad_maximum_fusion.6.q_ref.k_ref.v_ref, ...), custom_call_target="tpu_custom_call" | custom-call | tf_op jit(solution)/shard_map/attend_back/pallas_call | solution.py:239
  685.8 5.3 convolution_convert_fusion
  700.2 6.6 collective-permute-start.62
  719.4 23.2 %collective-permute-start.68 = (bf16[344,1024]{1,0:T(8,128)(2,1)}, bf16[344,1024]{1,0:T(8,128)(2,1)S(1)}, u32[]{:S(2)}, u32[]{:S(2)}) collective-permute-start(bf16[344,1024]{1,0:T(8,128)(2,1)} %add_convert_fusion.4), channel_id=1, source_target_pairs={{2,0},{0,2},{3,1},{1,3},{6,4},{4,6},{7,5},{5,7},{10,8},{8,10},{11,... | collective-permute-start | bytes 2113544 | tf_op jit(solution)/shard_map/ppermute | solution.py:46
  747.7 4.0 reduce-scatter.11.cloned.1.call-done
  761.6 8.9 collective-permute-done.64
  791.4 9.6 collective-permute-done.65
  801.0 10.2 collective-permute-done.66
  818.1 3.4 collective-permute-done.69
  822.1 13.0 %collective-permute-start.70 = (f32[768,512]{1,0:T(8,128)S(1)}, f32[768,512]{1,0:T(8,128)}, u32[]{:S(2)}, u32[]{:S(2)}) collective-permute-start(f32[768,512]{1,0:T(8,128)S(1)} %select_add_fusion), channel_id=1, source_target_pairs={{2,0},{0,2},{3,1},{1,3},{6,4},{4,6},{7,5},{5,7},{10,8},{8,10},{11,... | collective-permute-start | bytes 4718600 | tf_op jit(solution)/shard_map/ppermute | solution.py:46
  835.8 4.0 collective-permute-done.71
  840.8 3.7 collective-permute-done.72
  846.3 24.9 %collective-permute-done.74 = f32[16,1024]{1,0:T(8,128)S(1)} collective-permute-done((f32[16,1024]{1,0:T(8,128)S(1)}, f32[16,1024]{1,0:T(8,128)S(1)}, u32[]{:S(2)}, u32[]{:S(2)}) %collective-permute-start.74) | collective-permute-done | bytes 65568 | tf_op jit(solution)/shard_map/ppermute | solution.py:437
  871.4 5.3 collective-permute-done.75
  891.4 5.7 collective-permute-start.78
  900.7 73.5 %newton_schulz.1 = bf16[1024,1024]{1,0:T(8,128)(2,1)} custom-call(f32[512,512]{1,0:T(8,128)} %slice.802.first_ref, f32[512,512]{1,0:T(8,128)} %pad_maximum_fusion.27.side_ref, f32[512,512]{1,0:T(8,128)} %slice.805.last_ref, f32[1024,1024]{1,0:T(8,128)} %pad_maximum_fusion.start_ref), custom_call_target="tpu_custom_call" | custom-call | tf_op jit(solution)/shard_map/newton_schulz/pallas_call | solution.py:557
  976.3 3.5 slice_bitcast_fusion.10
  1000.8 3.2 collective-permute-start.86
  1007.0 13.9 %collective-permute-done.85 = bf16[256,512]{1,0:T(8,128)(2,1)} collective-permute-done((bf16[256,512]{1,0:T(8,128)(2,1)}, bf16[256,512]{1,0:T(8,128)(2,1)}, u32[]{:S(2)}, u32[]{:S(2)}) %collective-permute-start.85) | collective-permute-done | bytes 262176 | tf_op jit(solution)/shard_map/ppermute | solution.py:720
  1020.9 5.8 collective-permute-done.86
  1026.7 5.2 collective-permute-done.87
  (1062 shorter events, 361.6 us)
Async XLA Ops:
  7.2 36.8 %all-gather.9.cloned.1.call-start = ((), (), s32[]{:S(2)}) async-start(), calls=%async_computation.4 | async-start | bytes 1310720 | tf_op jit(solution)/shard_map/all_gather | solution.py:638
  10.8 33.2 %collective-permute-start.3 = (bf16[256,512]{0,1:T(8,128)(2,1)}, bf16[256,512]{0,1:T(8,128)(2,1)}, u32[]{:S(2)}, u32[]{:S(2)}) collective-permute-start(bf16[256,512]{0,1:T(8,128)(2,1)} %pad_maximum_fusion.49), channel_id=1, source_target_pairs={{0,4},{4,0},{1,5},{5,1},{2,6},{6,2},{3,7},{7,3},{8,12},{12,8},{9,1... | collective-permute-start | bytes 786440 | tf_op jit(solution)/shard_map/ppermute | solution.py:37
  14.9 57.0 %all-gather.11.cloned.1.call-start = ((), (), s32[]{:S(2)}) async-start(), calls=%async_computation.5 | async-start | bytes 1310720 | tf_op jit(solution)/shard_map/all_gather | solution.py:638
  17.0 25.7 %collective-permute-start = (bf16[172,1024]{1,0:T(8,128)(2,1)}, bf16[172,1024]{1,0:T(8,128)(2,1)}, u32[]{:S(2)}, u32[]{:S(2)}) collective-permute-start(bf16[172,1024]{1,0:T(8,128)(2,1)} %fusion.135), channel_id=1, source_target_pairs={{0,4},{4,0},{1,5},{5,1},{2,6},{6,2},{3,7},{7,3},{8,12},{12,8},{9,1... | collective-permute-start | bytes 1056776 | tf_op jit(solution)/shard_map/ppermute | solution.py:37
  17.0 28.9 %collective-permute-start.4 = (f32[2,2,384]{2,1,0:T(2,128)S(1)}, f32[2,2,384]{2,1,0:T(2,128)S(1)}, u32[]{:S(2)}, u32[]{:S(2)}) collective-permute-start(f32[2,2,384]{2,1,0:T(2,128)S(1)} %copy-done.257), channel_id=1, source_target_pairs={{0,4},{4,0},{1,5},{5,1},{2,6},{6,2},{3,7},{7,3},{8,12},{12,8},{9,1... | collective-permute-start | bytes 18440 | tf_op jit(solution)/shard_map/ppermute | solution.py:37
  44.0 101.5 %all-gather.13.cloned.1.call-start = ((), (), s32[]{:S(2)}) async-start(), calls=%async_computation.6 | async-start | bytes 2621440 | tf_op jit(solution)/shard_map/all_gather | solution.py:638
  45.9 27.3 %collective-permute-start.2 = (bf16[344,1024]{1,0:T(8,128)(2,1)}, bf16[344,1024]{1,0:T(8,128)(2,1)}, u32[]{:S(2)}, u32[]{:S(2)}) collective-permute-start(bf16[344,1024]{1,0:T(8,128)(2,1)} %add_convert_fusion.15), channel_id=1, source_target_pairs={{0,1},{1,0},{2,3},{3,2},{4,5},{5,4},{6,7},{7,6},{8,9},{9,8},{10,11... | collective-permute-start | bytes 2113544 | tf_op jit(solution)/shard_map/ppermute | solution.py:41
  46.1 30.0 %collective-permute-start.1 = (bf16[344,1024]{1,0:T(8,128)(2,1)}, bf16[344,1024]{1,0:T(8,128)(2,1)}, u32[]{:S(2)}, u32[]{:S(2)}) collective-permute-start(bf16[344,1024]{1,0:T(8,128)(2,1)} %add_convert_fusion.15), channel_id=1, source_target_pairs={{2,0},{0,2},{3,1},{1,3},{6,4},{4,6},{7,5},{5,7},{10,8},{8,10},{11,... | collective-permute-start | bytes 2113544 | tf_op jit(solution)/shard_map/ppermute | solution.py:46
  48.1 98.6 %all-gather.15.cloned.1.call-start = ((), (), s32[]{:S(2)}) async-start(), calls=%async_computation.7 | async-start | bytes 2621440 | tf_op jit(solution)/shard_map/all_gather | solution.py:638
  78.3 26.8 %collective-permute-start.6 = (bf16[256,1024]{1,0:T(8,128)(2,1)}, bf16[256,1024]{1,0:T(8,128)(2,1)}, u32[]{:S(2)}, u32[]{:S(2)}) collective-permute-start(bf16[256,1024]{1,0:T(8,128)(2,1)} %pad_maximum_fusion.39), channel_id=1, source_target_pairs={{0,4},{4,0},{1,5},{5,1},{2,6},{6,2},{3,7},{7,3},{8,12},{12,8},{9,1... | collective-permute-start | bytes 1572872 | tf_op jit(solution)/shard_map/ppermute | solution.py:37
  110.0 23.8 %collective-permute-start.8 = (bf16[344,1024]{1,0:T(8,128)(2,1)}, bf16[344,1024]{1,0:T(8,128)(2,1)}, u32[]{:S(2)}, u32[]{:S(2)}) collective-permute-start(bf16[344,1024]{1,0:T(8,128)(2,1)} %add_convert_fusion.14), channel_id=1, source_target_pairs={{2,0},{0,2},{3,1},{1,3},{6,4},{4,6},{7,5},{5,7},{10,8},{8,10},{11,... | collective-permute-start | bytes 2113544 | tf_op jit(solution)/shard_map/ppermute | solution.py:46
  110.5 21.3 %collective-permute-start.9 = (bf16[256,512]{0,1:T(8,128)(2,1)}, bf16[256,512]{0,1:T(8,128)(2,1)}, u32[]{:S(2)}, u32[]{:S(2)}) collective-permute-start(bf16[256,512]{0,1:T(8,128)(2,1)} %pad_maximum_fusion.50), channel_id=1, source_target_pairs={{0,4},{4,0},{1,5},{5,1},{2,6},{6,2},{3,7},{7,3},{8,12},{12,8},{9,1... | collective-permute-start | bytes 786440 | tf_op jit(solution)/shard_map/ppermute | solution.py:37
  113.9 94.4 %all-gather.17.cloned.1.call-start = ((), (), s32[]{:S(2)}) async-start(), calls=%async_computation.8 | async-start | bytes 1310720 | tf_op jit(solution)/shard_map/all_gather | solution.py:638
  141.2 19.4 %collective-permute-start.11 = (bf16[344,1024]{1,0:T(8,128)(2,1)}, bf16[344,1024]{1,0:T(8,128)(2,1)}, u32[]{:S(2)}, u32[]{:S(2)}) collective-permute-start(bf16[344,1024]{1,0:T(8,128)(2,1)} %add_convert_fusion.13), channel_id=1, source_target_pairs={{2,0},{0,2},{3,1},{1,3},{6,4},{4,6},{7,5},{5,7},{10,8},{8,10},{11,... | collective-permute-start | bytes 2113544 | tf_op jit(solution)/shard_map/ppermute | solution.py:46
  179.3 54.9 %all-gather.19.cloned.1.call-start = ((), (), s32[]{:S(2)}) async-start(), calls=%async_computation.9 | async-start | bytes 1310720 | tf_op jit(solution)/shard_map/all_gather | solution.py:638
  183.9 18.1 %collective-permute-start.16 = (bf16[344,1024]{1,0:T(8,128)(2,1)}, bf16[344,1024]{1,0:T(8,128)(2,1)}, u32[]{:S(2)}, u32[]{:S(2)}) collective-permute-start(bf16[344,1024]{1,0:T(8,128)(2,1)} %add_convert_fusion.12), channel_id=1, source_target_pairs={{2,0},{0,2},{3,1},{1,3},{6,4},{4,6},{7,5},{5,7},{10,8},{8,10},{11,... | collective-permute-start | bytes 2113544 | tf_op jit(solution)/shard_map/ppermute | solution.py:46
  185.4 127.3 %all-gather.21.cloned.1.call-start = ((), (), s32[]{:S(2)}) async-start(), calls=%async_computation.10 | async-start | bytes 2621440 | tf_op jit(solution)/shard_map/all_gather | solution.py:638
  205.8 29.7 %collective-permute-start.18 = (bf16[344,1024]{1,0:T(8,128)(2,1)}, bf16[344,1024]{1,0:T(8,128)(2,1)}, u32[]{:S(2)}, u32[]{:S(2)}) collective-permute-start(bf16[344,1024]{1,0:T(8,128)(2,1)} %add_convert_fusion.11), channel_id=1, source_target_pairs={{0,1},{1,0},{2,3},{3,2},{4,5},{5,4},{6,7},{7,6},{8,9},{9,8},{10,11... | collective-permute-start | bytes 2113544 | tf_op jit(solution)/shard_map/ppermute | solution.py:41
  205.8 33.2 %collective-permute-start.17 = (bf16[344,1024]{1,0:T(8,128)(2,1)}, bf16[344,1024]{1,0:T(8,128)(2,1)}, u32[]{:S(2)}, u32[]{:S(2)}) collective-permute-start(bf16[344,1024]{1,0:T(8,128)(2,1)} %add_convert_fusion.11), channel_id=1, source_target_pairs={{2,0},{0,2},{3,1},{1,3},{6,4},{4,6},{7,5},{5,7},{10,8},{8,10},{11,... | collective-permute-start | bytes 2113544 | tf_op jit(solution)/shard_map/ppermute | solution.py:46
  239.0 73.7 %all-gather.23.cloned.1.call-start = ((), (), s32[]{:S(2)}) async-start(), calls=%async_computation.11 | async-start | bytes 2621440 | tf_op jit(solution)/shard_map/all_gather | solution.py:638
  243.4 26.6 %collective-permute-start.20 = (bf16[256,1024]{1,0:T(8,128)(2,1)S(1)}, bf16[256,1024]{1,0:T(8,128)(2,1)}, u32[]{:S(2)}, u32[]{:S(2)}) collective-permute-start(bf16[256,1024]{1,0:T(8,128)(2,1)S(1)} %copy-done.126), channel_id=1, source_target_pairs={{0,4},{4,0},{1,5},{5,1},{2,6},{6,2},{3,7},{7,3},{8,12},{12,8},{9,1... | collective-permute-start | bytes 1572872 | tf_op jit(solution)/shard_map/ppermute | solution.py:37
  274.9 25.9 %collective-permute-start.22 = (bf16[344,1024]{1,0:T(8,128)(2,1)}, bf16[344,1024]{1,0:T(8,128)(2,1)}, u32[]{:S(2)}, u32[]{:S(2)}) collective-permute-start(bf16[344,1024]{1,0:T(8,128)(2,1)} %add_convert_fusion.10), channel_id=1, source_target_pairs={{2,0},{0,2},{3,1},{1,3},{6,4},{4,6},{7,5},{5,7},{10,8},{8,10},{11,... | collective-permute-start | bytes 2113544 | tf_op jit(solution)/shard_map/ppermute | solution.py:46
  275.3 23.4 %collective-permute-start.23 = (bf16[172,1024]{1,0:T(8,128)(2,1)}, bf16[172,1024]{1,0:T(8,128)(2,1)}, u32[]{:S(2)}, u32[]{:S(2)}) collective-permute-start(bf16[172,1024]{1,0:T(8,128)(2,1)} %fusion.136), channel_id=1, source_target_pairs={{0,4},{4,0},{1,5},{5,1},{2,6},{6,2},{3,7},{7,3},{8,12},{12,8},{9,1... | collective-permute-start | bytes 1056776 | tf_op jit(solution)/shard_map/ppermute | solution.py:37
  278.8 315.9 %reduce-scatter.5.cloned.1.call-start = ((), (), s32[]{:S(2)}) async-start(), calls=%async_computation.12 | async-start | bytes 7864320 | tf_op jit(solution)/shard_map/reduce_scatter | solution.py:641
  307.3 18.8 %collective-permute-start.30 = (bf16[344,1024]{1,0:T(8,128)(2,1)}, bf16[344,1024]{1,0:T(8,128)(2,1)}, u32[]{:S(2)}, u32[]{:S(2)}) collective-permute-start(bf16[344,1024]{1,0:T(8,128)(2,1)} %add_convert_fusion.9), channel_id=1, source_target_pairs={{2,0},{0,2},{3,1},{1,3},{6,4},{4,6},{7,5},{5,7},{10,8},{8,10},{11,... | collective-permute-start | bytes 2113544 | tf_op jit(solution)/shard_map/ppermute | solution.py:46
  344.1 18.0 %collective-permute-start.40 = (bf16[344,1024]{1,0:T(8,128)(2,1)S(1)}, bf16[344,1024]{1,0:T(8,128)(2,1)S(1)}, u32[]{:S(2)}, u32[]{:S(2)}) collective-permute-start(bf16[344,1024]{1,0:T(8,128)(2,1)S(1)} %add_convert_fusion.7), channel_id=1, source_target_pairs={{2,0},{0,2},{3,1},{1,3},{6,4},{4,6},{7,5},{5,7},{10,8},{8,10},{11,... | collective-permute-start | bytes 2113544 | tf_op jit(solution)/shard_map/ppermute | solution.py:46
  364.5 18.3 %collective-permute-start.25 = (bf16[344,1024]{1,0:T(8,128)(2,1)S(1)}, bf16[344,1024]{1,0:T(8,128)(2,1)}, u32[]{:S(2)}, u32[]{:S(2)}) collective-permute-start(bf16[344,1024]{1,0:T(8,128)(2,1)S(1)} %get-tuple-element.559), channel_id=1, source_target_pairs={{2,0},{0,2},{3,1},{1,3},{6,4},{4,6},{7,5},{5,7},{10,8},{8,10},{11,... | collective-permute-start | bytes 2113544 | tf_op jit(solution)/shard_map/ppermute | solution.py:46
  401.6 18.7 %collective-permute-start.28 = (bf16[344,1024]{1,0:T(8,128)(2,1)S(1)}, bf16[344,1024]{1,0:T(8,128)(2,1)S(1)}, u32[]{:S(2)}, u32[]{:S(2)}) collective-permute-start(bf16[344,1024]{1,0:T(8,128)(2,1)S(1)} %slice.639), channel_id=1, source_target_pairs={{0,1},{1,0},{2,3},{3,2},{4,5},{5,4},{6,7},{7,6},{8,9},{9,8},{10,11... | collective-permute-start | bytes 2113544 | tf_op jit(solution)/shard_map/ppermute | solution.py:41
  402.5 17.9 %collective-permute-start.33 = (bf16[344,1024]{1,0:T(8,128)(2,1)S(1)}, bf16[344,1024]{1,0:T(8,128)(2,1)S(1)}, u32[]{:S(2)}, u32[]{:S(2)}) collective-permute-start(bf16[344,1024]{1,0:T(8,128)(2,1)S(1)} %add_convert_fusion.8), channel_id=1, source_target_pairs={{2,0},{0,2},{3,1},{1,3},{6,4},{4,6},{7,5},{5,7},{10,8},{8,10},{11,... | collective-permute-start | bytes 2113544 | tf_op jit(solution)/shard_map/ppermute | solution.py:46
  425.9 17.5 %collective-permute-start.34 = (bf16[344,1024]{1,0:T(8,128)(2,1)S(1)}, bf16[344,1024]{1,0:T(8,128)(2,1)S(1)}, u32[]{:S(2)}, u32[]{:S(2)}) collective-permute-start(bf16[344,1024]{1,0:T(8,128)(2,1)S(1)} %multiply_convert_fusion.2), channel_id=1, source_target_pairs={{2,0},{0,2},{3,1},{1,3},{6,4},{4,6},{7,5},{5,7},{10,8},{8,10},{11,... | collective-permute-start | bytes 2113544 | tf_op jit(solution)/shard_map/ppermute | solution.py:46
  448.6 37.7 %collective-permute-start.37 = (bf16[256,1536]{1,0:T(8,128)(2,1)}, bf16[256,1536]{1,0:T(8,128)(2,1)S(1)}, u32[]{:S(2)}, u32[]{:S(2)}) collective-permute-start(bf16[256,1536]{1,0:T(8,128)(2,1)} %get-tuple-element.260), channel_id=1, source_target_pairs={{0,4},{4,0},{1,5},{5,1},{2,6},{6,2},{3,7},{7,3},{8,12},{12,8},{9,1... | collective-permute-start | bytes 2359304 | tf_op jit(solution)/shard_map/ppermute | solution.py:37
  508.1 139.0 %reduce-scatter.7.cloned.1.call-start = ((), (), s32[]{:S(2)}) async-start(), calls=%async_computation.13 | async-start | bytes 2621440 | tf_op jit(solution)/shard_map/reduce_scatter | solution.py:641
  512.1 25.9 %collective-permute-start.42 = (bf16[344,1024]{1,0:T(8,128)(2,1)S(1)}, bf16[344,1024]{1,0:T(8,128)(2,1)S(1)}, u32[]{:S(2)}, u32[]{:S(2)}) collective-permute-start(bf16[344,1024]{1,0:T(8,128)(2,1)S(1)} %copy-done.166), channel_id=1, source_target_pairs={{2,0},{0,2},{3,1},{1,3},{6,4},{4,6},{7,5},{5,7},{10,8},{8,10},{11,... | collective-permute-start | bytes 2113544 | tf_op jit(solution)/shard_map/ppermute | solution.py:46
  513.4 22.4 %collective-permute-start.44 = (bf16[172,1024]{1,0:T(8,128)(2,1)S(1)}, bf16[172,1024]{1,0:T(8,128)(2,1)}, u32[]{:S(2)}, u32[]{:S(2)}) collective-permute-start(bf16[172,1024]{1,0:T(8,128)(2,1)S(1)} %slice.920), channel_id=1, source_target_pairs={{0,4},{4,0},{1,5},{5,1},{2,6},{6,2},{3,7},{7,3},{8,12},{12,8},{9,1... | collective-permute-start | bytes 1056776 | tf_op jit(solution)/shard_map/ppermute | solution.py:37
  542.5 18.2 %collective-permute-start.45 = (bf16[344,1024]{1,0:T(8,128)(2,1)S(1)}, bf16[344,1024]{1,0:T(8,128)(2,1)S(1)}, u32[]{:S(2)}, u32[]{:S(2)}) collective-permute-start(bf16[344,1024]{1,0:T(8,128)(2,1)S(1)} %multiply_convert_fusion.1), channel_id=1, source_target_pairs={{2,0},{0,2},{3,1},{1,3},{6,4},{4,6},{7,5},{5,7},{10,8},{8,10},{11,... | collective-permute-start | bytes 2113544 | tf_op jit(solution)/shard_map/ppermute | solution.py:46
  575.1 18.2 %collective-permute-start.50 = (bf16[344,1024]{1,0:T(8,128)(2,1)}, bf16[344,1024]{1,0:T(8,128)(2,1)}, u32[]{:S(2)}, u32[]{:S(2)}) collective-permute-start(bf16[344,1024]{1,0:T(8,128)(2,1)} %add_convert_fusion.5), channel_id=1, source_target_pairs={{2,0},{0,2},{3,1},{1,3},{6,4},{4,6},{7,5},{5,7},{10,8},{8,10},{11,... | collective-permute-start | bytes 2113544 | tf_op jit(solution)/shard_map/ppermute | solution.py:46
  593.3 92.4 %reduce-scatter.9.cloned.1.call-start = ((), (), s32[]{:S(2)}) async-start(), calls=%async_computation.14 | async-start | bytes 2621440 | tf_op jit(solution)/shard_map/reduce_scatter | solution.py:641
  606.2 18.0 %collective-permute-start.51 = (bf16[344,1024]{1,0:T(8,128)(2,1)}, bf16[344,1024]{1,0:T(8,128)(2,1)}, u32[]{:S(2)}, u32[]{:S(2)}) collective-permute-start(bf16[344,1024]{1,0:T(8,128)(2,1)} %multiply_convert_fusion), channel_id=1, source_target_pairs={{2,0},{0,2},{3,1},{1,3},{6,4},{4,6},{7,5},{5,7},{10,8},{8,10},{11,... | collective-permute-start | bytes 2113544 | tf_op jit(solution)/shard_map/ppermute | solution.py:46
  624.2 127.4 %reduce-scatter.11.cloned.1.call-start = ((), (), s32[]{:S(2)}) async-start(), calls=%async_computation.15 | async-start | bytes 2621440 | tf_op jit(solution)/shard_map/reduce_scatter | solution.py:641
  627.3 16.9 %collective-permute-start.54 = (bf16[344,1024]{1,0:T(8,128)(2,1)}, bf16[344,1024]{1,0:T(8,128)(2,1)S(1)}, u32[]{:S(2)}, u32[]{:S(2)}) collective-permute-start(bf16[344,1024]{1,0:T(8,128)(2,1)} %collective-permute-done.51), channel_id=1, source_target_pairs={{0,1},{1,0},{2,3},{3,2},{4,5},{5,4},{6,7},{7,6},{8,9},{9,8},{10,11... | collective-permute-start | bytes 2113544 | tf_op jit(solution)/shard_map/ppermute | solution.py:41
  632.2 52.7 %collective-permute-start.58 = (bf16[256,1024]{1,0:T(8,128)(2,1)S(1)}, bf16[256,1024]{1,0:T(8,128)(2,1)}, u32[]{:S(2)}, u32[]{:S(2)}) collective-permute-start(bf16[256,1024]{1,0:T(8,128)(2,1)S(1)} %pad_maximum_fusion.44), channel_id=1, source_target_pairs={{0,4},{1,5},{2,6},{3,7},{8,12},{9,13},{10,14},{11,15},{16,20},{17,... | collective-permute-start | bytes 1572872 | tf_op jit(solution)/shard_map/ppermute | solution.py:831
  648.3 36.6 %collective-permute-start.59 = (bf16[256,1024]{1,0:T(8,128)(2,1)S(1)}, bf16[256,1024]{1,0:T(8,128)(2,1)S(1)}, u32[]{:S(2)}, u32[]{:S(2)}) collective-permute-start(bf16[256,1024]{1,0:T(8,128)(2,1)S(1)} %pad_maximum_fusion.45), channel_id=1, source_target_pairs={{4,0},{5,1},{6,2},{7,3},{12,8},{13,9},{14,10},{15,11},{20,16},{21,... | collective-permute-start | bytes 1572872 | tf_op jit(solution)/shard_map/ppermute | solution.py:831
  651.9 33.0 %collective-permute-start.55 = (bf16[256,1024]{1,0:T(8,128)(2,1)S(1)}, bf16[256,1024]{1,0:T(8,128)(2,1)S(1)}, u32[]{:S(2)}, u32[]{:S(2)}) collective-permute-start(bf16[256,1024]{1,0:T(8,128)(2,1)S(1)} %get-tuple-element.548), channel_id=1, source_target_pairs={{0,8},{8,0},{16,24},{24,16},{1,9},{9,1},{17,25},{25,17},{2,10},{10... | collective-permute-start | bytes 1572872 | tf_op jit(solution)/shard_map/ppermute | solution.py:635
  653.3 32.4 %collective-permute-start.56 = (bf16[256,1024]{1,0:T(8,128)(2,1)S(1)}, bf16[256,1024]{1,0:T(8,128)(2,1)}, u32[]{:S(2)}, u32[]{:S(2)}) collective-permute-start(bf16[256,1024]{1,0:T(8,128)(2,1)S(1)} %get-tuple-element.547), channel_id=1, source_target_pairs={{0,16},{8,24},{16,0},{24,8},{1,17},{9,25},{17,1},{25,9},{2,18},{10... | collective-permute-start | bytes 1572872 | tf_op jit(solution)/shard_map/ppermute | solution.py:635
  654.2 31.5 %collective-permute-start.57 = (bf16[256,1024]{1,0:T(8,128)(2,1)S(1)}, bf16[256,1024]{1,0:T(8,128)(2,1)}, u32[]{:S(2)}, u32[]{:S(2)}) collective-permute-start(bf16[256,1024]{1,0:T(8,128)(2,1)S(1)} %get-tuple-element.546), channel_id=1, source_target_pairs={{0,24},{8,16},{16,8},{24,0},{1,25},{9,17},{17,9},{25,1},{2,26},{10... | collective-permute-start | bytes 1572872 | tf_op jit(solution)/shard_map/ppermute | solution.py:635
  700.2 42.6 %collective-permute-start.62 = (bf16[256,1024]{1,0:T(8,128)(2,1)}, bf16[256,1024]{1,0:T(8,128)(2,1)}, u32[]{:S(2)}, u32[]{:S(2)}) collective-permute-start(bf16[256,1024]{1,0:T(8,128)(2,1)} %pad_maximum_fusion.46), channel_id=1, source_target_pairs={{0,4},{1,5},{2,6},{3,7},{8,12},{9,13},{10,14},{11,15},{16,20},{17,... | collective-permute-start | bytes 1572872 | tf_op jit(solution)/shard_map/ppermute | solution.py:831
  715.4 27.1 %collective-permute-start.61 = (bf16[344,1024]{1,0:T(8,128)(2,1)S(1)}, bf16[344,1024]{1,0:T(8,128)(2,1)S(1)}, u32[]{:S(2)}, u32[]{:S(2)}) collective-permute-start(bf16[344,1024]{1,0:T(8,128)(2,1)S(1)} %slice.791), channel_id=1, source_target_pairs={{0,1},{1,0},{2,3},{3,2},{4,5},{5,4},{6,7},{7,6},{8,9},{9,8},{10,11... | collective-permute-start | bytes 2113544 | tf_op jit(solution)/shard_map/ppermute | solution.py:41
  716.5 26.3 %collective-permute-start.63 = (bf16[256,1024]{1,0:T(8,128)(2,1)S(1)}, bf16[256,1024]{1,0:T(8,128)(2,1)S(1)}, u32[]{:S(2)}, u32[]{:S(2)}) collective-permute-start(bf16[256,1024]{1,0:T(8,128)(2,1)S(1)} %pad_maximum_fusion.47), channel_id=1, source_target_pairs={{4,0},{5,1},{6,2},{7,3},{12,8},{13,9},{14,10},{15,11},{20,16},{21,... | collective-permute-start | bytes 1572872 | tf_op jit(solution)/shard_map/ppermute | solution.py:831
  719.4 39.5 %collective-permute-start.68 = (bf16[344,1024]{1,0:T(8,128)(2,1)}, bf16[344,1024]{1,0:T(8,128)(2,1)S(1)}, u32[]{:S(2)}, u32[]{:S(2)}) collective-permute-start(bf16[344,1024]{1,0:T(8,128)(2,1)} %add_convert_fusion.4), channel_id=1, source_target_pairs={{2,0},{0,2},{3,1},{1,3},{6,4},{4,6},{7,5},{5,7},{10,8},{8,10},{11,... | collective-permute-start | bytes 2113544 | tf_op jit(solution)/shard_map/ppermute | solution.py:46
  787.5 23.7 %collective-permute-start.66 = (bf16[256,1024]{1,0:T(8,128)(2,1)S(1)}, bf16[256,1024]{1,0:T(8,128)(2,1)S(1)}, u32[]{:S(2)}, u32[]{:S(2)}) collective-permute-start(bf16[256,1024]{1,0:T(8,128)(2,1)S(1)} %get-tuple-element.535), channel_id=1, source_target_pairs={{0,16},{8,24},{16,0},{24,8},{1,17},{9,25},{17,1},{25,9},{2,18},{10... | collective-permute-start | bytes 1572872 | tf_op jit(solution)/shard_map/ppermute | solution.py:635
  788.1 23.1 %collective-permute-start.67 = (bf16[256,1024]{1,0:T(8,128)(2,1)S(1)}, bf16[256,1024]{1,0:T(8,128)(2,1)S(1)}, u32[]{:S(2)}, u32[]{:S(2)}) collective-permute-start(bf16[256,1024]{1,0:T(8,128)(2,1)S(1)} %get-tuple-element.534), channel_id=1, source_target_pairs={{0,24},{8,16},{16,8},{24,0},{1,25},{9,17},{17,9},{25,1},{2,26},{10... | collective-permute-start | bytes 1572872 | tf_op jit(solution)/shard_map/ppermute | solution.py:635
  822.1 54.7 %collective-permute-start.70 = (f32[768,512]{1,0:T(8,128)S(1)}, f32[768,512]{1,0:T(8,128)}, u32[]{:S(2)}, u32[]{:S(2)}) collective-permute-start(f32[768,512]{1,0:T(8,128)S(1)} %select_add_fusion), channel_id=1, source_target_pairs={{2,0},{0,2},{3,1},{1,3},{6,4},{4,6},{7,5},{5,7},{10,8},{8,10},{11,... | collective-permute-start | bytes 4718600 | tf_op jit(solution)/shard_map/ppermute | solution.py:46
  845.9 25.3 %collective-permute-start.74 = (f32[16,1024]{1,0:T(8,128)S(1)}, f32[16,1024]{1,0:T(8,128)S(1)}, u32[]{:S(2)}, u32[]{:S(2)}) collective-permute-start(f32[16,1024]{1,0:T(8,128)S(1)} %slice_add_fusion), channel_id=1, source_target_pairs={{0,2},{2,0},{1,3},{3,1},{4,6},{6,4},{5,7},{7,5},{8,10},{10,8},{9,1... | collective-permute-start | bytes 196616 | tf_op jit(solution)/shard_map/ppermute | solution.py:437
  846.3 25.0 %collective-permute-start.76 = (f32[2,2,96]{2,1,0:T(2,128)S(1)}, f32[2,2,96]{2,1,0:T(2,128)S(1)}, u32[]{:S(2)}, u32[]{:S(2)}) collective-permute-start(f32[2,2,96]{2,1,0:T(2,128)S(1)} %constant_dynamic-slice_fusion.2), channel_id=1, source_target_pairs={{0,4},{4,0},{1,5},{5,1},{2,6},{6,2},{3,7},{7,3},{8,12},{12,8},{9,1... | collective-permute-start | bytes 4616 | tf_op jit(solution)/shard_map/ppermute | solution.py:37
  889.7 86.5 %collective-permute-start.79 = (bf16[256,1536]{1,0:T(8,128)(2,1)S(1)}, bf16[256,1536]{1,0:T(8,128)(2,1)S(1)}, u32[]{:S(2)}, u32[]{:S(2)}) collective-permute-start(bf16[256,1536]{1,0:T(8,128)(2,1)S(1)} %pad_maximum_fusion.35), channel_id=1, source_target_pairs={{4,0},{5,1},{6,2},{7,3},{12,8},{13,9},{14,10},{15,11},{20,16},{21,... | collective-permute-start | bytes 2359304 | tf_op jit(solution)/shard_map/ppermute | solution.py:854
  891.4 84.8 %collective-permute-start.78 = (bf16[256,1536]{1,0:T(8,128)(2,1)S(1)}, bf16[256,1536]{1,0:T(8,128)(2,1)S(1)}, u32[]{:S(2)}, u32[]{:S(2)}) collective-permute-start(bf16[256,1536]{1,0:T(8,128)(2,1)S(1)} %pad_maximum_fusion.34), channel_id=1, source_target_pairs={{0,4},{1,5},{2,6},{3,7},{8,12},{9,13},{10,14},{11,15},{16,20},{17,... | collective-permute-start | bytes 2359304 | tf_op jit(solution)/shard_map/ppermute | solution.py:854
  900.7 75.5 %collective-permute-start.80 = (bf16[172,1024]{1,0:T(8,128)(2,1)S(1)}, bf16[172,1024]{1,0:T(8,128)(2,1)S(1)}, u32[]{:S(2)}, u32[]{:S(2)}) collective-permute-start(bf16[172,1024]{1,0:T(8,128)(2,1)S(1)} %slice.919), channel_id=1, source_target_pairs={{0,4},{4,0},{1,5},{5,1},{2,6},{6,2},{3,7},{7,3},{8,12},{12,8},{9,1... | collective-permute-start | bytes 1056776 | tf_op jit(solution)/shard_map/ppermute | solution.py:37
  979.8 21.0 %collective-permute-start.81 = (bf16[256,512]{1,0:T(8,128)(2,1)}, bf16[256,512]{1,0:T(8,128)(2,1)}, u32[]{:S(2)}, u32[]{:S(2)}) collective-permute-start(bf16[256,512]{1,0:T(8,128)(2,1)} %get-tuple-element.533), channel_id=1, source_target_pairs={{0,8},{8,0},{16,24},{24,16},{1,9},{9,1},{17,25},{25,17},{2,10},{10... | collective-permute-start | bytes 786440 | tf_op jit(solution)/shard_map/ppermute | solution.py:635
  980.4 23.6 %collective-permute-start.82 = (bf16[256,512]{1,0:T(8,128)(2,1)}, bf16[256,512]{1,0:T(8,128)(2,1)}, u32[]{:S(2)}, u32[]{:S(2)}) collective-permute-start(bf16[256,512]{1,0:T(8,128)(2,1)} %get-tuple-element.532), channel_id=1, source_target_pairs={{0,16},{8,24},{16,0},{24,8},{1,17},{9,25},{17,1},{25,9},{2,18},{10... | collective-permute-start | bytes 786440 | tf_op jit(solution)/shard_map/ppermute | solution.py:635
  981.9 23.9 %collective-permute-start.83 = (bf16[256,512]{1,0:T(8,128)(2,1)}, bf16[256,512]{1,0:T(8,128)(2,1)}, u32[]{:S(2)}, u32[]{:S(2)}) collective-permute-start(bf16[256,512]{1,0:T(8,128)(2,1)} %get-tuple-element.531), channel_id=1, source_target_pairs={{0,24},{8,16},{16,8},{24,0},{1,25},{9,17},{17,9},{25,1},{2,26},{10... | collective-permute-start | bytes 786440 | tf_op jit(solution)/shard_map/ppermute | solution.py:635
  983.3 23.7 %collective-permute-start.84 = (bf16[256,512]{1,0:T(8,128)(2,1)}, bf16[256,512]{1,0:T(8,128)(2,1)}, u32[]{:S(2)}, u32[]{:S(2)}) collective-permute-start(bf16[256,512]{1,0:T(8,128)(2,1)} %get-tuple-element.530), channel_id=1, source_target_pairs={{0,4},{4,0},{8,12},{12,8},{16,20},{20,16},{24,28},{28,24},{1,5},{5... | collective-permute-start | bytes 786440 | tf_op jit(solution)/shard_map/ppermute | solution.py:720
  986.2 34.7 %collective-permute-start.85 = (bf16[256,512]{1,0:T(8,128)(2,1)}, bf16[256,512]{1,0:T(8,128)(2,1)}, u32[]{:S(2)}, u32[]{:S(2)}) collective-permute-start(bf16[256,512]{1,0:T(8,128)(2,1)} %get-tuple-element.529), channel_id=1, source_target_pairs={{0,12},{4,8},{8,4},{12,0},{16,28},{20,24},{24,20},{28,16},{1,13},{... | collective-permute-start | bytes 786440 | tf_op jit(solution)/shard_map/ppermute | solution.py:720
  1000.8 25.9 %collective-permute-start.86 = (bf16[256,512]{1,0:T(8,128)(2,1)S(1)}, bf16[256,512]{1,0:T(8,128)(2,1)S(1)}, u32[]{:S(2)}, u32[]{:S(2)}) collective-permute-start(bf16[256,512]{1,0:T(8,128)(2,1)S(1)} %copy-done.194), channel_id=1, source_target_pairs={{0,20},{4,16},{8,28},{12,24},{16,4},{20,0},{24,12},{28,8},{1,21},{... | collective-permute-start | bytes 786440 | tf_op jit(solution)/shard_map/ppermute | solution.py:720
  1004.0 27.9 %collective-permute-start.87 = (bf16[256,512]{1,0:T(8,128)(2,1)S(1)}, bf16[256,512]{1,0:T(8,128)(2,1)S(1)}, u32[]{:S(2)}, u32[]{:S(2)}) collective-permute-start(bf16[256,512]{1,0:T(8,128)(2,1)S(1)} %copy-done.193), channel_id=1, source_target_pairs={{0,28},{4,24},{8,20},{12,16},{16,12},{20,8},{24,4},{28,0},{1,29},{... | collective-permute-start | bytes 786440 | tf_op jit(solution)/shard_map/ppermute | solution.py:720
  (320 other events, 3347.6 us)
Sparse Core Ops, SparseCore 0:
  15.0 25.7 all-gather.8
  44.2 27.6 all-gather.10
  74.3 35.3 all-gather.12
  114.0 32.6 all-gather.14
  179.4 26.5 all-gather.16
  207.7 26.5 all-gather.18
  239.1 35.3 all-gather.20
  278.9 32.7 all-gather.22
  508.2 69.5 reduce-scatter.4
  593.4 34.5 reduce-scatter.6
  631.3 41.1 reduce-scatter.8
  693.2 58.4 reduce-scatter.10

commit v2 on v1

--- a/solution.py
+++ b/solution.py
@@ -272,7 +272,9 @@
 
 def gelu_and_slope(values):
     size = jnp.abs(values)
-    inner = 1.0 / (1.0 + (0.3275911 * 0.5**0.5) * size)
+    below = 1.0 + (0.3275911 * 0.5**0.5) * size
+    inner = pl.reciprocal(below, approx=True)
+    inner = inner * (2.0 - below * inner)
     tail = 0.5 * 1.061405429
     for term in (-1.453152027, 1.421413741, -0.284496736, 0.254829592):
         tail = tail * inner + 0.5 * term
@@ -692,25 +694,23 @@
             at += width
         return items
 
+    def reordered(parts):
+        bit = 1
+        while bit < data_count:
+            swap = (data_index & bit) != 0
+            parts = [jnp.where(swap, parts[i ^ bit], part) for i, part in enumerate(parts)]
+            bit *= 2
+        return parts
+
     def to_owner(items):
-        stack = jnp.stack([rows for _, rows in sorted(items, key=lambda item: item[0])])
-        blocks = []
-        for offset in range(data_count):
-            block = lax.dynamic_index_in_dim(stack, data_index ^ offset, 0, keepdims=False)
-            blocks.append(dp_xor(block, offset) if offset else block)
-        return blocks
+        blocks = reordered([rows for _, rows in sorted(items, key=lambda item: item[0])])
+        return [dp_xor(block, offset) if offset else block for offset, block in enumerate(blocks)]
 
     def from_owner(matrix):
         blocks = jnp.split(matrix, data_count)
 
-        def gathered(parts):
-            return [
-                lax.dynamic_index_in_dim(jnp.stack(parts), data_index ^ owner, 0, keepdims=False)
-                for owner in range(data_count)
-            ]
-
         if not wide:
-            parts = gathered([dp_xor(b, i) if i else b for i, b in enumerate(blocks)])
+            parts = reordered([dp_xor(b, i) if i else b for i, b in enumerate(blocks)])
             return [parts[layer * KINDS : (layer + 1) * KINDS] for layer in range(layer_count)]
         far, near = [], []
         for offset, block in enumerate(blocks):
@@ -722,7 +722,7 @@
             near.append(
                 dp_xor(block[:, :pad_width], offset) if offset else block[:, :pad_width]
             )
-        near, far = gathered(near), gathered(far)
+        near, far = reordered(near), reordered(far)
         return [
             [jnp.where(half == layer, n, f) for n, f in zip(near, far)]
             for layer in range(layer_count)
@@ -781,7 +781,6 @@
                 heads_far, hidden_other, own_low[block_index + 1][0]
             )
             aside = half_swap(first_own)
-            first_own = data_gather(first_own)
         hidden_other = data_gather(hidden_other)
         sums, query_held = pin(far_sums(times_t(heads_far, w_out).astype(LOW)), query_near)
         back = to_pairs(sums)
@@ -790,7 +789,9 @@
         if last:
             other_cotangent = aside
         else:
-            first_other = data_gather(aside)
+            first_own, first_other = jnp.split(
+                data_gather(jnp.concatenate([first_own, aside], axis=1)), 2, axis=1
+            )
         total = chip_sum(times_t(heads_near, w_out).astype(LOW))
         branch_one = arrived(total, back) + row_set[2]
         middle = residual + row_set[3] * branch_one

time: 1060 us -> 1040 us (0.981)
  waiting for transfers between devices: 335 us -> 320 us
    all_gather x8 -> x7, waiting for transfers between devices: 48.8 us -> 38.5 us  [data_gather(): return lax.all_gather(piece, 'dp', axis=0, tiled=True)]
    unnamed x574 -> x614, local copies, waits for them, and re-layouts: 56.4 us -> 62.8 us
  transfers between devices with their start and end apart: 100 -> 99, of which waited for: 51 -> 48; matrix products, arithmetic and copies ran while one was open for 19% -> 18% of each run, Pallas kernels for 21% -> 21%
where the time goes in v2:
time: 1040 us; the launch traced here: 1030 us
  waiting for transfers between devices  320 us (31%)
  Pallas kernels  249 us (24%)
  starting transfers between devices  137 us (13%)
  other arithmetic  122 us (12%)
  local copies, waits for them, and re-layouts  114 us (11%)
  matrix products  67 us (6%)
  between operations  19.7 us (2%)
    ppermute x17, waiting for transfers between devices, pair_from(): lax.ppermute(values, 'pair', [((i + shift) % count, i) for i in range(cou...  89.1 us
    pallas_call x8, Pallas kernels, hidden_call(): pl.pallas_call(kernel, out_shape=tuple((shape for shape, _ in outs)), gri...  79.2 us
    pallas_call x1, Pallas kernels, orthogonalize(): pl.pallas_call(newton_schulz_kernel, out_shape=jax.ShapeDtypeStruct((size...  73.5 us
    ppermute x11, waiting for transfers between devices, half_swap(): return lax.ppermute(values, 'half', [(0, 1), (1, 0)])  68.4 us
    dot_general x25, matrix products, dot(): lax.dot_general(left, right, (dims, ((), ())), preferred_element_type=F32)  67 us
    unnamed x614, local copies, waits for them, and re-layouts  62.8 us
    ppermute x17, starting transfers between devices, pair_from(): lax.ppermute(values, 'pair', [((i + shift) % count, i) for i in range(cou...  53.8 us
    pallas_call x2, Pallas kernels, attend_back(): pl.pallas_call(attend_back_kernel, out_shape=(jax.ShapeDtypeStruct((rows,...  53.3 us
  transfers between devices with their start and end apart: 99, of which 48 were waited for; matrix products, arithmetic and copies ran while one was open for 18% of the time, Pallas kernels for 21%

profile of v2, /device:TPU:0, one launch (start us, length us, event | category | flops | bytes accessed | tf_op | source)
XLA Modules:
  0.0 1028.6 jit_solution(15864173114045692174)
XLA Ops:
  10.8 4.0 collective-permute-start.3
  26.3 16.4 %collective-permute-done = bf16[172,1024]{1,0:T(8,128)(2,1)} collective-permute-done((bf16[172,1024]{1,0:T(8,128)(2,1)}, bf16[172,1024]{1,0:T(8,128)(2,1)}, u32[]{:S(2)}, u32[]{:S(2)}) %collective-permute-start) | collective-permute-done | bytes 352288 | tf_op jit(solution)/shard_map/ppermute | solution.py:37
  47.2 24.6 %all-gather.10.cloned.1.call-done = bf16[1024,512]{0,1:T(8,128)(2,1)} async-done(((bf16[256,512]{0,1:T(8,128)(2,1)}), bf16[1024,512]{0,1:T(8,128)(2,1)}) %all-gather.10.cloned.1.call-update) | async-done | bytes 1048592 | tf_op jit(solution)/shard_map/all_gather | solution.py:640
  85.9 10.7 %attend.4 = (bf16[688,256]{1,0:T(8,128)(2,1)S(1)}, f32[688,256]{1,0:T(8,128)S(1)}) custom-call(bf16[688,768]{1,0:T(8,128)(2,1)S(1)} %fusion.97.q_ref.kf_ref.vf_ref, bf16[688,768]{1,0:T(8,128)(2,1)S(1)} %fusion.94.kn_ref.vn_ref.q_ref, bf16[688,768]{1,0:T(8,128)(2,1)S(1)} %fusion.97.q_ref.kf_ref.vf_ref, bf16[688,768]{1,0:T(8,128)(2,1)S(1)} %fusion.94.kn_ref.vn_ref.q_ref, ...), custom_call_target="tpu_custom_call" | custom-call | tf_op jit(solution)/shard_map/attend/pallas_call | solution.py:165
  97.5 7.1 collective-permute-done.6
  109.0 3.4 collective-permute-start.9
  112.9 10.7 %attend.5 = (bf16[688,256]{1,0:T(8,128)(2,1)S(1)}, f32[688,256]{1,0:T(8,128)S(1)}) custom-call(bf16[688,768]{1,0:T(8,128)(2,1)S(1)} %fusion.94.kn_ref.vn_ref.q_ref, bf16[688,768]{1,0:T(8,128)(2,1)S(1)} %fusion.94.kn_ref.vn_ref.q_ref, bf16[688,768]{1,0:T(8,128)(2,1)S(1)} %fusion.97.q_ref.kf_ref.vf_ref, bf16[688,768]{1,0:T(8,128)(2,1)S(1)} %fusion.94.kn_ref.vn_ref.q_ref, ...), custom_call_target="tpu_custom_call" | custom-call | tf_op jit(solution)/shard_map/attend/pallas_call | solution.py:165
  123.7 6.6 collective-permute-done.9
  142.0 4.7 all-gather.14.cloned.1.call-done.far_up.far_down
  146.7 10.9 %hidden_layer.4 = (bf16[688,1024]{1,0:T(8,128)(2,1)S(1)}, bf16[688,1024]{1,0:T(8,128)(2,1)S(1)}, bf16[688,1024]{1,0:T(8,128)(2,1)S(1)}) custom-call(bf16[688,1024]{1,0:T(8,128)(2,1)S(1)} %pad_maximum_fusion.14.rows_ref, bf16[1024,1024]{1,0:T(8,128)(2,1)} %all-gather.12.cloned.1.call-done.own_up.own_down, ...), custom_call_target="tpu_custom_call" | custom-call | tf_op jit(solution)/shard_map/hidden_layer/pallas_call | solution.py:358
  165.5 11.1 %hidden_layer.5 = (bf16[688,1024]{1,0:T(8,128)(2,1)S(1)}, bf16[688,1024]{1,0:T(8,128)(2,1)S(1)}, bf16[688,1024]{1,0:T(8,128)(2,1)S(1)}) custom-call(bf16[688,1024]{1,0:T(8,128)(2,1)S(1)} %pad_maximum_fusion.15.rows_ref, bf16[1024,1024]{1,0:T(8,128)(2,1)} %all-gather.12.cloned.1.call-done.own_up.own_down, ...), custom_call_target="tpu_custom_call" | custom-call | tf_op jit(solution)/shard_map/hidden_layer/pallas_call | solution.py:358
  186.1 16.6 %collective-permute-done.16 = bf16[344,1024]{1,0:T(8,128)(2,1)S(1)} collective-permute-done((bf16[344,1024]{1,0:T(8,128)(2,1)S(1)}, bf16[344,1024]{1,0:T(8,128)(2,1)S(1)}, u32[]{:S(2)}, u32[]{:S(2)}) %collective-permute-start.16) | collective-permute-done | bytes 704544 | tf_op jit(solution)/shard_map/ppermute | solution.py:46
  208.0 9.1 all-gather.16.cloned.1.call-done
  235.5 10.9 %attend.6 = (bf16[688,256]{1,0:T(8,128)(2,1)S(1)}, f32[688,256]{1,0:T(8,128)S(1)}) custom-call(bf16[688,768]{1,0:T(8,128)(2,1)S(1)} %fusion.103.q_ref.kf_ref.vf_ref, bf16[688,768]{1,0:T(8,128)(2,1)S(1)} %fusion.100.kn_ref.vn_ref.q_ref, bf16[688,768]{1,0:T(8,128)(2,1)S(1)} %fusion.103.q_ref.kf_ref.vf_ref, bf16[688,768]{1,0:T(8,128)(2,1)S(1)} %fusion.100.kn_ref.vn_ref.q_ref, ...), custom_call_target="tpu_custom_call" | custom-call | tf_op jit(solution)/shard_map/attend/pallas_call | solution.py:165
  247.4 7.1 collective-permute-done.20
  259.9 3.5 collective-permute-start.23
  264.7 10.7 %attend.7 = (bf16[688,256]{1,0:T(8,128)(2,1)S(1)}, f32[688,256]{1,0:T(8,128)S(1)}) custom-call(bf16[688,768]{1,0:T(8,128)(2,1)S(1)} %fusion.100.kn_ref.vn_ref.q_ref, bf16[688,768]{1,0:T(8,128)(2,1)S(1)} %fusion.100.kn_ref.vn_ref.q_ref, bf16[688,768]{1,0:T(8,128)(2,1)S(1)} %copy-done.1, bf16[688,768]{1,0:T(8,128)(2,1)S(1)} %fusion.100.kn_ref.vn_ref.q_ref, ...), custom_call_target="tpu_custom_call" | custom-call | tf_op jit(solution)/shard_map/attend/pallas_call | solution.py:165
  275.4 7.9 collective-permute-done.23
  298.9 10.9 %hidden_layer.6 = (bf16[688,1024]{1,0:T(8,128)(2,1)S(1)}, bf16[688,1024]{1,0:T(8,128)(2,1)S(1)}, bf16[688,1024]{1,0:T(8,128)(2,1)S(1)}) custom-call(bf16[688,1024]{1,0:T(8,128)(2,1)S(1)} %copy-done.3, bf16[1024,1024]{1,0:T(8,128)(2,1)} %all-gather.18.cloned.1.call-done.own_up.own_down, bf16[1024,1024]{1,0:T(8,128)(2,1)} %all-gather.18.cloned.1.call-done.own_up.own_down, ...), custom_call_target="tpu_custom_call" | custom-call | tf_op jit(solution)/shard_map/hidden_layer/pallas_call | solution.py:358
  314.8 11.4 %hidden_layer.7 = (bf16[688,1024]{1,0:T(8,128)(2,1)S(1)}, bf16[688,1024]{1,0:T(8,128)(2,1)S(1)}, bf16[688,1024]{1,0:T(8,128)(2,1)S(1)}) custom-call(bf16[688,1024]{1,0:T(8,128)(2,1)S(1)} %pad_maximum_fusion.20.rows_ref, bf16[1024,1024]{1,0:T(8,128)(2,1)} %all-gather.18.cloned.1.call-done.own_up.own_down, ...), custom_call_target="tpu_custom_call" | custom-call | tf_op jit(solution)/shard_map/hidden_layer/pallas_call | solution.py:358
  332.0 15.0 %collective-permute-done.40 = bf16[344,1024]{1,0:T(8,128)(2,1)S(1)} collective-permute-done((bf16[344,1024]{1,0:T(8,128)(2,1)S(1)}, bf16[344,1024]{1,0:T(8,128)(2,1)S(1)}, u32[]{:S(2)}, u32[]{:S(2)}) %collective-permute-start.40) | collective-permute-done | bytes 704544 | tf_op jit(solution)/shard_map/ppermute | solution.py:46
  352.5 8.7 hidden_back.4
  361.3 6.5 collective-permute-done.25
  375.7 8.8 hidden_back.5
  389.4 6.3 fusion.61
  395.8 9.6 collective-permute-done.33
  412.7 6.2 fusion.56
  419.8 8.6 collective-permute-done.34
  439.2 26.8 %attend_back.2 = (bf16[1376,768]{1,0:T(8,128)(2,1)}, f32[8,256]{1,0:T(8,128)}) custom-call(bf16[1376,768]{1,0:T(8,128)(2,1)} %pad_maximum_fusion.5.q_ref.k_ref.v_ref, bf16[1376,768]{1,0:T(8,128)(2,1)} %pad_maximum_fusion.5.q_ref.k_ref.v_ref, bf16[1376,768]{1,0:T(8,128)(2,1)} %pad_maximum_fusion.5.q_ref.k_ref.v_ref, ...), custom_call_target="tpu_custom_call" | custom-call | tf_op jit(solution)/shard_map/attend_back/pallas_call | solution.py:239
  465.9 5.2 collective-permute-done.37
  471.2 3.3 convolution_convert_fusion.5
  499.3 3.3 collective-permute-start.44
  502.9 17.9 %collective-permute-done.44 = bf16[172,1024]{1,0:T(8,128)(2,1)S(1)} collective-permute-done((bf16[172,1024]{1,0:T(8,128)(2,1)S(1)}, bf16[172,1024]{1,0:T(8,128)(2,1)S(1)}, u32[]{:S(2)}, u32[]{:S(2)}) %collective-permute-start.44) | collective-permute-done | bytes 352288 | tf_op jit(solution)/shard_map/ppermute | solution.py:37
  528.5 8.7 hidden_back.6
  537.2 7.2 collective-permute-done.45
  546.7 8.7 hidden_back.7
  560.4 4.8 fusion.51
  565.3 11.7 %collective-permute-done.50 = bf16[344,1024]{1,0:T(8,128)(2,1)} collective-permute-done((bf16[344,1024]{1,0:T(8,128)(2,1)}, bf16[344,1024]{1,0:T(8,128)(2,1)}, u32[]{:S(2)}, u32[]{:S(2)}) %collective-permute-start.50) | collective-permute-done | bytes 704544 | tf_op jit(solution)/shard_map/ppermute | solution.py:46
  590.8 6.3 fusion.46
  599.5 7.6 collective-permute-done.51
  610.5 3.6 collective-permute-start.53
  618.2 8.2 collective-permute-done.53
  637.8 26.6 %attend_back.3 = (bf16[1376,768]{1,0:T(8,128)(2,1)}, f32[8,256]{1,0:T(8,128)}) custom-call(bf16[1376,768]{1,0:T(8,128)(2,1)} %pad_maximum_fusion.6.q_ref.k_ref.v_ref, bf16[1376,768]{1,0:T(8,128)(2,1)} %pad_maximum_fusion.6.q_ref.k_ref.v_ref, bf16[1376,768]{1,0:T(8,128)(2,1)} %pad_maximum_fusion.6.q_ref.k_ref.v_ref, ...), custom_call_target="tpu_custom_call" | custom-call | tf_op jit(solution)/shard_map/attend_back/pallas_call | solution.py:239
  668.7 5.3 convolution_convert_fusion
  681.8 7.1 collective-permute-start.62
  702.7 23.4 %collective-permute-start.68 = (bf16[344,1024]{1,0:T(8,128)(2,1)}, bf16[344,1024]{1,0:T(8,128)(2,1)}, u32[]{:S(2)}, u32[]{:S(2)}) collective-permute-start(bf16[344,1024]{1,0:T(8,128)(2,1)} %add_convert_fusion.4), channel_id=1, source_target_pairs={{2,0},{0,2},{3,1},{1,3},{6,4},{4,6},{7,5},{5,7},{10,8},{8,10},{11,... | collective-permute-start | bytes 2113544 | tf_op jit(solution)/shard_map/ppermute | solution.py:46
  728.9 6.5 reduce-scatter.11.cloned.1.call-done
  745.7 19.9 %collective-permute-done.64 = bf16[256,1024]{1,0:T(8,128)(2,1)} collective-permute-done((bf16[256,1024]{1,0:T(8,128)(2,1)}, bf16[256,1024]{1,0:T(8,128)(2,1)}, u32[]{:S(2)}, u32[]{:S(2)}) %collective-permute-start.64) | collective-permute-done | bytes 524320 | tf_op jit(solution)/shard_map/ppermute | solution.py:832
  790.2 7.0 collective-permute-done.66
  803.7 3.4 collective-permute-done.69
  807.6 9.0 collective-permute-start.70
  817.4 3.9 collective-permute-done.71
  822.4 3.6 collective-permute-done.72
  827.8 24.9 %collective-permute-done.74 = f32[16,1024]{1,0:T(8,128)S(1)} collective-permute-done((f32[16,1024]{1,0:T(8,128)S(1)}, f32[16,1024]{1,0:T(8,128)S(1)}, u32[]{:S(2)}, u32[]{:S(2)}) %collective-permute-start.74) | collective-permute-done | bytes 65568 | tf_op jit(solution)/shard_map/ppermute | solution.py:439
  852.9 5.3 collective-permute-done.75
  872.6 5.7 collective-permute-start.78
  881.9 73.5 %newton_schulz.1 = bf16[1024,1024]{1,0:T(8,128)(2,1)} custom-call(f32[512,512]{1,0:T(8,128)} %slice.806.first_ref, f32[512,512]{1,0:T(8,128)} %pad_maximum_fusion.25.side_ref, f32[512,512]{1,0:T(8,128)} %slice.809.last_ref, f32[1024,1024]{1,0:T(8,128)} %pad_maximum_fusion.start_ref), custom_call_target="tpu_custom_call" | custom-call | tf_op jit(solution)/shard_map/newton_schulz/pallas_call | solution.py:559
  957.5 3.4 fusion.167
  964.4 3.8 collective-permute-start.84
  978.1 3.8 collective-permute-start.86
  981.9 7.8 collective-permute-start.87
  995.2 7.8 collective-permute-done.85
  1003.0 5.9 collective-permute-done.86
  1008.9 4.3 collective-permute-done.87
  (1088 shorter events, 355.5 us)
Async XLA Ops:
  7.2 36.8 %all-gather.8.cloned.1.call-start = ((), (), s32[]{:S(2)}) async-start(), calls=%async_computation.4 | async-start | bytes 1310720 | tf_op jit(solution)/shard_map/all_gather | solution.py:640
  10.8 33.2 %collective-permute-start.3 = (bf16[256,512]{0,1:T(8,128)(2,1)}, bf16[256,512]{0,1:T(8,128)(2,1)}, u32[]{:S(2)}, u32[]{:S(2)}) collective-permute-start(bf16[256,512]{0,1:T(8,128)(2,1)} %pad_maximum_fusion.51), channel_id=1, source_target_pairs={{0,4},{4,0},{1,5},{5,1},{2,6},{6,2},{3,7},{7,3},{8,12},{12,8},{9,1... | collective-permute-start | bytes 786440 | tf_op jit(solution)/shard_map/ppermute | solution.py:37
  14.9 57.0 %all-gather.10.cloned.1.call-start = ((), (), s32[]{:S(2)}) async-start(), calls=%async_computation.5 | async-start | bytes 1310720 | tf_op jit(solution)/shard_map/all_gather | solution.py:640
  17.0 25.7 %collective-permute-start = (bf16[172,1024]{1,0:T(8,128)(2,1)}, bf16[172,1024]{1,0:T(8,128)(2,1)}, u32[]{:S(2)}, u32[]{:S(2)}) collective-permute-start(bf16[172,1024]{1,0:T(8,128)(2,1)} %fusion.132), channel_id=1, source_target_pairs={{0,4},{4,0},{1,5},{5,1},{2,6},{6,2},{3,7},{7,3},{8,12},{12,8},{9,1... | collective-permute-start | bytes 1056776 | tf_op jit(solution)/shard_map/ppermute | solution.py:37
  17.0 28.8 %collective-permute-start.4 = (f32[2,2,384]{2,1,0:T(2,128)S(1)}, f32[2,2,384]{2,1,0:T(2,128)S(1)}, u32[]{:S(2)}, u32[]{:S(2)}) collective-permute-start(f32[2,2,384]{2,1,0:T(2,128)S(1)} %copy-done.278), channel_id=1, source_target_pairs={{0,4},{4,0},{1,5},{5,1},{2,6},{6,2},{3,7},{7,3},{8,12},{12,8},{9,1... | collective-permute-start | bytes 18440 | tf_op jit(solution)/shard_map/ppermute | solution.py:37
  44.0 98.0 %all-gather.12.cloned.1.call-start = ((), (), s32[]{:S(2)}) async-start(), calls=%async_computation.6 | async-start | bytes 2621440 | tf_op jit(solution)/shard_map/all_gather | solution.py:640
  45.8 27.3 %collective-permute-start.2 = (bf16[344,1024]{1,0:T(8,128)(2,1)}, bf16[344,1024]{1,0:T(8,128)(2,1)}, u32[]{:S(2)}, u32[]{:S(2)}) collective-permute-start(bf16[344,1024]{1,0:T(8,128)(2,1)} %add_convert_fusion.15), channel_id=1, source_target_pairs={{0,1},{1,0},{2,3},{3,2},{4,5},{5,4},{6,7},{7,6},{8,9},{9,8},{10,11... | collective-permute-start | bytes 2113544 | tf_op jit(solution)/shard_map/ppermute | solution.py:41
  46.1 30.0 %collective-permute-start.1 = (bf16[344,1024]{1,0:T(8,128)(2,1)}, bf16[344,1024]{1,0:T(8,128)(2,1)}, u32[]{:S(2)}, u32[]{:S(2)}) collective-permute-start(bf16[344,1024]{1,0:T(8,128)(2,1)} %add_convert_fusion.15), channel_id=1, source_target_pairs={{2,0},{0,2},{3,1},{1,3},{6,4},{4,6},{7,5},{5,7},{10,8},{8,10},{11,... | collective-permute-start | bytes 2113544 | tf_op jit(solution)/shard_map/ppermute | solution.py:46
  47.2 99.5 %all-gather.14.cloned.1.call-start = ((), (), s32[]{:S(2)}) async-start(), calls=%async_computation.7 | async-start | bytes 2621440 | tf_op jit(solution)/shard_map/all_gather | solution.py:640
  77.8 26.8 %collective-permute-start.6 = (bf16[256,1024]{1,0:T(8,128)(2,1)}, bf16[256,1024]{1,0:T(8,128)(2,1)}, u32[]{:S(2)}, u32[]{:S(2)}) collective-permute-start(bf16[256,1024]{1,0:T(8,128)(2,1)} %pad_maximum_fusion.35), channel_id=1, source_target_pairs={{0,4},{4,0},{1,5},{5,1},{2,6},{6,2},{3,7},{7,3},{8,12},{12,8},{9,1... | collective-permute-start | bytes 1572872 | tf_op jit(solution)/shard_map/ppermute | solution.py:37
  108.5 23.7 %collective-permute-start.8 = (bf16[344,1024]{1,0:T(8,128)(2,1)}, bf16[344,1024]{1,0:T(8,128)(2,1)S(1)}, u32[]{:S(2)}, u32[]{:S(2)}) collective-permute-start(bf16[344,1024]{1,0:T(8,128)(2,1)} %add_convert_fusion.14), channel_id=1, source_target_pairs={{2,0},{0,2},{3,1},{1,3},{6,4},{4,6},{7,5},{5,7},{10,8},{8,10},{11,... | collective-permute-start | bytes 2113544 | tf_op jit(solution)/shard_map/ppermute | solution.py:46
  109.0 21.3 %collective-permute-start.9 = (bf16[256,512]{0,1:T(8,128)(2,1)}, bf16[256,512]{0,1:T(8,128)(2,1)}, u32[]{:S(2)}, u32[]{:S(2)}) collective-permute-start(bf16[256,512]{0,1:T(8,128)(2,1)} %pad_maximum_fusion.52), channel_id=1, source_target_pairs={{0,4},{4,0},{1,5},{5,1},{2,6},{6,2},{3,7},{7,3},{8,12},{12,8},{9,1... | collective-permute-start | bytes 786440 | tf_op jit(solution)/shard_map/ppermute | solution.py:37
  112.4 104.7 %all-gather.16.cloned.1.call-start = ((), (), s32[]{:S(2)}) async-start(), calls=%async_computation.8 | async-start | bytes 2621440 | tf_op jit(solution)/shard_map/all_gather | solution.py:640
  137.6 23.4 %collective-permute-start.11 = (bf16[344,1024]{1,0:T(8,128)(2,1)}, bf16[344,1024]{1,0:T(8,128)(2,1)}, u32[]{:S(2)}, u32[]{:S(2)}) collective-permute-start(bf16[344,1024]{1,0:T(8,128)(2,1)} %add_convert_fusion.13), channel_id=1, source_target_pairs={{2,0},{0,2},{3,1},{1,3},{6,4},{4,6},{7,5},{5,7},{10,8},{8,10},{11,... | collective-permute-start | bytes 2113544 | tf_op jit(solution)/shard_map/ppermute | solution.py:46
  181.8 115.8 %all-gather.18.cloned.1.call-start = ((), (), s32[]{:S(2)}) async-start(), calls=%async_computation.9 | async-start | bytes 2621440 | tf_op jit(solution)/shard_map/all_gather | solution.py:640
  184.6 18.1 %collective-permute-start.16 = (bf16[344,1024]{1,0:T(8,128)(2,1)S(1)}, bf16[344,1024]{1,0:T(8,128)(2,1)S(1)}, u32[]{:S(2)}, u32[]{:S(2)}) collective-permute-start(bf16[344,1024]{1,0:T(8,128)(2,1)S(1)} %add_convert_fusion.12), channel_id=1, source_target_pairs={{2,0},{0,2},{3,1},{1,3},{6,4},{4,6},{7,5},{5,7},{10,8},{8,10},{11,... | collective-permute-start | bytes 2113544 | tf_op jit(solution)/shard_map/ppermute | solution.py:46
  206.5 19.2 %collective-permute-start.17 = (bf16[344,1024]{1,0:T(8,128)(2,1)}, bf16[344,1024]{1,0:T(8,128)(2,1)}, u32[]{:S(2)}, u32[]{:S(2)}) collective-permute-start(bf16[344,1024]{1,0:T(8,128)(2,1)} %add_convert_fusion.11), channel_id=1, source_target_pairs={{2,0},{0,2},{3,1},{1,3},{6,4},{4,6},{7,5},{5,7},{10,8},{8,10},{11,... | collective-permute-start | bytes 2113544 | tf_op jit(solution)/shard_map/ppermute | solution.py:46
  222.7 74.9 %all-gather.20.cloned.1.call-start = ((), (), s32[]{:S(2)}) async-start(), calls=%async_computation.10 | async-start | bytes 2621440 | tf_op jit(solution)/shard_map/all_gather | solution.py:640
  228.0 26.6 %collective-permute-start.20 = (bf16[256,1024]{1,0:T(8,128)(2,1)S(1)}, bf16[256,1024]{1,0:T(8,128)(2,1)}, u32[]{:S(2)}, u32[]{:S(2)}) collective-permute-start(bf16[256,1024]{1,0:T(8,128)(2,1)S(1)} %copy-done.139), channel_id=1, source_target_pairs={{0,4},{4,0},{1,5},{5,1},{2,6},{6,2},{3,7},{7,3},{8,12},{12,8},{9,1... | collective-permute-start | bytes 1572872 | tf_op jit(solution)/shard_map/ppermute | solution.py:37
  259.5 25.9 %collective-permute-start.22 = (bf16[344,1024]{1,0:T(8,128)(2,1)}, bf16[344,1024]{1,0:T(8,128)(2,1)}, u32[]{:S(2)}, u32[]{:S(2)}) collective-permute-start(bf16[344,1024]{1,0:T(8,128)(2,1)} %add_convert_fusion.10), channel_id=1, source_target_pairs={{2,0},{0,2},{3,1},{1,3},{6,4},{4,6},{7,5},{5,7},{10,8},{8,10},{11,... | collective-permute-start | bytes 2113544 | tf_op jit(solution)/shard_map/ppermute | solution.py:46
  259.9 23.4 %collective-permute-start.23 = (bf16[172,1024]{1,0:T(8,128)(2,1)}, bf16[172,1024]{1,0:T(8,128)(2,1)}, u32[]{:S(2)}, u32[]{:S(2)}) collective-permute-start(bf16[172,1024]{1,0:T(8,128)(2,1)} %fusion.133), channel_id=1, source_target_pairs={{0,4},{4,0},{1,5},{5,1},{2,6},{6,2},{3,7},{7,3},{8,12},{12,8},{9,1... | collective-permute-start | bytes 1056776 | tf_op jit(solution)/shard_map/ppermute | solution.py:37
  263.4 315.0 %reduce-scatter.5.cloned.1.call-start = ((), (), s32[]{:S(2)}) async-start(), calls=%async_computation.11 | async-start | bytes 7864320 | tf_op jit(solution)/shard_map/reduce_scatter | solution.py:643
  292.2 18.8 %collective-permute-start.30 = (bf16[344,1024]{1,0:T(8,128)(2,1)}, bf16[344,1024]{1,0:T(8,128)(2,1)}, u32[]{:S(2)}, u32[]{:S(2)}) collective-permute-start(bf16[344,1024]{1,0:T(8,128)(2,1)} %add_convert_fusion.9), channel_id=1, source_target_pairs={{2,0},{0,2},{3,1},{1,3},{6,4},{4,6},{7,5},{5,7},{10,8},{8,10},{11,... | collective-permute-start | bytes 2113544 | tf_op jit(solution)/shard_map/ppermute | solution.py:46
  328.8 18.3 %collective-permute-start.40 = (bf16[344,1024]{1,0:T(8,128)(2,1)S(1)}, bf16[344,1024]{1,0:T(8,128)(2,1)S(1)}, u32[]{:S(2)}, u32[]{:S(2)}) collective-permute-start(bf16[344,1024]{1,0:T(8,128)(2,1)S(1)} %add_convert_fusion.7), channel_id=1, source_target_pairs={{2,0},{0,2},{3,1},{1,3},{6,4},{4,6},{7,5},{5,7},{10,8},{8,10},{11,... | collective-permute-start | bytes 2113544 | tf_op jit(solution)/shard_map/ppermute | solution.py:46
  349.5 18.3 %collective-permute-start.25 = (bf16[344,1024]{1,0:T(8,128)(2,1)S(1)}, bf16[344,1024]{1,0:T(8,128)(2,1)}, u32[]{:S(2)}, u32[]{:S(2)}) collective-permute-start(bf16[344,1024]{1,0:T(8,128)(2,1)S(1)} %get-tuple-element.569), channel_id=1, source_target_pairs={{2,0},{0,2},{3,1},{1,3},{6,4},{4,6},{7,5},{5,7},{10,8},{8,10},{11,... | collective-permute-start | bytes 2113544 | tf_op jit(solution)/shard_map/ppermute | solution.py:46
  386.6 18.8 %collective-permute-start.28 = (bf16[344,1024]{1,0:T(8,128)(2,1)S(1)}, bf16[344,1024]{1,0:T(8,128)(2,1)S(1)}, u32[]{:S(2)}, u32[]{:S(2)}) collective-permute-start(bf16[344,1024]{1,0:T(8,128)(2,1)S(1)} %slice.643), channel_id=1, source_target_pairs={{0,1},{1,0},{2,3},{3,2},{4,5},{5,4},{6,7},{7,6},{8,9},{9,8},{10,11... | collective-permute-start | bytes 2113544 | tf_op jit(solution)/shard_map/ppermute | solution.py:41
  387.4 17.9 %collective-permute-start.33 = (bf16[344,1024]{1,0:T(8,128)(2,1)S(1)}, bf16[344,1024]{1,0:T(8,128)(2,1)S(1)}, u32[]{:S(2)}, u32[]{:S(2)}) collective-permute-start(bf16[344,1024]{1,0:T(8,128)(2,1)S(1)} %add_convert_fusion.8), channel_id=1, source_target_pairs={{2,0},{0,2},{3,1},{1,3},{6,4},{4,6},{7,5},{5,7},{10,8},{8,10},{11,... | collective-permute-start | bytes 2113544 | tf_op jit(solution)/shard_map/ppermute | solution.py:46
  410.9 17.5 %collective-permute-start.34 = (bf16[344,1024]{1,0:T(8,128)(2,1)S(1)}, bf16[344,1024]{1,0:T(8,128)(2,1)S(1)}, u32[]{:S(2)}, u32[]{:S(2)}) collective-permute-start(bf16[344,1024]{1,0:T(8,128)(2,1)S(1)} %multiply_convert_fusion.2), channel_id=1, source_target_pairs={{2,0},{0,2},{3,1},{1,3},{6,4},{4,6},{7,5},{5,7},{10,8},{8,10},{11,... | collective-permute-start | bytes 2113544 | tf_op jit(solution)/shard_map/ppermute | solution.py:46
  433.8 37.4 %collective-permute-start.37 = (bf16[256,1536]{1,0:T(8,128)(2,1)}, bf16[256,1536]{1,0:T(8,128)(2,1)S(1)}, u32[]{:S(2)}, u32[]{:S(2)}) collective-permute-start(bf16[256,1536]{1,0:T(8,128)(2,1)} %get-tuple-element.260), channel_id=1, source_target_pairs={{0,4},{4,0},{1,5},{5,1},{2,6},{6,2},{3,7},{7,3},{8,12},{12,8},{9,1... | collective-permute-start | bytes 2359304 | tf_op jit(solution)/shard_map/ppermute | solution.py:37
  493.0 137.1 %reduce-scatter.7.cloned.1.call-start = ((), (), s32[]{:S(2)}) async-start(), calls=%async_computation.12 | async-start | bytes 2621440 | tf_op jit(solution)/shard_map/reduce_scatter | solution.py:643
  497.9 25.1 %collective-permute-start.42 = (bf16[344,1024]{1,0:T(8,128)(2,1)S(1)}, bf16[344,1024]{1,0:T(8,128)(2,1)S(1)}, u32[]{:S(2)}, u32[]{:S(2)}) collective-permute-start(bf16[344,1024]{1,0:T(8,128)(2,1)S(1)} %copy-done.177), channel_id=1, source_target_pairs={{2,0},{0,2},{3,1},{1,3},{6,4},{4,6},{7,5},{5,7},{10,8},{8,10},{11,... | collective-permute-start | bytes 2113544 | tf_op jit(solution)/shard_map/ppermute | solution.py:46
  499.3 21.6 %collective-permute-start.44 = (bf16[172,1024]{1,0:T(8,128)(2,1)S(1)}, bf16[172,1024]{1,0:T(8,128)(2,1)S(1)}, u32[]{:S(2)}, u32[]{:S(2)}) collective-permute-start(bf16[172,1024]{1,0:T(8,128)(2,1)S(1)} %slice.933), channel_id=1, source_target_pairs={{0,4},{4,0},{1,5},{5,1},{2,6},{6,2},{3,7},{7,3},{8,12},{12,8},{9,1... | collective-permute-start | bytes 1056776 | tf_op jit(solution)/shard_map/ppermute | solution.py:37
  526.2 18.2 %collective-permute-start.45 = (bf16[344,1024]{1,0:T(8,128)(2,1)S(1)}, bf16[344,1024]{1,0:T(8,128)(2,1)S(1)}, u32[]{:S(2)}, u32[]{:S(2)}) collective-permute-start(bf16[344,1024]{1,0:T(8,128)(2,1)S(1)} %multiply_convert_fusion.1), channel_id=1, source_target_pairs={{2,0},{0,2},{3,1},{1,3},{6,4},{4,6},{7,5},{5,7},{10,8},{8,10},{11,... | collective-permute-start | bytes 2113544 | tf_op jit(solution)/shard_map/ppermute | solution.py:46
  558.8 18.1 %collective-permute-start.50 = (bf16[344,1024]{1,0:T(8,128)(2,1)}, bf16[344,1024]{1,0:T(8,128)(2,1)}, u32[]{:S(2)}, u32[]{:S(2)}) collective-permute-start(bf16[344,1024]{1,0:T(8,128)(2,1)} %add_convert_fusion.5), channel_id=1, source_target_pairs={{2,0},{0,2},{3,1},{1,3},{6,4},{4,6},{7,5},{5,7},{10,8},{8,10},{11,... | collective-permute-start | bytes 2113544 | tf_op jit(solution)/shard_map/ppermute | solution.py:46
  577.0 91.7 %reduce-scatter.9.cloned.1.call-start = ((), (), s32[]{:S(2)}) async-start(), calls=%async_computation.13 | async-start | bytes 2621440 | tf_op jit(solution)/shard_map/reduce_scatter | solution.py:643
  589.2 17.9 %collective-permute-start.51 = (bf16[344,1024]{1,0:T(8,128)(2,1)S(1)}, bf16[344,1024]{1,0:T(8,128)(2,1)}, u32[]{:S(2)}, u32[]{:S(2)}) collective-permute-start(bf16[344,1024]{1,0:T(8,128)(2,1)S(1)} %multiply_convert_fusion), channel_id=1, source_target_pairs={{2,0},{0,2},{3,1},{1,3},{6,4},{4,6},{7,5},{5,7},{10,8},{8,10},{11,... | collective-permute-start | bytes 2113544 | tf_op jit(solution)/shard_map/ppermute | solution.py:46
  607.1 128.3 %reduce-scatter.11.cloned.1.call-start = ((), (), s32[]{:S(2)}) async-start(), calls=%async_computation.14 | async-start | bytes 2621440 | tf_op jit(solution)/shard_map/reduce_scatter | solution.py:643
  610.4 16.8 %collective-permute-start.54 = (bf16[344,1024]{1,0:T(8,128)(2,1)}, bf16[344,1024]{1,0:T(8,128)(2,1)S(1)}, u32[]{:S(2)}, u32[]{:S(2)}) collective-permute-start(bf16[344,1024]{1,0:T(8,128)(2,1)} %collective-permute-done.51), channel_id=1, source_target_pairs={{0,1},{1,0},{2,3},{3,2},{4,5},{5,4},{6,7},{7,6},{8,9},{9,8},{10,11... | collective-permute-start | bytes 2113544 | tf_op jit(solution)/shard_map/ppermute | solution.py:41
  610.5 15.8 %collective-permute-start.53 = (bf16[256,1024]{1,0:T(8,128)(2,1)S(1)}, bf16[256,1024]{1,0:T(8,128)(2,1)S(1)}, u32[]{:S(2)}, u32[]{:S(2)}) collective-permute-start(bf16[256,1024]{1,0:T(8,128)(2,1)S(1)} %pad_maximum_fusion.40), channel_id=1, source_target_pairs={{0,4},{1,5},{2,6},{3,7},{8,12},{9,13},{10,14},{11,15},{16,20},{17,... | collective-permute-start | bytes 1572872 | tf_op jit(solution)/shard_map/ppermute | solution.py:832
  615.9 51.2 %collective-permute-start.58 = (bf16[256,1024]{1,0:T(8,128)(2,1)}, bf16[256,1024]{1,0:T(8,128)(2,1)}, u32[]{:S(2)}, u32[]{:S(2)}) collective-permute-start(bf16[256,1024]{1,0:T(8,128)(2,1)} %pad_maximum_fusion.44), channel_id=1, source_target_pairs={{0,4},{1,5},{2,6},{3,7},{8,12},{9,13},{10,14},{11,15},{16,20},{17,... | collective-permute-start | bytes 1572872 | tf_op jit(solution)/shard_map/ppermute | solution.py:832
  631.3 35.8 %collective-permute-start.59 = (bf16[256,1024]{1,0:T(8,128)(2,1)S(1)}, bf16[256,1024]{1,0:T(8,128)(2,1)}, u32[]{:S(2)}, u32[]{:S(2)}) collective-permute-start(bf16[256,1024]{1,0:T(8,128)(2,1)S(1)} %pad_maximum_fusion.45), channel_id=1, source_target_pairs={{4,0},{5,1},{6,2},{7,3},{12,8},{13,9},{14,10},{15,11},{20,16},{21,... | collective-permute-start | bytes 1572872 | tf_op jit(solution)/shard_map/ppermute | solution.py:832
  633.1 34.0 %collective-permute-start.55 = (bf16[256,1024]{1,0:T(8,128)(2,1)S(1)}, bf16[256,1024]{1,0:T(8,128)(2,1)S(1)}, u32[]{:S(2)}, u32[]{:S(2)}) collective-permute-start(bf16[256,1024]{1,0:T(8,128)(2,1)S(1)} %get-tuple-element.553), channel_id=1, source_target_pairs={{0,8},{8,0},{16,24},{24,16},{1,9},{9,1},{17,25},{25,17},{2,10},{10... | collective-permute-start | bytes 1572872 | tf_op jit(solution)/shard_map/ppermute | solution.py:637
  634.7 32.5 %collective-permute-start.57 = (bf16[256,1024]{1,0:T(8,128)(2,1)S(1)}, bf16[256,1024]{1,0:T(8,128)(2,1)S(1)}, u32[]{:S(2)}, u32[]{:S(2)}) collective-permute-start(bf16[256,1024]{1,0:T(8,128)(2,1)S(1)} %get-tuple-element.552), channel_id=1, source_target_pairs={{0,24},{8,16},{16,8},{24,0},{1,25},{9,17},{17,9},{25,1},{2,26},{10... | collective-permute-start | bytes 1572872 | tf_op jit(solution)/shard_map/ppermute | solution.py:637
  637.3 31.5 %collective-permute-start.56 = (bf16[256,1024]{1,0:T(8,128)(2,1)S(1)}, bf16[256,1024]{1,0:T(8,128)(2,1)S(1)}, u32[]{:S(2)}, u32[]{:S(2)}) collective-permute-start(bf16[256,1024]{1,0:T(8,128)(2,1)S(1)} %get-tuple-element.554), channel_id=1, source_target_pairs={{0,16},{8,24},{16,0},{24,8},{1,17},{9,25},{17,1},{25,9},{2,18},{10... | collective-permute-start | bytes 1572872 | tf_op jit(solution)/shard_map/ppermute | solution.py:637
  681.8 44.6 %collective-permute-start.62 = (bf16[256,1024]{1,0:T(8,128)(2,1)S(1)}, bf16[256,1024]{1,0:T(8,128)(2,1)}, u32[]{:S(2)}, u32[]{:S(2)}) collective-permute-start(bf16[256,1024]{1,0:T(8,128)(2,1)S(1)} %pad_maximum_fusion.47), channel_id=1, source_target_pairs={{0,4},{1,5},{2,6},{3,7},{8,12},{9,13},{10,14},{11,15},{16,20},{17,... | collective-permute-start | bytes 1572872 | tf_op jit(solution)/shard_map/ppermute | solution.py:832
  697.5 28.6 %collective-permute-start.61 = (bf16[344,1024]{1,0:T(8,128)(2,1)S(1)}, bf16[344,1024]{1,0:T(8,128)(2,1)S(1)}, u32[]{:S(2)}, u32[]{:S(2)}) collective-permute-start(bf16[344,1024]{1,0:T(8,128)(2,1)S(1)} %slice.795), channel_id=1, source_target_pairs={{0,1},{1,0},{2,3},{3,2},{4,5},{5,4},{6,7},{7,6},{8,9},{9,8},{10,11... | collective-permute-start | bytes 2113544 | tf_op jit(solution)/shard_map/ppermute | solution.py:41
  698.5 27.8 %collective-permute-start.63 = (bf16[256,1024]{1,0:T(8,128)(2,1)S(1)}, bf16[256,1024]{1,0:T(8,128)(2,1)S(1)}, u32[]{:S(2)}, u32[]{:S(2)}) collective-permute-start(bf16[256,1024]{1,0:T(8,128)(2,1)S(1)} %pad_maximum_fusion.48), channel_id=1, source_target_pairs={{4,0},{5,1},{6,2},{7,3},{12,8},{13,9},{14,10},{15,11},{20,16},{21,... | collective-permute-start | bytes 1572872 | tf_op jit(solution)/shard_map/ppermute | solution.py:832
  702.7 39.8 %collective-permute-start.68 = (bf16[344,1024]{1,0:T(8,128)(2,1)}, bf16[344,1024]{1,0:T(8,128)(2,1)}, u32[]{:S(2)}, u32[]{:S(2)}) collective-permute-start(bf16[344,1024]{1,0:T(8,128)(2,1)} %add_convert_fusion.4), channel_id=1, source_target_pairs={{2,0},{0,2},{3,1},{1,3},{6,4},{4,6},{7,5},{5,7},{10,8},{8,10},{11,... | collective-permute-start | bytes 2113544 | tf_op jit(solution)/shard_map/ppermute | solution.py:46
  737.4 28.1 %collective-permute-start.64 = (bf16[256,1024]{1,0:T(8,128)(2,1)}, bf16[256,1024]{1,0:T(8,128)(2,1)}, u32[]{:S(2)}, u32[]{:S(2)}) collective-permute-start(bf16[256,1024]{1,0:T(8,128)(2,1)} %pad_maximum_fusion.50), channel_id=1, source_target_pairs={{4,0},{5,1},{6,2},{7,3},{12,8},{13,9},{14,10},{15,11},{20,16},{21,... | collective-permute-start | bytes 1572872 | tf_op jit(solution)/shard_map/ppermute | solution.py:832
  782.4 14.8 %collective-permute-start.66 = (bf16[256,1024]{1,0:T(8,128)(2,1)S(1)}, bf16[256,1024]{1,0:T(8,128)(2,1)S(1)}, u32[]{:S(2)}, u32[]{:S(2)}) collective-permute-start(bf16[256,1024]{1,0:T(8,128)(2,1)S(1)} %get-tuple-element.558), channel_id=1, source_target_pairs={{0,16},{8,24},{16,0},{24,8},{1,17},{9,25},{17,1},{25,9},{2,18},{10... | collective-permute-start | bytes 1572872 | tf_op jit(solution)/shard_map/ppermute | solution.py:637
  783.0 14.2 %collective-permute-start.67 = (bf16[256,1024]{1,0:T(8,128)(2,1)S(1)}, bf16[256,1024]{1,0:T(8,128)(2,1)S(1)}, u32[]{:S(2)}, u32[]{:S(2)}) collective-permute-start(bf16[256,1024]{1,0:T(8,128)(2,1)S(1)} %get-tuple-element.556), channel_id=1, source_target_pairs={{0,24},{8,16},{16,8},{24,0},{1,25},{9,17},{17,9},{25,1},{2,26},{10... | collective-permute-start | bytes 1572872 | tf_op jit(solution)/shard_map/ppermute | solution.py:637
  807.6 51.3 %collective-permute-start.70 = (f32[768,512]{1,0:T(8,128)S(1)}, f32[768,512]{1,0:T(8,128)}, u32[]{:S(2)}, u32[]{:S(2)}) collective-permute-start(f32[768,512]{1,0:T(8,128)S(1)} %select_add_fusion), channel_id=1, source_target_pairs={{2,0},{0,2},{3,1},{1,3},{6,4},{4,6},{7,5},{5,7},{10,8},{8,10},{11,... | collective-permute-start | bytes 4718600 | tf_op jit(solution)/shard_map/ppermute | solution.py:46
  827.4 25.3 %collective-permute-start.74 = (f32[16,1024]{1,0:T(8,128)S(1)}, f32[16,1024]{1,0:T(8,128)S(1)}, u32[]{:S(2)}, u32[]{:S(2)}) collective-permute-start(f32[16,1024]{1,0:T(8,128)S(1)} %slice_add_fusion), channel_id=1, source_target_pairs={{0,2},{2,0},{1,3},{3,1},{4,6},{6,4},{5,7},{7,5},{8,10},{10,8},{9,1... | collective-permute-start | bytes 196616 | tf_op jit(solution)/shard_map/ppermute | solution.py:439
  827.8 25.0 %collective-permute-start.76 = (f32[2,2,96]{2,1,0:T(2,128)S(1)}, f32[2,2,96]{2,1,0:T(2,128)S(1)}, u32[]{:S(2)}, u32[]{:S(2)}) collective-permute-start(f32[2,2,96]{2,1,0:T(2,128)S(1)} %constant_dynamic-slice_fusion), channel_id=1, source_target_pairs={{0,4},{4,0},{1,5},{5,1},{2,6},{6,2},{3,7},{7,3},{8,12},{12,8},{9,1... | collective-permute-start | bytes 4616 | tf_op jit(solution)/shard_map/ppermute | solution.py:37
  871.0 86.5 %collective-permute-start.79 = (bf16[256,1536]{1,0:T(8,128)(2,1)S(1)}, bf16[256,1536]{1,0:T(8,128)(2,1)S(1)}, u32[]{:S(2)}, u32[]{:S(2)}) collective-permute-start(bf16[256,1536]{1,0:T(8,128)(2,1)S(1)} %pad_maximum_fusion.31), channel_id=1, source_target_pairs={{4,0},{5,1},{6,2},{7,3},{12,8},{13,9},{14,10},{15,11},{20,16},{21,... | collective-permute-start | bytes 2359304 | tf_op jit(solution)/shard_map/ppermute | solution.py:855
  872.6 84.8 %collective-permute-start.78 = (bf16[256,1536]{1,0:T(8,128)(2,1)S(1)}, bf16[256,1536]{1,0:T(8,128)(2,1)S(1)}, u32[]{:S(2)}, u32[]{:S(2)}) collective-permute-start(bf16[256,1536]{1,0:T(8,128)(2,1)S(1)} %pad_maximum_fusion.30), channel_id=1, source_target_pairs={{0,4},{1,5},{2,6},{3,7},{8,12},{9,13},{10,14},{11,15},{16,20},{17,... | collective-permute-start | bytes 2359304 | tf_op jit(solution)/shard_map/ppermute | solution.py:855
  881.9 75.5 %collective-permute-start.80 = (bf16[172,1024]{1,0:T(8,128)(2,1)S(1)}, bf16[172,1024]{1,0:T(8,128)(2,1)S(1)}, u32[]{:S(2)}, u32[]{:S(2)}) collective-permute-start(bf16[172,1024]{1,0:T(8,128)(2,1)S(1)} %slice.932), channel_id=1, source_target_pairs={{0,4},{4,0},{1,5},{5,1},{2,6},{6,2},{3,7},{7,3},{8,12},{12,8},{9,1... | collective-permute-start | bytes 1056776 | tf_op jit(solution)/shard_map/ppermute | solution.py:37
  960.9 17.1 %collective-permute-start.81 = (bf16[256,512]{1,0:T(8,128)(2,1)}, bf16[256,512]{1,0:T(8,128)(2,1)}, u32[]{:S(2)}, u32[]{:S(2)}) collective-permute-start(bf16[256,512]{1,0:T(8,128)(2,1)} %get-tuple-element.539), channel_id=1, source_target_pairs={{0,24},{8,16},{16,8},{24,0},{1,25},{9,17},{17,9},{25,1},{2,26},{10... | collective-permute-start | bytes 786440 | tf_op jit(solution)/shard_map/ppermute | solution.py:637
  962.4 19.5 %collective-permute-start.82 = (bf16[256,512]{1,0:T(8,128)(2,1)}, bf16[256,512]{1,0:T(8,128)(2,1)}, u32[]{:S(2)}, u32[]{:S(2)}) collective-permute-start(bf16[256,512]{1,0:T(8,128)(2,1)} %get-tuple-element.538), channel_id=1, source_target_pairs={{0,16},{8,24},{16,0},{24,8},{1,17},{9,25},{17,1},{25,9},{2,18},{10... | collective-permute-start | bytes 786440 | tf_op jit(solution)/shard_map/ppermute | solution.py:637
  963.1 32.1 %collective-permute-start.83 = (bf16[256,512]{1,0:T(8,128)(2,1)}, bf16[256,512]{1,0:T(8,128)(2,1)}, u32[]{:S(2)}, u32[]{:S(2)}) collective-permute-start(bf16[256,512]{1,0:T(8,128)(2,1)} %get-tuple-element.537), channel_id=1, source_target_pairs={{0,8},{8,0},{16,24},{24,16},{1,9},{9,1},{17,25},{25,17},{2,10},{10... | collective-permute-start | bytes 786440 | tf_op jit(solution)/shard_map/ppermute | solution.py:637
  964.4 30.8 %collective-permute-start.84 = (bf16[256,512]{1,0:T(8,128)(2,1)}, bf16[256,512]{1,0:T(8,128)(2,1)}, u32[]{:S(2)}, u32[]{:S(2)}) collective-permute-start(bf16[256,512]{1,0:T(8,128)(2,1)} %get-tuple-element.536), channel_id=1, source_target_pairs={{0,28},{4,24},{8,20},{12,16},{16,12},{20,8},{24,4},{28,0},{1,29},{... | collective-permute-start | bytes 786440 | tf_op jit(solution)/shard_map/ppermute | solution.py:720
  968.3 34.8 %collective-permute-start.85 = (bf16[256,512]{1,0:T(8,128)(2,1)}, bf16[256,512]{1,0:T(8,128)(2,1)}, u32[]{:S(2)}, u32[]{:S(2)}) collective-permute-start(bf16[256,512]{1,0:T(8,128)(2,1)} %get-tuple-element.533), channel_id=1, source_target_pairs={{0,20},{4,16},{8,28},{12,24},{16,4},{20,0},{24,12},{28,8},{1,21},{... | collective-permute-start | bytes 786440 | tf_op jit(solution)/shard_map/ppermute | solution.py:720
  978.1 30.9 %collective-permute-start.86 = (bf16[256,512]{1,0:T(8,128)(2,1)}, bf16[256,512]{1,0:T(8,128)(2,1)}, u32[]{:S(2)}, u32[]{:S(2)}) collective-permute-start(bf16[256,512]{1,0:T(8,128)(2,1)} %get-tuple-element.535), channel_id=1, source_target_pairs={{0,12},{4,8},{8,4},{12,0},{16,28},{20,24},{24,20},{28,16},{1,13},{... | collective-permute-start | bytes 786440 | tf_op jit(solution)/shard_map/ppermute | solution.py:720
  981.9 31.3 %collective-permute-start.87 = (bf16[256,512]{1,0:T(8,128)(2,1)S(1)}, bf16[256,512]{1,0:T(8,128)(2,1)}, u32[]{:S(2)}, u32[]{:S(2)}) collective-permute-start(bf16[256,512]{1,0:T(8,128)(2,1)S(1)} %copy-done.213), channel_id=1, source_target_pairs={{0,4},{4,0},{8,12},{12,8},{16,20},{20,16},{24,28},{28,24},{1,5},{5... | collective-permute-start | bytes 786440 | tf_op jit(solution)/shard_map/ppermute | solution.py:720
  (338 other events, 3211.5 us)
Sparse Core Ops, SparseCore 0:
  15.0 25.7 all-gather.7
  44.2 27.6 all-gather.9
  74.3 35.3 all-gather.11
  112.6 34.0 all-gather.13
  181.9 35.1 all-gather.15
  222.8 35.3 all-gather.17
  263.5 32.5 all-gather.19
  493.1 69.5 reduce-scatter.4
  577.1 34.6 reduce-scatter.6
  614.9 51.0 reduce-scatter.8
  676.1 59.2 reduce-scatter.10
